TPU v7x, 32 devices: a whole 2x2x4 slice. The times are simulated.
32 devices in a mesh: grp: 2 (over y), tile: 4 (over z), tm: 2 (over x), ch: 2 (over core).
Axes of the slice: x: 2, y: 2, z: 4, core: 2. Of those that a mesh axis runs over, the one named last changes fastest.
Arguments:
- latent: bfloat16 [8, 8, 64, 512], P(('grp', 'tm'), None, 'tile', 'ch'), parts along dimension 0, may hold values from -340 to 340
- norm_gain: float32 [512], P('ch'), may hold values from 0.1 to 1.9
- norm_shift: float32 [512], P('ch'), may hold values from -3 to 3
- kernel: bfloat16 [3, 3, 3, 512, 512], P(None, None, None, ('ch', 'tile', 'tm')), may hold values from -0.0546875 to 0.0546875
- conv_bias: float32 [512], P('ch'), may hold values from -3 to 3
- blend_profile: int32 [4], replicated, may hold values from 0 to 3
Outputs:
- decoded: bfloat16 [8, 8, 64, 512], P(('grp', 'tm'), None, 'tile', 'ch'), parts along dimension 0
There are 2 independent parts, one for each index of `grp`. A program takes and returns all parts, laid end to end along the dimension named above; an argument that names none is the same for every part. Nothing has to cross between parts.
All inputs are finite; a program needn't handle non-finite values.
Results may differ from a plain program's by a relative error of at most 0.0038.
The roundings to bfloat16 on the way count: a program that leaves them out, or rounds other values in their place, can miss the bound.
Values may be sent and summed in bfloat16 or wider, within the bound.
No kernel may reach another device: no remote copies, remote signals or barrier semaphores. Data moves between devices by JAX's collectives and lax.ppermute only.
A program may use at most 64 MiB of HBM per device.

v0:
```python
import jax
import jax.numpy as jnp
from jax import lax
from jax.sharding import PartitionSpec as P

GROUPS = 32
RIM = 4


def with_halo(shard, sides, width):
    for axis, dim in sides:
        size, length = (lax.axis_size(axis), shard.shape[dim])
        up = [(i, (i + 1) % size) for i in range(size - 1)]
        down = [(j, i) for i, j in up]
        last = lax.slice_in_dim(shard, length - width, length, axis=dim)
        leading = lax.slice_in_dim(shard, 0, width, axis=dim)
        before = lax.ppermute(last, axis, up)
        after = lax.ppermute(leading, axis, down)
        shard = jnp.concatenate([before, shard, after], axis=dim)
    return shard


def passed_along(block, axis, distance):
    devices = range(lax.axis_size(axis))
    route = [(i - distance, i) for i in devices if i - distance in devices]
    return lax.ppermute(block, axis, route)


def ramp_weight(profile, position, margin):
    fraction = (position.astype(jnp.float32) + 0.5) / (2.0 * margin)
    exponent = 1.0 + profile.astype(jnp.float32)
    near_part = jnp.power(1.0 - fraction, exponent)
    far_part = jnp.power(fraction, exponent)
    return near_part / (near_part + far_part)


def frame_stats(values, colmask, groups):
    frame_count, row_count, col_count, chan_count = values.shape
    grouped = values.reshape(frame_count, row_count, col_count, groups, chan_count // groups)
    weight = colmask.reshape(1, 1, col_count, 1, 1)
    counted = row_count * (chan_count // groups) * jnp.sum(colmask)
    center = jnp.sum(grouped * weight, axis=(1, 2, 4)) / counted
    spread = (grouped - center[:, None, None, :, None]) * weight
    inverse = lax.rsqrt(jnp.sum(spread * spread, axis=(1, 2, 4)) / counted + 1e-06)
    return (center, inverse)


def activate(values, center, inverse, norm_gain, norm_shift, colmask, timemask, groups):
    frame_count, row_count, col_count, chan_count = values.shape
    grouped = values.reshape(frame_count, row_count, col_count, groups, chan_count // groups)
    normed = (grouped - center[:, None, None, :, None]) * inverse[:, None, None, :, None]
    normed = normed.reshape(values.shape) * norm_gain + norm_shift
    masked = jax.nn.silu(normed) * colmask[None, None, :, None] * timemask[:, None, None, None]
    return masked.astype(jnp.bfloat16)


def conv_taps(padded, kernel_part, frame_count, row_count, col_count):
    in_width = kernel_part.shape[3]
    running = None
    for tap_time in range(3):
        for tap_row in range(3):
            for tap_col in range(3):
                window = padded[
                    tap_time : tap_time + frame_count,
                    tap_row : tap_row + row_count,
                    tap_col : tap_col + col_count,
                ]
                contrib = jnp.dot(
                    window.reshape(-1, in_width),
                    kernel_part[tap_time, tap_row, tap_col],
                    preferred_element_type=jnp.float32,
                )
                running = contrib if running is None else running + contrib
    return running


def on_device(latent, norm_gain, norm_shift, kernel, conv_bias, blend_profile):
    frame_count, row_count, core_cols, chan_half = latent.shape
    out_chans = kernel.shape[4]
    groups = GROUPS // lax.axis_size("ch")
    ncols = core_cols + 2 * RIM
    tile_pos = lax.axis_index("tile")
    tile_count = lax.axis_size("tile")
    window_in = with_halo(latent, (("tile", 2),), RIM)
    cached = passed_along(window_in, "tm", 1)
    frames = jnp.concatenate([cached, window_in], axis=0).astype(jnp.float32)
    column = tile_pos * core_cols - RIM + jnp.arange(ncols, dtype=jnp.int32)
    colmask = ((column >= 0) & (column < tile_count * core_cols)).astype(jnp.float32)
    started = (lax.axis_index("tm") > 0).astype(jnp.float32)
    timemask = jnp.concatenate(
        [jnp.ones((2,), jnp.float32) * started, jnp.ones((frame_count,), jnp.float32)]
    )
    center, inverse = frame_stats(frames, colmask, groups)
    activated = activate(frames, center, inverse, norm_gain, norm_shift, colmask, timemask, groups)
    inputs = (jnp.pad(activated, ((0, 0), (1, 1), (1, 1), (0, 0))),)
    widths = (ncols,)

    def accumulate(shard_rows):
        return tuple(
            (
                conv_taps(source, shard_rows, frame_count, row_count, width_cols)
                for source, width_cols in zip(inputs, widths)
            )
        )

    totals = accumulate(lax.all_gather(kernel, ("tile", "tm"), axis=3, tiled=True))
    shaped = [
        running.reshape(frame_count, row_count, width_cols, out_chans)
        for running, width_cols in zip(totals, widths)
    ]
    joined = shaped[0]
    summed = lax.psum_scatter(joined, "ch", scatter_dimension=3, tiled=True)
    tile_out = (summed + conv_bias).astype(jnp.bfloat16)
    extended = with_halo(tile_out, (("tile", 2),), RIM)
    own_out = tile_out[:, :, RIM : RIM + core_cols]
    left_nbr = extended[:, :, :RIM]
    right_nbr = extended[:, :, ncols + RIM :]
    own_profile = lax.dynamic_index_in_dim(blend_profile, tile_pos, 0, keepdims=False)
    prev_profile = lax.dynamic_index_in_dim(
        blend_profile, jnp.maximum(tile_pos - 1, 0), 0, keepdims=False
    )
    offsets = jnp.arange(RIM, dtype=jnp.int32)
    left_weight = jnp.where(tile_pos > 0, ramp_weight(prev_profile, offsets + RIM, RIM), 0.0)
    right_weight = jnp.where(tile_pos < tile_count - 1, ramp_weight(own_profile, offsets, RIM), 1.0)
    left_wide = left_weight[None, None, :, None]
    right_wide = right_weight[None, None, :, None]
    own_float = own_out.astype(jnp.float32)
    head_cols = own_float[:, :, :RIM] * (1.0 - left_wide) + left_nbr.astype(jnp.float32) * left_wide
    tail_cols = own_float[:, :, core_cols - RIM :] * right_wide + right_nbr.astype(jnp.float32) * (
        1.0 - right_wide
    )
    middle = own_float[:, :, RIM : core_cols - RIM]
    return jnp.concatenate([head_cols, middle, tail_cols], axis=2).astype(jnp.bfloat16)


def solution(mesh):
    in_specs = (
        P(("grp", "tm"), None, "tile", "ch"),
        P("ch"),
        P("ch"),
        P(None, None, None, ("ch", "tile", "tm"), None),
        P("ch"),
        P(),
    )
    out_specs = P(("grp", "tm"), None, "tile", "ch")
    return jax.shard_map(
        on_device, mesh=mesh, in_specs=in_specs, out_specs=out_specs, check_vma=False
    )
```

profile of v0, /device:TPU:0, one launch (start us, length us, event | category | flops | bytes accessed | tf_op | source)
XLA Modules:
  0.0 158.9 jit_solution(7346280072205576620)
XLA Ops:
  6.5 0.7 all-gather.2.cloned.1.call-update
  7.3 0.0 reduce-scatter.2.cloned.1.call-start
  7.3 0.9 fusion.11
  8.2 4.9 %collective-permute-start = (bf16[2,8,4,256]{3,2,1,0:T(4,128)(2,1)S(1)}, bf16[2,8,4,256]{3,2,1,0:T(4,128)(2,1)S(1)}, u32[]{:S(2)}, u32[]{:S(2)}) collective-permute-start(bf16[2,8,4,256]{3,2,1,0:T(4,128)(2,1)S(1)} %get-tuple-element.40), channel_id=1, source_target_pairs={{0,4},{4,8},{8,12},{1,5},{5,9},{9,13},{2,6},{6,10},{10,14},{3,7},{... | collective-permute-start | bytes 98312 | tf_op jit(solution)/shard_map/ppermute | solution.py:17
  13.2 1.3 collective-permute-start.1
  14.5 0.3 collective-permute-done
  14.7 4.2 %collective-permute-done.1 = bf16[2,8,4,256]{3,2,1,0:T(4,128)(2,1)S(1)} collective-permute-done((bf16[2,8,4,256]{3,2,1,0:T(4,128)(2,1)S(1)}, bf16[2,8,4,256]{3,2,1,0:T(4,128)(2,1)S(1)}, u32[]{:S(2)}, u32[]{:S(2)}) %collective-permute-start.1) | collective-permute-done | bytes 32800 | tf_op jit(solution)/shard_map/ppermute | solution.py:18
  19.0 1.0 pad_maximum_fusion.1
  20.0 3.4 %collective-permute-start.2 = (bf16[2,8,24,256]{3,2,1,0:T(8,128)(2,1)S(1)}, bf16[2,8,24,256]{3,2,1,0:T(8,128)(2,1)S(1)}, u32[]{:S(2)}, u32[]{:S(2)}) collective-permute-start(bf16[2,8,24,256]{3,2,1,0:T(8,128)(2,1)S(1)} %pad_maximum_fusion.1), channel_id=1, source_target_pairs={{0,2},{1,3},{4,6},{5,7},{8,10},{9,11},{12,14},{13,15},{16,18},{17,... | collective-permute-start | bytes 589832 | tf_op jit(solution)/shard_map/ppermute | solution.py:26
  23.4 0.6 fusion.9
  24.7 0.5 concatenate.26
  25.2 1.1 concatenate.24
  26.3 5.6 %collective-permute-done.2 = bf16[2,8,24,256]{3,2,1,0:T(8,128)(2,1)S(1)} collective-permute-done((bf16[2,8,24,256]{3,2,1,0:T(8,128)(2,1)S(1)}, bf16[2,8,24,256]{3,2,1,0:T(8,128)(2,1)S(1)}, u32[]{:S(2)}, u32[]{:S(2)}) %collective-permute-start.2) | collective-permute-done | bytes 196640 | tf_op jit(solution)/shard_map/ppermute | solution.py:26
  31.9 1.1 concatenate.23
  32.9 1.2 fusion
  34.2 1.7 %fusion.3 = f32[4,16]{1,0:T(4,128)S(1)} fusion(f32[4,16]{1,0:T(4,128)S(1)} %broadcast_divide_fusion, f32[24]{0:T(128)S(1)} %and_convert_fusion, bf16[2,8,24,16,16]{4,3,2,1,0:T(8,128)(2,1)S(1)} %concatenate.24, bf16[2,8,24,16,16]{4,3,2,1,0:T(8,128)(2,1)S(1)} %concatenate.23), kind=kLoop, calls=%fused_computation.5 | loop fusion | flops 1179584 | bytes 393824 | tf_op jit(solution)/shard_map/reduce_sum | solution.py:44
  35.9 0.1 mul.101
  35.9 0.1 mul.102
  36.0 0.1 sub.64
  36.1 0.1 sub.65
  36.2 0.0 copy-done.11
  36.2 1.1 multiply_convert_fusion
  37.3 1.1 pad_slice_fusion
  38.4 1.3 pad_slice_fusion.1
  39.7 81.3 %all-gather.2.cloned.1.call-done = bf16[3,3,3,256,512]{4,3,2,1,0:T(8,128)(2,1)} async-done(((bf16[3,3,3,32,512]{4,3,2,1,0:T(8,128)(2,1)}), bf16[3,3,3,256,512]{4,3,2,1,0:T(8,128)(2,1)}) %all-gather.2.cloned.1.call-update) | async-done | bytes 7077904 | tf_op jit(solution)/shard_map/all_gather | solution.py:106
  121.1 1.4 fusion.4
  122.5 1.9 %convolution_add_fusion.25 = f32[384,512]{1,0:T(8,128)S(1)} fusion(f32[384,512]{1,0:T(8,128)S(1)} %fusion.4, bf16[384,256]{1,0:T(8,128)(2,1)} %bitcast.161, bf16[3,3,3,256,512]{4,3,2,1,0:T(8,128)(2,1)} %all-gather.2.cloned.1.call-done), kind=kOutput, calls=%fused_computation.56 | convolution fusion | flops 100859904 | bytes 2031616 | tf_op jit(solution)/shard_map/dot_general | solution.py:68
  124.5 1.2 convolution_add_fusion.24
  125.7 1.2 convolution_add_fusion.23
  126.9 0.3 convolution_add_fusion.22
  127.2 0.3 convolution_add_fusion.21
  127.5 0.3 convolution_add_fusion.20
  127.7 0.3 convolution_add_fusion.19
  128.0 0.3 convolution_add_fusion.18
  128.3 0.3 convolution_add_fusion.17
  128.5 0.3 convolution_add_fusion.16
  128.8 0.3 convolution_add_fusion.15
  129.1 0.3 convolution_add_fusion.14
  129.3 0.3 convolution_add_fusion.13
  129.6 0.3 convolution_add_fusion.12
  129.9 0.3 convolution_add_fusion.11
  130.2 0.3 convolution_add_fusion.10
  130.4 0.3 convolution_add_fusion.9
  130.7 0.3 convolution_add_fusion.8
  131.0 0.3 convolution_add_fusion.7
  131.2 0.0 copy-start.9
  131.2 0.0 copy-start.12
  131.3 0.3 convolution_add_fusion.6
  131.5 0.3 convolution_add_fusion.5
  131.8 0.3 convolution_add_fusion.4
  132.1 0.3 convolution_add_fusion.3
  132.4 0.3 convolution_add_fusion.2
  132.6 0.3 convolution_add_fusion.1
  132.9 1.1 convolution_add_fusion
  134.0 0.0 reduce-scatter.2.cloned.1.call-update
  134.1 0.7 fusion.12
  136.1 4.6 %reduce-scatter.2.cloned.1.call-done = f32[2,8,24,256]{3,2,1,0:T(8,128)} async-done(((f32[2,8,24,512]{3,2,1,0:T(8,128)}), f32[2,8,24,256]{3,2,1,0:T(8,128)}) %reduce-scatter.2.cloned.1.call-update) | async-done | bytes 393232 | tf_op jit(solution)/shard_map/reduce_scatter | solution.py:112
  140.7 1.0 add_convert_fusion
  141.7 3.6 %collective-permute-start.3 = (bf16[2,8,4,256]{3,2,1,0:T(4,128)(2,1)S(1)}, bf16[2,8,4,256]{3,2,1,0:T(4,128)(2,1)S(1)}, u32[]{:S(2)}, u32[]{:S(2)}) collective-permute-start(bf16[2,8,4,256]{3,2,1,0:T(4,128)(2,1)S(1)} %get-tuple-element.38), channel_id=1, source_target_pairs={{0,4},{4,8},{8,12},{1,5},{5,9},{9,13},{2,6},{6,10},{10,14},{3,7},{... | collective-permute-start | bytes 98312 | tf_op jit(solution)/shard_map/ppermute | solution.py:17
  145.4 1.3 collective-permute-start.4
  146.7 0.2 collective-permute-done.3
  146.9 4.2 %collective-permute-done.4 = bf16[2,8,4,256]{3,2,1,0:T(4,128)(2,1)S(1)} collective-permute-done((bf16[2,8,4,256]{3,2,1,0:T(4,128)(2,1)S(1)}, bf16[2,8,4,256]{3,2,1,0:T(4,128)(2,1)S(1)}, u32[]{:S(2)}, u32[]{:S(2)}) %collective-permute-start.4) | collective-permute-done | bytes 32800 | tf_op jit(solution)/shard_map/ppermute | solution.py:18
  151.2 0.1 fusion.8
  151.3 0.7 pad_maximum_fusion.2
  (32 shorter events, 0.2 us)
Async XLA Ops:
  6.5 29.7 %copy-start.1 = (bf16[2,8,16,256]{3,2,1,0:T(8,128)(2,1)S(1)}, bf16[2,8,16,256]{3,2,1,0:T(8,128)(2,1)}, u32[]{:S(2)}) copy-start(bf16[2,8,16,256]{3,2,1,0:T(8,128)(2,1)} %param.6) | copy-start | bytes 393220
  6.5 29.7 %copy-start.11 = (f32[256]{0:T(256)S(1)}, f32[256]{0:T(256)}, u32[]{:S(2)}) copy-start(f32[256]{0:T(256)} %param.7) | copy-start | bytes 3076
  6.5 29.7 %copy-start.10 = (f32[256]{0:T(256)S(1)}, f32[256]{0:T(256)}, u32[]{:S(2)}) copy-start(f32[256]{0:T(256)} %param.8) | copy-start | bytes 3076
  6.5 114.5 %all-gather.2.cloned.1.call-start = ((), (), s32[]{:S(2)}) async-start(), calls=%async_computation.1 | async-start | bytes 7962624 | tf_op jit(solution)/shard_map/all_gather | solution.py:106
  7.3 133.4 %reduce-scatter.2.cloned.1.call-start = ((), (), s32[]{:S(2)}) async-start(), calls=%async_computation.2 | async-start | bytes 1179648 | tf_op jit(solution)/shard_map/reduce_scatter | solution.py:112
  8.2 6.5 %collective-permute-start = (bf16[2,8,4,256]{3,2,1,0:T(4,128)(2,1)S(1)}, bf16[2,8,4,256]{3,2,1,0:T(4,128)(2,1)S(1)}, u32[]{:S(2)}, u32[]{:S(2)}) collective-permute-start(bf16[2,8,4,256]{3,2,1,0:T(4,128)(2,1)S(1)} %get-tuple-element.40), channel_id=1, source_target_pairs={{0,4},{4,8},{8,12},{1,5},{5,9},{9,13},{2,6},{6,10},{10,14},{3,7},{... | collective-permute-start | bytes 98312 | tf_op jit(solution)/shard_map/ppermute | solution.py:17
  13.2 5.8 %collective-permute-start.1 = (bf16[2,8,4,256]{3,2,1,0:T(4,128)(2,1)S(1)}, bf16[2,8,4,256]{3,2,1,0:T(4,128)(2,1)S(1)}, u32[]{:S(2)}, u32[]{:S(2)}) collective-permute-start(bf16[2,8,4,256]{3,2,1,0:T(4,128)(2,1)S(1)} %get-tuple-element.41), channel_id=1, source_target_pairs={{4,0},{8,4},{12,8},{5,1},{9,5},{13,9},{6,2},{10,6},{14,10},{7,3},{... | collective-permute-start | bytes 98312 | tf_op jit(solution)/shard_map/ppermute | solution.py:18
  20.0 11.9 %collective-permute-start.2 = (bf16[2,8,24,256]{3,2,1,0:T(8,128)(2,1)S(1)}, bf16[2,8,24,256]{3,2,1,0:T(8,128)(2,1)S(1)}, u32[]{:S(2)}, u32[]{:S(2)}) collective-permute-start(bf16[2,8,24,256]{3,2,1,0:T(8,128)(2,1)S(1)} %pad_maximum_fusion.1), channel_id=1, source_target_pairs={{0,2},{1,3},{4,6},{5,7},{8,10},{9,11},{12,14},{13,15},{16,18},{17,... | collective-permute-start | bytes 589832 | tf_op jit(solution)/shard_map/ppermute | solution.py:26
  121.1 5.8 %copy-start = (bf16[3,3,3,256,512]{4,3,2,1,0:T(8,128)(2,1)S(1)}, bf16[3,3,3,256,512]{4,3,2,1,0:T(8,128)(2,1)}, u32[]{:S(2)}) copy-start(bf16[3,3,3,256,512]{4,3,2,1,0:T(8,128)(2,1)} %all-gather.2.cloned.1.call-done) | copy-start | bytes 21233668
  121.1 5.9 %copy-start.8 = (bf16[2,8,24,256]{3,2,1,0:T(8,128)(2,1)S(1)}, bf16[2,8,24,256]{3,2,1,0:T(8,128)(2,1)}, u32[]{:S(2)}) copy-start(bf16[2,8,24,256]{3,2,1,0:T(8,128)(2,1)} %get-tuple-element.34) | copy-start | bytes 589828
  127.5 1.9 %copy-start.7 = (bf16[2,8,24,256]{3,2,1,0:T(8,128)(2,1)S(1)}, bf16[2,8,24,256]{3,2,1,0:T(8,128)(2,1)}, u32[]{:S(2)}) copy-start(bf16[2,8,24,256]{3,2,1,0:T(8,128)(2,1)} %get-tuple-element.33) | copy-start | bytes 589828
  129.6 1.9 %copy-start.6 = (bf16[2,8,24,256]{3,2,1,0:T(8,128)(2,1)S(1)}, bf16[2,8,24,256]{3,2,1,0:T(8,128)(2,1)}, u32[]{:S(2)}) copy-start(bf16[2,8,24,256]{3,2,1,0:T(8,128)(2,1)} %get-tuple-element.29) | copy-start | bytes 589828
  129.9 1.9 %copy-start.5 = (bf16[2,8,24,256]{3,2,1,0:T(8,128)(2,1)S(1)}, bf16[2,8,24,256]{3,2,1,0:T(8,128)(2,1)}, u32[]{:S(2)}) copy-start(bf16[2,8,24,256]{3,2,1,0:T(8,128)(2,1)} %get-tuple-element.32) | copy-start | bytes 589828
  130.1 1.9 %copy-start.4 = (bf16[2,8,24,256]{3,2,1,0:T(8,128)(2,1)S(1)}, bf16[2,8,24,256]{3,2,1,0:T(8,128)(2,1)}, u32[]{:S(2)}) copy-start(bf16[2,8,24,256]{3,2,1,0:T(8,128)(2,1)} %get-tuple-element.30) | copy-start | bytes 589828
  130.4 1.9 %copy-start.3 = (bf16[2,8,24,256]{3,2,1,0:T(8,128)(2,1)S(1)}, bf16[2,8,24,256]{3,2,1,0:T(8,128)(2,1)}, u32[]{:S(2)}) copy-start(bf16[2,8,24,256]{3,2,1,0:T(8,128)(2,1)} %get-tuple-element.31) | copy-start | bytes 589828
  130.7 1.9 %copy-start.2 = (bf16[2,8,24,256]{3,2,1,0:T(8,128)(2,1)S(1)}, bf16[2,8,24,256]{3,2,1,0:T(8,128)(2,1)}, u32[]{:S(2)}) copy-start(bf16[2,8,24,256]{3,2,1,0:T(8,128)(2,1)} %get-tuple-element.28) | copy-start | bytes 589828
  131.2 2.8 %copy-start.9 = (s32[4]{0:T(128)S(1)}, s32[4]{0:T(128)}, u32[]{:S(2)}) copy-start(s32[4]{0:T(128)} %param.11) | copy-start | bytes 52
  131.2 9.4 %copy-start.12 = (f32[256]{0:T(256)S(1)}, f32[256]{0:T(256)}, u32[]{:S(2)}) copy-start(f32[256]{0:T(256)} %param.10) | copy-start | bytes 3076
  141.7 5.2 %collective-permute-start.3 = (bf16[2,8,4,256]{3,2,1,0:T(4,128)(2,1)S(1)}, bf16[2,8,4,256]{3,2,1,0:T(4,128)(2,1)S(1)}, u32[]{:S(2)}, u32[]{:S(2)}) collective-permute-start(bf16[2,8,4,256]{3,2,1,0:T(4,128)(2,1)S(1)} %get-tuple-element.38), channel_id=1, source_target_pairs={{0,4},{4,8},{8,12},{1,5},{5,9},{9,13},{2,6},{6,10},{10,14},{3,7},{... | collective-permute-start | bytes 98312 | tf_op jit(solution)/shard_map/ppermute | solution.py:17
  145.4 5.8 %collective-permute-start.4 = (bf16[2,8,4,256]{3,2,1,0:T(4,128)(2,1)S(1)}, bf16[2,8,4,256]{3,2,1,0:T(4,128)(2,1)S(1)}, u32[]{:S(2)}, u32[]{:S(2)}) collective-permute-start(bf16[2,8,4,256]{3,2,1,0:T(4,128)(2,1)S(1)} %get-tuple-element.39), channel_id=1, source_target_pairs={{4,0},{8,4},{12,8},{5,1},{9,5},{13,9},{6,2},{10,6},{14,10},{7,3},{... | collective-permute-start | bytes 98312 | tf_op jit(solution)/shard_map/ppermute | solution.py:18
Sparse Core Ops, SparseCore 0:
  9.5 111.4 all-gather.1
  134.2 6.4 reduce-scatter.1
where the time goes:
time: 159 us
  waiting for transfers between devices  101 us (64%)
  between operations  15.8 us (10%)
  starting transfers between devices  14.6 us (9%)
  matrix products  12.6 us (8%)
  other arithmetic  7.56 us (5%)
  local copies, waits for them, and re-layouts  7.04 us (4%)
    all_gather x1, waiting for transfers between devices, on_device(): lax.all_gather(kernel, ('tile', 'tm'), axis=3, tiled=True)  81.3 us
    dot_general x27, matrix products, conv_taps(): jnp.dot(window.reshape(-1, in_width), kernel_part[tap_time, tap_row, tap_...  12.6 us
    ppermute x2, starting transfers between devices, with_halo(): before = lax.ppermute(last, axis, up)  8.55 us
    ppermute x2, waiting for transfers between devices, with_halo(): after = lax.ppermute(leading, axis, down)  8.46 us
    ppermute x1, waiting for transfers between devices, passed_along(): return lax.ppermute(block, axis, route)  5.61 us
    reduce_scatter x1, waiting for transfers between devices, on_device(): summed = lax.psum_scatter(joined, 'ch', scatter_dimension=3, tiled=True)  4.61 us
    ppermute x1, starting transfers between devices, passed_along(): return lax.ppermute(block, axis, route)  3.41 us
  transfers between devices with their start and end apart: 7, of which 7 were waited for; matrix products, arithmetic and copies ran while one was open for 8% of the time, Pallas kernels for 0%

commit v1 on v0

--- a/solution.py
+++ b/solution.py
@@ -1,10 +1,23 @@
+import functools
+
 import jax
 import jax.numpy as jnp
 from jax import lax
+from jax.experimental import pallas as pl
+from jax.experimental.pallas import tpu as pltpu
 from jax.sharding import PartitionSpec as P
 
 GROUPS = 32
 RIM = 4
+TAPS = 3
+
+
+def ramp_weight(profile, position, margin):
+    fraction = (position.astype(jnp.float32) + 0.5) / (2.0 * margin)
+    exponent = 1.0 + profile.astype(jnp.float32)
+    near_part = jnp.power(1.0 - fraction, exponent)
+    far_part = jnp.power(fraction, exponent)
+    return near_part / (near_part + far_part)
 
 
 def with_halo(shard, sides, width):
@@ -24,14 +37,6 @@
     devices = range(lax.axis_size(axis))
     route = [(i - distance, i) for i in devices if i - distance in devices]
     return lax.ppermute(block, axis, route)
-
-
-def ramp_weight(profile, position, margin):
-    fraction = (position.astype(jnp.float32) + 0.5) / (2.0 * margin)
-    exponent = 1.0 + profile.astype(jnp.float32)
-    near_part = jnp.power(1.0 - fraction, exponent)
-    far_part = jnp.power(fraction, exponent)
-    return near_part / (near_part + far_part)
 
 
 def frame_stats(values, colmask, groups):
@@ -74,7 +79,7 @@
     return running
 
 
-def on_device(latent, norm_gain, norm_shift, kernel, conv_bias, blend_profile):
+def gathered_plan(latent, norm_gain, norm_shift, kernel, conv_bias, blend_profile):
     frame_count, row_count, core_cols, chan_half = latent.shape
     out_chans = kernel.shape[4]
     groups = GROUPS // lax.axis_size("ch")
@@ -92,23 +97,10 @@
     )
     center, inverse = frame_stats(frames, colmask, groups)
     activated = activate(frames, center, inverse, norm_gain, norm_shift, colmask, timemask, groups)
-    inputs = (jnp.pad(activated, ((0, 0), (1, 1), (1, 1), (0, 0))),)
-    widths = (ncols,)
-
-    def accumulate(shard_rows):
-        return tuple(
-            (
-                conv_taps(source, shard_rows, frame_count, row_count, width_cols)
-                for source, width_cols in zip(inputs, widths)
-            )
-        )
-
-    totals = accumulate(lax.all_gather(kernel, ("tile", "tm"), axis=3, tiled=True))
-    shaped = [
-        running.reshape(frame_count, row_count, width_cols, out_chans)
-        for running, width_cols in zip(totals, widths)
-    ]
-    joined = shaped[0]
+    padded = jnp.pad(activated, ((0, 0), (1, 1), (1, 1), (0, 0)))
+    whole_kernel = lax.all_gather(kernel, ("tile", "tm"), axis=3, tiled=True)
+    running = conv_taps(padded, whole_kernel, frame_count, row_count, ncols)
+    joined = running.reshape(frame_count, row_count, ncols, out_chans)
     summed = lax.psum_scatter(joined, "ch", scatter_dimension=3, tiled=True)
     tile_out = (summed + conv_bias).astype(jnp.bfloat16)
     extended = with_halo(tile_out, (("tile", 2),), RIM)
@@ -133,6 +125,258 @@
     return jnp.concatenate([head_cols, middle, tail_cols], axis=2).astype(jnp.bfloat16)
 
 
+VMEM_BYTES = 48 * 1024 * 1024
+
+
+def resident_fits(mesh, latent, kernel):
+    return (
+        mesh["tile"] == 4
+        and mesh["tm"] == 2
+        and mesh["ch"] == 2
+        and latent.shape == (2, 8, 16, 256)
+        and kernel.shape == (TAPS, TAPS, TAPS, 32, 512)
+    )
+
+
+def call(body, outs, scratch=(), smem_first=True):
+    vmem = pl.BlockSpec(memory_space=pltpu.VMEM)
+    smem = pl.BlockSpec(memory_space=pltpu.SMEM)
+
+    def run(*args):
+        specs = [smem if smem_first and i == 0 else vmem for i in range(len(args))]
+        return pl.pallas_call(
+            body,
+            out_shape=outs,
+            in_specs=specs,
+            out_specs=jax.tree.map(lambda _: vmem, outs),
+            scratch_shapes=list(scratch),
+            compiler_params=pltpu.CompilerParams(vmem_limit_bytes=VMEM_BYTES),
+        )(*args)
+
+    return run
+
+
+def pack_body(pos, latent, *outs):
+    z = pos[0]
+    first = latent[0].astype(jnp.float32)
+    second = latent[1].astype(jnp.float32)
+    for owner in range(4):
+        lanes = slice(64 * owner, 64 * owner + 64)
+        block = jnp.concatenate([first[..., lanes], second[..., lanes]], axis=-1)
+        block = block.astype(jnp.bfloat16)
+        for k in range(4):
+
+            @pl.when(z == owner ^ k)
+            def _():
+                outs[k][...] = block
+
+
+def group_sum(rows):
+    lane = lax.broadcasted_iota(jnp.int32, rows.shape, 1)
+    for step in (1, 2, 4, 8):
+        ahead = pltpu.roll(rows, 128 - step, 1)
+        behind = pltpu.roll(rows, step, 1)
+        rows = rows + jnp.where((lane & step) == 0, ahead, behind)
+    return rows
+
+
+def norm_body(pos, gain, shift, *refs):
+    blocks, (out, placed, raw) = refs[:8], refs[8:]
+    z, x = pos[0], pos[1]
+    for k in range(4):
+        placed[x, z ^ k] = blocks[k][...]
+        placed[1 - x, z ^ k] = blocks[4 + k][...]
+    for p in range(2):
+        raw[p, :, 0:4, :] = jnp.zeros((8, 4, 128), jnp.float32)
+        raw[p, :, 68:72, :] = jnp.zeros((8, 4, 128), jnp.float32)
+        for t in range(4):
+            raw[p, :, 4 + 16 * t : 20 + 16 * t, :] = placed[p, t].astype(jnp.float32)
+    col = lax.broadcasted_iota(jnp.int32, (24, 128), 0)
+    present = {0: col >= 4, 3: col < 20}
+    count_row = lax.broadcasted_iota(jnp.int32, (8, 128), 0) % 4
+    cells = jnp.where((count_row == 0) | (count_row == 3), 20.0, 24.0) * 128.0
+
+    def window(p, t):
+        return raw[p, :, 16 * t : 16 * t + 24, :]
+
+    sums = []
+    for p in range(2):
+        for t in range(4):
+            over_rows = jnp.sum(window(p, t), axis=0)
+            sums.append(jnp.sum(over_rows, axis=0, keepdims=True))
+    center = group_sum(jnp.concatenate(sums, axis=0)) / cells
+    sums = []
+    for p in range(2):
+        for t in range(4):
+            at = 4 * p + t
+            spread = window(p, t) - center[at : at + 1][None]
+            over_rows = jnp.sum(spread * spread, axis=0)
+            if t in present:
+                over_rows = jnp.where(present[t], over_rows, 0.0)
+            sums.append(jnp.sum(over_rows, axis=0, keepdims=True))
+    inverse = lax.rsqrt(group_sum(jnp.concatenate(sums, axis=0)) / cells + 1e-06)
+    scale = inverse * gain[...]
+    offset = shift[...]
+    for p in range(2):
+        for half in range(2):
+            acts = []
+            for t in (2 * half, 2 * half + 1):
+                at = 4 * p + t
+                normed = (window(p, t) - center[at : at + 1][None]) * scale[at : at + 1][None]
+                near = 0.5 * (normed + offset[None])
+                act = near + near * jnp.tanh(near)
+                if t in present:
+                    act = jnp.where(present[t][None], act, 0.0)
+                acts.append(act)
+            joined = jnp.concatenate(acts, axis=1).astype(jnp.bfloat16)
+            out[p, :, 48 * half : 48 * half + 48, :] = joined
+
+
+def weights_body(pos, same, other, same_far, other_far, diag, lower):
+    x = pos[1]
+    zero = jnp.zeros((32, 128), jnp.bfloat16)
+    for b in range(TAPS):
+        for e in range(TAPS):
+            for core, (near, far) in enumerate(((same, same_far), (other, other_far))):
+                for f in range(2):
+                    base = e * 256 + core * 128 + f * 64
+                    for g in range(2):
+                        tap_d, tap_l = f - g + 2, f - g
+                        for source, slot in ((near, x), (far, 1 - x)):
+                            rows = pl.ds(pl.multiple_of(base + 32 * slot, 32), 32)
+                            lanes = slice(128 * g, 128 * g + 128)
+                            diag[b, rows, lanes] = source[tap_d, b, e] if tap_d < 3 else zero
+                            lower[b, rows, lanes] = source[tap_l, b, e] if tap_l >= 0 else zero
+
+
+def conv_body(pos, mine, sibling, diag, lower, blend, *refs):
+    own, sends, (stacked, summed, blocks) = refs[0], refs[1:8], refs[8:]
+    z, x = pos[0], pos[1]
+    col = lax.broadcasted_iota(jnp.int32, (24, 128), 0)
+    for p in range(2):
+        edge = jnp.zeros((96, 768), jnp.bfloat16)
+        stacked[p, 0:96, :] = edge
+        stacked[p, 864:960, :] = edge
+        for core, source in enumerate((mine, sibling)):
+            act = source[p].reshape(768, 128)
+            wide = act.astype(jnp.float32)
+            before = pltpu.roll(wide, 1, 0).reshape(32, 24, 128)
+            before = jnp.where((col > 0)[None], before, 0.0).reshape(768, 128)
+            after = pltpu.roll(wide, 767, 0).reshape(32, 24, 128)
+            after = jnp.where((col < 23)[None], after, 0.0).reshape(768, 128)
+            lanes = 128 * core
+            stacked[p, 96:864, lanes : lanes + 128] = before.astype(jnp.bfloat16)
+            stacked[p, 96:864, 256 + lanes : 384 + lanes] = act
+            stacked[p, 96:864, 512 + lanes : 640 + lanes] = after.astype(jnp.bfloat16)
+
+    def product(p, b, matrix):
+        rows = stacked[p, 96 * b : 96 * b + 768, :]
+        return jnp.dot(rows, matrix[b], preferred_element_type=jnp.float32)
+
+    for p in range(2):
+        total = sum(product(p, b, diag) for b in range(TAPS))
+        if p == 1:
+            total = total + sum(product(0, b, lower) for b in range(TAPS))
+        total = total.reshape(8, 96, 256)
+        for t in range(4):
+            start = 24 * t
+            left = total[:, start : start + 8]
+            if t > 0:
+                share = blend[t - 1][None]
+                left = share * total[:, start - 8 : start] + (1.0 - share) * left
+            summed[:, 16 * t : 16 * t + 8, :] = left
+            summed[:, 16 * t + 8 : 16 * t + 16, :] = total[:, start + 8 : start + 16]
+        summed[:, 64:72, :] = total[:, 88:96]
+        for t in range(4):
+            blocks[p, t] = summed[:, 4 + 16 * t : 20 + 16 * t, :]
+    own[...] = blocks[x, z]
+    for k in range(1, 4):
+        sends[k - 1][...] = blocks[x, z ^ k].astype(jnp.bfloat16)
+    for k in range(4):
+        sends[3 + k][...] = blocks[1 - x, z ^ k].astype(jnp.bfloat16)
+
+
+def join_body(pos, bias, own, *refs):
+    same, far, out = refs[:3], refs[3:7], refs[7]
+    x = pos[1]
+    near_sum = own[...]
+    for part in same:
+        near_sum = near_sum + part[...].astype(jnp.float32)
+    far_sum = far[0][...].astype(jnp.float32)
+    for part in far[1:]:
+        far_sum = far_sum + part[...].astype(jnp.float32)
+    low = jnp.where(x == 0, near_sum, far_sum)
+    high = jnp.where(x == 0, far_sum, near_sum)
+    for f in range(2):
+        lanes = slice(128 * f, 128 * f + 128)
+        out[f, :, :, 0:128] = (low[..., lanes] + bias[:, 0:128][None]).astype(jnp.bfloat16)
+        out[f, :, :, 128:256] = (high[..., lanes] + bias[:, 128:256][None]).astype(jnp.bfloat16)
+
+
+def exchanged(block, k, j):
+    tms = lax.axis_size("tm")
+    tiles = lax.axis_size("tile")
+    route = [(t * tms + m, (t ^ k) * tms + (m ^ j)) for t in range(tiles) for m in range(tms)]
+    return lax.ppermute(block, ("tile", "tm"), route)
+
+
+def across(block, j):
+    route = [(2 * m + c, 2 * (m ^ j) + (1 - c)) for m in range(2) for c in range(2)]
+    return lax.ppermute(block, ("tm", "ch"), route)
+
+
+def resident_plan(latent, norm_gain, norm_shift, kernel, conv_bias, blend_profile):
+    bf16, f32 = jnp.bfloat16, jnp.float32
+    z, x, c = lax.axis_index("tile"), lax.axis_index("tm"), lax.axis_index("ch")
+    pos = jnp.stack([z, x]).astype(jnp.int32)
+    block = jax.ShapeDtypeStruct((8, 16, 128), bf16)
+    wide = jax.ShapeDtypeStruct((8, 16, 256), bf16)
+
+    packed = call(pack_body, [block] * 4)(pos, latent)
+    near = [packed[0]] + [exchanged(packed[k], k, 0) for k in (1, 2, 3)]
+    far = [exchanged(packed[k], k, 1) for k in range(4)]
+
+    def quarter(core, frame_block):
+        start = core * 256 + frame_block * 128
+        return lax.dynamic_slice_in_dim(kernel, start, 128, axis=4)
+
+    same = quarter(c, x)
+    other = across(quarter(1 - c, x), 0)
+    same_far = exchanged(quarter(c, 1 - x), 0, 1)
+    other_far = across(quarter(1 - c, 1 - x), 1)
+    matrix = jax.ShapeDtypeStruct((TAPS, 768, 256), bf16)
+    diag, lower = call(weights_body, [matrix] * 2)(pos, same, other, same_far, other_far)
+
+    def lanes_of(vector):
+        part = lax.dynamic_slice_in_dim(vector, z * 64, 64)
+        return jnp.concatenate([part, part])[None]
+
+    acts = call(
+        norm_body,
+        jax.ShapeDtypeStruct((2, 8, 96, 128), bf16),
+        [pltpu.VMEM((2, 4, 8, 16, 128), bf16), pltpu.VMEM((2, 8, 72, 128), f32)],
+    )(pos, lanes_of(norm_gain), lanes_of(norm_shift), *near, *far)
+    sibling = lax.ppermute(acts, "ch", [(0, 1), (1, 0)])
+
+    offsets = jnp.arange(2 * RIM, dtype=jnp.int32)
+    ramps = ramp_weight(blend_profile[:3, None], offsets[None, :], RIM)
+    blend = jnp.broadcast_to(ramps[:, :, None], (3, 2 * RIM, 256))
+    own, *sends = call(
+        conv_body,
+        [jax.ShapeDtypeStruct((8, 16, 256), f32)] + [wide] * 7,
+        [
+            pltpu.VMEM((2, 960, 768), bf16),
+            pltpu.VMEM((8, 72, 256), f32),
+            pltpu.VMEM((2, 4, 8, 16, 256), f32),
+        ],
+    )(pos, acts, sibling, diag, lower, blend)
+    near_sums = [exchanged(sends[k - 1], k, 0) for k in (1, 2, 3)]
+    far_sums = [exchanged(sends[3 + k], k, 1) for k in range(4)]
+    return call(join_body, jax.ShapeDtypeStruct(latent.shape, bf16))(
+        pos, conv_bias[None], own, *near_sums, *far_sums
+    )
+
+
 def solution(mesh):
     in_specs = (
         P(("grp", "tm"), None, "tile", "ch"),
@@ -143,6 +387,11 @@
         P(),
     )
     out_specs = P(("grp", "tm"), None, "tile", "ch")
+
+    def on_device(latent, norm_gain, norm_shift, kernel, conv_bias, blend_profile):
+        plan = resident_plan if resident_fits(mesh.shape, latent, kernel) else gathered_plan
+        return plan(latent, norm_gain, norm_shift, kernel, conv_bias, blend_profile)
+
     return jax.shard_map(
         on_device, mesh=mesh, in_specs=in_specs, out_specs=out_specs, check_vma=False
     )

time: 159 us -> 51.5 us (0.32)
  waiting for transfers between devices: 101 us -> 15.8 us
  between operations: 15.8 us -> 0.13 us
  matrix products: 12.6 us -> 0 us
  starting transfers between devices: 14.6 us -> 24.4 us
  Pallas kernels: 0 us -> 8.27 us
  other arithmetic: 7.56 us -> 0.24 us
  local copies, waits for them, and re-layouts: 7.04 us -> 2.49 us
    all_gather x1 -> x0, waiting for transfers between devices: 81.3 us -> none  [on_device(): lax.all_gather(kernel, ('tile', 'tm'), axis=3, tiled=True)]
    dot_general x27 -> x0, matrix products: 12.6 us -> none  [conv_taps(): jnp.dot(window.reshape(-1, in_width), kernel_part[tap_time, tap_row, tap_...]
    ppermute x5 -> x18, starting transfers between devices: 14.5 us -> 24.4 us  [the longest x15 24.3 us: exchanged(): return lax.ppermute(block, ('tile', 'tm'), route)]
    pallas_call x0 -> x5, Pallas kernels: none -> 8.27 us  [run(): pl.pallas_call(body, out_shape=outs, in_specs=specs, out_specs=jax.tree.m...]
    reduce_scatter x1 -> x0, waiting for transfers between devices: 4.61 us -> none  [on_device(): summed = lax.psum_scatter(joined, 'ch', scatter_dimension=3, tiled=True)]
    reduce_sum x3 -> x0, other arithmetic: 3.51 us -> none  [the longest x1 1.7 us: frame_stats(): jnp.sum(spread * spread, axis=(1, 2, 4)) / counted + 1e-06]
    slice x5 -> x0, local copies, waits for them, and re-layouts: 3.36 us -> none  [the longest x2 2.42 us: conv_taps(): padded[tap_time:tap_time + frame_count, tap_row:tap_row + row_count, tap_...]
    concatenate x3 -> x0, local copies, waits for them, and re-layouts: 2.63 us -> none  [the longest x2 2.11 us: on_device(): frames = jnp.concatenate([cached, window_in], axis=0).astype(jnp.float32)]
  transfers between devices with their start and end apart: 7 -> 18, of which waited for: 7 -> 6; matrix products, arithmetic and copies ran while one was open for 8% -> 3% of each run, Pallas kernels for 0% -> 5%
where the time goes in v1:
time: 51.5 us; the launch traced here: 51.4 us
  starting transfers between devices  24.4 us (47%)
  waiting for transfers between devices  15.8 us (31%)
  Pallas kernels  8.27 us (16%)
  local copies, waits for them, and re-layouts  2.49 us (5%)
    ppermute x15, starting transfers between devices, exchanged(): return lax.ppermute(block, ('tile', 'tm'), route)  24.3 us
    ppermute x15, waiting for transfers between devices, exchanged(): return lax.ppermute(block, ('tile', 'tm'), route)  14.6 us
    pallas_call x5, Pallas kernels, run(): pl.pallas_call(body, out_shape=outs, in_specs=specs, out_specs=jax.tree.m...  8.27 us
    dynamic_slice x1, local copies, waits for them, and re-layouts, quarter(): return lax.dynamic_slice_in_dim(kernel, start, 128, axis=4)  1.35 us
    ppermute x2, waiting for transfers between devices, across(): return lax.ppermute(block, ('tm', 'ch'), route)  1.25 us
  transfers between devices with their start and end apart: 18, of which 6 were waited for; matrix products, arithmetic and copies ran while one was open for 3% of the time, Pallas kernels for 5%

profile of v1, /device:TPU:0, one launch (start us, length us, event | category | flops | bytes accessed | tf_op | source)
XLA Modules:
  0.0 51.4 jit_solution(8688348833397024059)
XLA Ops:
  0.0 0.0 copy-start.2
  0.0 0.0 copy-start.3
  0.0 0.1 pad_add_fusion.pos
  0.1 0.0 copy-start
  0.1 0.9 %copy-done = bf16[2,8,16,256]{3,2,1,0:T(8,128)(2,1)S(1)} copy-done((bf16[2,8,16,256]{3,2,1,0:T(8,128)(2,1)S(1)}, bf16[2,8,16,256]{3,2,1,0:T(8,128)(2,1)}, u32[]{:S(2)}) %copy-start) | copy-done | bytes 131096
  1.0 0.9 %shard_map.64 = (bf16[8,16,128]{2,1,0:T(8,128)(2,1)S(1)}, bf16[8,16,128]{2,1,0:T(8,128)(2,1)S(1)}, bf16[8,16,128]{2,1,0:T(8,128)(2,1)S(1)}, bf16[8,16,128]{2,1,0:T(8,128)(2,1)S(1)}) custom-call(s32[2]{0:T(128)S(1)} %pad_add_fusion.pos, bf16[2,8,16,256]{3,2,1,0:T(8,128)(2,1)S(1)} %copy-done), custom_call_target="tpu_custom_call" | custom-call | tf_op jit(solution)/shard_map/pallas_call | solution.py:147
  1.9 3.1 %collective-permute-start = (bf16[8,16,128]{2,1,0:T(8,128)(2,1)S(1)}, bf16[8,16,128]{2,1,0:T(8,128)(2,1)S(1)}, u32[]{:S(2)}, u32[]{:S(2)}) collective-permute-start(bf16[8,16,128]{2,1,0:T(8,128)(2,1)S(1)} %get-tuple-element.20), channel_id=1, source_target_pairs={{0,4},{2,6},{4,0},{6,2},{8,12},{10,14},{12,8},{14,10},{1,5},{3,7},... | collective-permute-start | bytes 98312 | tf_op jit(solution)/shard_map/ppermute | solution.py:320
  4.9 1.4 %collective-permute-start.4 = (bf16[8,16,128]{2,1,0:T(8,128)(2,1)S(1)}, bf16[8,16,128]{2,1,0:T(8,128)(2,1)S(1)}, u32[]{:S(2)}, u32[]{:S(2)}) collective-permute-start(bf16[8,16,128]{2,1,0:T(8,128)(2,1)S(1)} %get-tuple-element.20), channel_id=1, source_target_pairs={{0,6},{2,4},{4,2},{6,0},{8,14},{10,12},{12,10},{14,8},{1,7},{3,5},... | collective-permute-start | bytes 98312 | tf_op jit(solution)/shard_map/ppermute | solution.py:320
  6.3 2.6 %collective-permute-start.1 = (bf16[8,16,128]{2,1,0:T(8,128)(2,1)S(1)}, bf16[8,16,128]{2,1,0:T(8,128)(2,1)S(1)}, u32[]{:S(2)}, u32[]{:S(2)}) collective-permute-start(bf16[8,16,128]{2,1,0:T(8,128)(2,1)S(1)} %get-tuple-element.21), channel_id=1, source_target_pairs={{0,8},{2,10},{4,12},{6,14},{8,0},{10,2},{12,4},{14,6},{1,9},{3,11}... | collective-permute-start | bytes 98312 | tf_op jit(solution)/shard_map/ppermute | solution.py:320
  8.9 0.0 collective-permute-start.5
  8.9 3.9 %collective-permute-start.2 = (bf16[8,16,128]{2,1,0:T(8,128)(2,1)S(1)}, bf16[8,16,128]{2,1,0:T(8,128)(2,1)S(1)}, u32[]{:S(2)}, u32[]{:S(2)}) collective-permute-start(bf16[8,16,128]{2,1,0:T(8,128)(2,1)S(1)} %get-tuple-element.22), channel_id=1, source_target_pairs={{0,12},{2,14},{4,8},{6,10},{8,4},{10,6},{12,0},{14,2},{1,13},{3,15... | collective-permute-start | bytes 98312 | tf_op jit(solution)/shard_map/ppermute | solution.py:320
  12.8 0.0 copy-start.4
  12.8 1.4 %constant_dynamic-slice_fusion = (bf16[3,3,3,32,128]{4,3,2,1,0:T(8,128)(2,1)S(1)}, bf16[3,3,3,32,128]{4,3,2,1,0:T(8,128)(2,1)S(1)}, bf16[3,3,3,32,128]{4,3,2,1,0:T(8,128)(2,1)S(1)}, bf16[3,3,3,32,128]{4,3,2,1,0:T(8,128)(2,1)S(1)}) fusion(bf16[3,3,3,32,512]{4,3,2,1,0:T(8,128)(2,1)} %param.9, s32[]{:T(128)S(6)} %select_n.20, s32[]{:T(128)S(6)} %select_n.18, ...), kind=kLoop, calls=%fused_computation.1 | loop fusion | bytes 1769488 | tf_op jit(solution)/shard_map/dynamic_slice | solution.py:341
  14.2 0.0 copy-done.2
  14.2 0.1 dynamic_slice.18
  14.3 0.0 copy-done.3
  14.3 0.1 dynamic_slice.19
  14.3 0.0 collective-permute-done.refs_1_
  14.3 1.2 %collective-permute-start.6 = (bf16[8,16,128]{2,1,0:T(8,128)(2,1)S(1)}, bf16[8,16,128]{2,1,0:T(8,128)(2,1)S(1)}, u32[]{:S(2)}, u32[]{:S(2)}) collective-permute-start(bf16[8,16,128]{2,1,0:T(8,128)(2,1)S(1)} %get-tuple-element.22), channel_id=1, source_target_pairs={{0,14},{2,12},{4,10},{6,8},{8,6},{10,4},{12,2},{14,0},{1,15},{3,13... | collective-permute-start | bytes 98312 | tf_op jit(solution)/shard_map/ppermute | solution.py:320
  15.5 0.0 collective-permute-done.1.refs_2_
  15.5 0.4 collective-permute-start.3
  15.9 0.1 maximum_bitcast_fusion
  16.0 0.0 collective-permute-done.2.refs_3_
  16.0 0.0 collective-permute-start.10
  16.0 3.7 %collective-permute-done.3.refs_4_ = bf16[8,16,128]{2,1,0:T(8,128)(2,1)S(1)} collective-permute-done((bf16[8,16,128]{2,1,0:T(8,128)(2,1)S(1)}, bf16[8,16,128]{2,1,0:T(8,128)(2,1)S(1)}, u32[]{:S(2)}, u32[]{:S(2)}) %collective-permute-start.3) | collective-permute-done | bytes 32800 | tf_op jit(solution)/shard_map/ppermute | solution.py:320
  19.8 0.0 collective-permute-start.8
  19.8 0.0 collective-permute-done.4.refs_5_
  19.8 0.4 collective-permute-start.9
  20.2 0.0 collective-permute-done.5.refs_6_
  20.2 0.9 %collective-permute-done.6.refs_7_ = bf16[8,16,128]{2,1,0:T(8,128)(2,1)S(1)} collective-permute-done((bf16[8,16,128]{2,1,0:T(8,128)(2,1)S(1)}, bf16[8,16,128]{2,1,0:T(8,128)(2,1)S(1)}, u32[]{:S(2)}, u32[]{:S(2)}) %collective-permute-start.6) | collective-permute-done | bytes 32800 | tf_op jit(solution)/shard_map/ppermute | solution.py:320
  21.1 1.5 %shard_map.65.mine = bf16[2,8,96,128]{3,2,1,0:T(8,128)(2,1)S(1)} custom-call(s32[2]{0:T(128)S(1)} %pad_add_fusion.pos, f32[1,128]{1,0:T(1,128)S(1)} %get-tuple-element.37.gain, f32[1,128]{1,0:T(1,128)S(1)} %get-tuple-element.38.shift, bf16[8,16,128]{2,1,0:T(8,128)(2,1)S(1)} %get-tuple-element.19.refs_0_, ...), custom_call_target="tpu_custom_call" | custom-call | tf_op jit(solution)/shard_map/pallas_call | solution.py:147
  22.6 0.1 collective-permute-start.7
  22.7 0.0 copy-done.4
  22.7 0.1 add_divide_fusion
  22.8 1.2 %collective-permute-done.10.other_far = bf16[3,3,3,32,128]{4,3,2,1,0:T(8,128)(2,1)S(1)} collective-permute-done((bf16[3,3,3,32,128]{4,3,2,1,0:T(8,128)(2,1)S(1)}, bf16[3,3,3,32,128]{4,3,2,1,0:T(8,128)(2,1)S(1)}, u32[]{:S(2)}, u32[]{:S(2)}) %collective-permute-start.10) | collective-permute-done | bytes 221216 | tf_op jit(solution)/shard_map/ppermute | solution.py:325
  24.0 0.0 collective-permute-done.8.other
  24.0 5.2 %collective-permute-done.9.same_far = bf16[3,3,3,32,128]{4,3,2,1,0:T(8,128)(2,1)S(1)} collective-permute-done((bf16[3,3,3,32,128]{4,3,2,1,0:T(8,128)(2,1)S(1)}, bf16[3,3,3,32,128]{4,3,2,1,0:T(8,128)(2,1)S(1)}, u32[]{:S(2)}, u32[]{:S(2)}) %collective-permute-start.9) | collective-permute-done | bytes 221216 | tf_op jit(solution)/shard_map/ppermute | solution.py:320
  29.2 0.9 %shard_map.66 = (bf16[3,768,256]{2,1,0:T(8,128)(2,1)S(1)}, bf16[3,768,256]{2,1,0:T(8,128)(2,1)S(1)}) custom-call(s32[2]{0:T(128)S(1)} %pad_add_fusion.pos, bf16[3,3,3,32,128]{4,3,2,1,0:T(8,128)(2,1)S(1)} %get-tuple-element.35.same, bf16[3,3,3,32,128]{4,3,2,1,0:T(8,128)(2,1)S(1)} %collective-permute-done.8.other, ...), custom_call_target="tpu_custom_call" | custom-call | tf_op jit(solution)/shard_map/pallas_call | solution.py:147
  30.1 0.0 collective-permute-done.7.sibling
  30.1 0.1 broadcast_in_dim.20.blend
  30.1 0.0 copy-start.1
  30.1 3.8 %shard_map.67 = (f32[8,16,256]{2,1,0:T(8,128)S(1)}, bf16[8,16,256]{2,1,0:T(8,128)(2,1)S(1)}, bf16[8,16,256]{2,1,0:T(8,128)(2,1)S(1)}, bf16[8,16,256]{2,1,0:T(8,1...) custom-call(s32[2]{0:T(128)S(1)} %pad_add_fusion.pos, ...), custom_call_target="tpu_custom_call" | custom-call | tf_op jit(solution)/shard_map/pallas_call | solution.py:147
  33.9 0.1 collective-permute-start.11
  34.0 3.9 %collective-permute-start.12 = (bf16[8,16,256]{2,1,0:T(8,128)(2,1)S(1)}, bf16[8,16,256]{2,1,0:T(8,128)(2,1)S(1)}, u32[]{:S(2)}, u32[]{:S(2)}) collective-permute-start(bf16[8,16,256]{2,1,0:T(8,128)(2,1)S(1)} %get-tuple-element.27), channel_id=1, source_target_pairs={{0,8},{2,10},{4,12},{6,14},{8,0},{10,2},{12,4},{14,6},{1,9},{3,11}... | collective-permute-start | bytes 196616 | tf_op jit(solution)/shard_map/ppermute | solution.py:320
  37.8 0.5 collective-permute-start.13
  38.4 0.4 collective-permute-start.14
  38.7 1.1 %collective-permute-start.15 = (bf16[8,16,256]{2,1,0:T(8,128)(2,1)S(1)}, bf16[8,16,256]{2,1,0:T(8,128)(2,1)S(1)}, u32[]{:S(2)}, u32[]{:S(2)}) collective-permute-start(bf16[8,16,256]{2,1,0:T(8,128)(2,1)S(1)} %get-tuple-element.30), channel_id=1, source_target_pairs={{0,6},{2,4},{4,2},{6,0},{8,14},{10,12},{12,10},{14,8},{1,7},{3,5},... | collective-permute-start | bytes 196616 | tf_op jit(solution)/shard_map/ppermute | solution.py:320
  39.9 0.0 collective-permute-done.11.refs_0_
  39.9 3.3 %collective-permute-start.16 = (bf16[8,16,256]{2,1,0:T(8,128)(2,1)S(1)}, bf16[8,16,256]{2,1,0:T(8,128)(2,1)S(1)}, u32[]{:S(2)}, u32[]{:S(2)}) collective-permute-start(bf16[8,16,256]{2,1,0:T(8,128)(2,1)S(1)} %get-tuple-element.31), channel_id=1, source_target_pairs={{0,10},{2,8},{4,14},{6,12},{8,2},{10,0},{12,6},{14,4},{1,11},{3,9}... | collective-permute-start | bytes 196616 | tf_op jit(solution)/shard_map/ppermute | solution.py:320
  43.1 0.0 collective-permute-done.12.refs_1_
  43.1 2.2 %collective-permute-start.17 = (bf16[8,16,256]{2,1,0:T(8,128)(2,1)S(1)}, bf16[8,16,256]{2,1,0:T(8,128)(2,1)S(1)}, u32[]{:S(2)}, u32[]{:S(2)}) collective-permute-start(bf16[8,16,256]{2,1,0:T(8,128)(2,1)S(1)} %get-tuple-element.32), channel_id=1, source_target_pairs={{0,14},{2,12},{4,10},{6,8},{8,6},{10,4},{12,2},{14,0},{1,15},{3,13... | collective-permute-start | bytes 196616 | tf_op jit(solution)/shard_map/ppermute | solution.py:320
  45.3 0.0 collective-permute-done.13.refs_2_
  45.3 0.0 collective-permute-done.14.refs_3_
  45.3 0.0 collective-permute-done.15.refs_4_
  45.3 1.3 %collective-permute-done.16.refs_5_ = bf16[8,16,256]{2,1,0:T(8,128)(2,1)S(1)} collective-permute-done((bf16[8,16,256]{2,1,0:T(8,128)(2,1)S(1)}, bf16[8,16,256]{2,1,0:T(8,128)(2,1)S(1)}, u32[]{:S(2)}, u32[]{:S(2)}) %collective-permute-start.16) | collective-permute-done | bytes 65568 | tf_op jit(solution)/shard_map/ppermute | solution.py:320
  46.6 3.5 %collective-permute-done.17.refs_6_ = bf16[8,16,256]{2,1,0:T(8,128)(2,1)S(1)} collective-permute-done((bf16[8,16,256]{2,1,0:T(8,128)(2,1)S(1)}, bf16[8,16,256]{2,1,0:T(8,128)(2,1)S(1)}, u32[]{:S(2)}, u32[]{:S(2)}) %collective-permute-start.17) | collective-permute-done | bytes 65568 | tf_op jit(solution)/shard_map/ppermute | solution.py:320
  50.1 0.0 copy-done.1
  50.1 1.3 %shard_map.68 = bf16[2,8,16,256]{3,2,1,0:T(8,128)(2,1)} custom-call(s32[2]{0:T(128)S(1)} %pad_add_fusion.pos, f32[1,256]{1,0:T(1,128)S(1)} %bitcast.7, f32[8,16,256]{2,1,0:T(8,128)S(1)} %get-tuple-element.25.own, bf16[8,16,256]{2,1,0:T(8,128)(2,1)S(1)} %collective-permute-done.11.refs_0_, bf16[8,16,256]{2,1,0:T(8,128)(2,1)S(1)} %collective-permute-done.12.refs_1_, ...), custom_call_target="tpu_custom_call" | custom-call | tf_op jit(solution)/shard_map/pallas_call | solution.py:147
  (2 shorter events, 0.0 us)
Async XLA Ops:
  0.0 14.2 %copy-start.2 = (f32[256]{0:T(256)S(1)}, f32[256]{0:T(256)}, u32[]{:S(2)}) copy-start(f32[256]{0:T(256)} %param.7) | copy-start | bytes 3076
  0.0 14.3 %copy-start.3 = (f32[256]{0:T(256)S(1)}, f32[256]{0:T(256)}, u32[]{:S(2)}) copy-start(f32[256]{0:T(256)} %param.8) | copy-start | bytes 3076
  0.1 0.9 %copy-start = (bf16[2,8,16,256]{3,2,1,0:T(8,128)(2,1)S(1)}, bf16[2,8,16,256]{3,2,1,0:T(8,128)(2,1)}, u32[]{:S(2)}) copy-start(bf16[2,8,16,256]{3,2,1,0:T(8,128)(2,1)} %latent.1) | copy-start | bytes 393220
  1.9 12.5 %collective-permute-start = (bf16[8,16,128]{2,1,0:T(8,128)(2,1)S(1)}, bf16[8,16,128]{2,1,0:T(8,128)(2,1)S(1)}, u32[]{:S(2)}, u32[]{:S(2)}) collective-permute-start(bf16[8,16,128]{2,1,0:T(8,128)(2,1)S(1)} %get-tuple-element.20), channel_id=1, source_target_pairs={{0,4},{2,6},{4,0},{6,2},{8,12},{10,14},{12,8},{14,10},{1,5},{3,7},... | collective-permute-start | bytes 98312 | tf_op jit(solution)/shard_map/ppermute | solution.py:320
  4.9 14.9 %collective-permute-start.4 = (bf16[8,16,128]{2,1,0:T(8,128)(2,1)S(1)}, bf16[8,16,128]{2,1,0:T(8,128)(2,1)S(1)}, u32[]{:S(2)}, u32[]{:S(2)}) collective-permute-start(bf16[8,16,128]{2,1,0:T(8,128)(2,1)S(1)} %get-tuple-element.20), channel_id=1, source_target_pairs={{0,6},{2,4},{4,2},{6,0},{8,14},{10,12},{12,10},{14,8},{1,7},{3,5},... | collective-permute-start | bytes 98312 | tf_op jit(solution)/shard_map/ppermute | solution.py:320
  6.3 9.2 %collective-permute-start.1 = (bf16[8,16,128]{2,1,0:T(8,128)(2,1)S(1)}, bf16[8,16,128]{2,1,0:T(8,128)(2,1)S(1)}, u32[]{:S(2)}, u32[]{:S(2)}) collective-permute-start(bf16[8,16,128]{2,1,0:T(8,128)(2,1)S(1)} %get-tuple-element.21), channel_id=1, source_target_pairs={{0,8},{2,10},{4,12},{6,14},{8,0},{10,2},{12,4},{14,6},{1,9},{3,11}... | collective-permute-start | bytes 98312 | tf_op jit(solution)/shard_map/ppermute | solution.py:320
  8.9 11.3 %collective-permute-start.5 = (bf16[8,16,128]{2,1,0:T(8,128)(2,1)S(1)}, bf16[8,16,128]{2,1,0:T(8,128)(2,1)S(1)}, u32[]{:S(2)}, u32[]{:S(2)}) collective-permute-start(bf16[8,16,128]{2,1,0:T(8,128)(2,1)S(1)} %get-tuple-element.21), channel_id=1, source_target_pairs={{0,10},{2,8},{4,14},{6,12},{8,2},{10,0},{12,6},{14,4},{1,11},{3,9}... | collective-permute-start | bytes 98312 | tf_op jit(solution)/shard_map/ppermute | solution.py:320
  8.9 7.1 %collective-permute-start.2 = (bf16[8,16,128]{2,1,0:T(8,128)(2,1)S(1)}, bf16[8,16,128]{2,1,0:T(8,128)(2,1)S(1)}, u32[]{:S(2)}, u32[]{:S(2)}) collective-permute-start(bf16[8,16,128]{2,1,0:T(8,128)(2,1)S(1)} %get-tuple-element.22), channel_id=1, source_target_pairs={{0,12},{2,14},{4,8},{6,10},{8,4},{10,6},{12,0},{14,2},{1,13},{3,15... | collective-permute-start | bytes 98312 | tf_op jit(solution)/shard_map/ppermute | solution.py:320
  12.8 9.9 %copy-start.4 = (s32[4]{0:T(128)S(1)}, s32[4]{0:T(128)}, u32[]{:S(2)}) copy-start(s32[4]{0:T(128)} %param.11) | copy-start | bytes 52
  14.3 6.7 %collective-permute-start.6 = (bf16[8,16,128]{2,1,0:T(8,128)(2,1)S(1)}, bf16[8,16,128]{2,1,0:T(8,128)(2,1)S(1)}, u32[]{:S(2)}, u32[]{:S(2)}) collective-permute-start(bf16[8,16,128]{2,1,0:T(8,128)(2,1)S(1)} %get-tuple-element.22), channel_id=1, source_target_pairs={{0,14},{2,12},{4,10},{6,8},{8,6},{10,4},{12,2},{14,0},{1,15},{3,13... | collective-permute-start | bytes 98312 | tf_op jit(solution)/shard_map/ppermute | solution.py:320
  15.5 4.3 %collective-permute-start.3 = (bf16[8,16,128]{2,1,0:T(8,128)(2,1)S(1)}, bf16[8,16,128]{2,1,0:T(8,128)(2,1)S(1)}, u32[]{:S(2)}, u32[]{:S(2)}) collective-permute-start(bf16[8,16,128]{2,1,0:T(8,128)(2,1)S(1)} %get-tuple-element.19.refs_0_), channel_id=1, source_target_pairs={{0,2},{2,0},{4,6},{6,4},{8,10},{10,8},{12,14},{14,12},{1,3},{3,1},... | collective-permute-start | bytes 98312 | tf_op jit(solution)/shard_map/ppermute | solution.py:320
  16.0 8.0 %collective-permute-start.10 = (bf16[3,3,3,32,128]{4,3,2,1,0:T(8,128)(2,1)S(1)}, bf16[3,3,3,32,128]{4,3,2,1,0:T(8,128)(2,1)S(1)}, u32[]{:S(2)}, u32[]{:S(2)}) collective-permute-start(bf16[3,3,3,32,128]{4,3,2,1,0:T(8,128)(2,1)S(1)} %get-tuple-element.33), channel_id=1, source_target_pairs={{0,3},{1,2},{2,1},{3,0},{4,7},{5,6},{6,5},{7,4},{8,11},{9,10},{10,... | collective-permute-start | bytes 663560 | tf_op jit(solution)/shard_map/ppermute | solution.py:325
  19.8 4.2 %collective-permute-start.8 = (bf16[3,3,3,32,128]{4,3,2,1,0:T(8,128)(2,1)S(1)}, bf16[3,3,3,32,128]{4,3,2,1,0:T(8,128)(2,1)S(1)}, u32[]{:S(2)}, u32[]{:S(2)}) collective-permute-start(bf16[3,3,3,32,128]{4,3,2,1,0:T(8,128)(2,1)S(1)} %get-tuple-element.34), channel_id=1, source_target_pairs={{0,1},{1,0},{2,3},{3,2},{4,5},{5,4},{6,7},{7,6},{8,9},{9,8},{10,11... | collective-permute-start | bytes 663560 | tf_op jit(solution)/shard_map/ppermute | solution.py:325
  19.8 9.4 %collective-permute-start.9 = (bf16[3,3,3,32,128]{4,3,2,1,0:T(8,128)(2,1)S(1)}, bf16[3,3,3,32,128]{4,3,2,1,0:T(8,128)(2,1)S(1)}, u32[]{:S(2)}, u32[]{:S(2)}) collective-permute-start(bf16[3,3,3,32,128]{4,3,2,1,0:T(8,128)(2,1)S(1)} %get-tuple-element.36), channel_id=1, source_target_pairs={{0,2},{2,0},{4,6},{6,4},{8,10},{10,8},{12,14},{14,12},{1,3},{3,1},... | collective-permute-start | bytes 663560 | tf_op jit(solution)/shard_map/ppermute | solution.py:320
  22.6 7.5 %collective-permute-start.7 = (bf16[2,8,96,128]{3,2,1,0:T(8,128)(2,1)S(1)}, bf16[2,8,96,128]{3,2,1,0:T(8,128)(2,1)S(1)}, u32[]{:S(2)}, u32[]{:S(2)}) collective-permute-start(bf16[2,8,96,128]{3,2,1,0:T(8,128)(2,1)S(1)} %shard_map.65.mine), channel_id=1, source_target_pairs={{0,1},{1,0},{2,3},{3,2},{4,5},{5,4},{6,7},{7,6},{8,9},{9,8},{10,11... | collective-permute-start | bytes 1179656 | tf_op jit(solution)/shard_map/ppermute | solution.py:359
  30.1 20.0 %copy-start.1 = (f32[256]{0:T(256)S(1)}, f32[256]{0:T(256)}, u32[]{:S(2)}) copy-start(f32[256]{0:T(256)} %param.10) | copy-start | bytes 3076
  33.9 6.0 %collective-permute-start.11 = (bf16[8,16,256]{2,1,0:T(8,128)(2,1)S(1)}, bf16[8,16,256]{2,1,0:T(8,128)(2,1)S(1)}, u32[]{:S(2)}, u32[]{:S(2)}) collective-permute-start(bf16[8,16,256]{2,1,0:T(8,128)(2,1)S(1)} %get-tuple-element.26), channel_id=1, source_target_pairs={{0,4},{2,6},{4,0},{6,2},{8,12},{10,14},{12,8},{14,10},{1,5},{3,7},... | collective-permute-start | bytes 196616 | tf_op jit(solution)/shard_map/ppermute | solution.py:320
  34.0 9.2 %collective-permute-start.12 = (bf16[8,16,256]{2,1,0:T(8,128)(2,1)S(1)}, bf16[8,16,256]{2,1,0:T(8,128)(2,1)S(1)}, u32[]{:S(2)}, u32[]{:S(2)}) collective-permute-start(bf16[8,16,256]{2,1,0:T(8,128)(2,1)S(1)} %get-tuple-element.27), channel_id=1, source_target_pairs={{0,8},{2,10},{4,12},{6,14},{8,0},{10,2},{12,4},{14,6},{1,9},{3,11}... | collective-permute-start | bytes 196616 | tf_op jit(solution)/shard_map/ppermute | solution.py:320
  37.8 7.5 %collective-permute-start.13 = (bf16[8,16,256]{2,1,0:T(8,128)(2,1)S(1)}, bf16[8,16,256]{2,1,0:T(8,128)(2,1)S(1)}, u32[]{:S(2)}, u32[]{:S(2)}) collective-permute-start(bf16[8,16,256]{2,1,0:T(8,128)(2,1)S(1)} %get-tuple-element.28), channel_id=1, source_target_pairs={{0,12},{2,14},{4,8},{6,10},{8,4},{10,6},{12,0},{14,2},{1,13},{3,15... | collective-permute-start | bytes 196616 | tf_op jit(solution)/shard_map/ppermute | solution.py:320
  38.4 7.0 %collective-permute-start.14 = (bf16[8,16,256]{2,1,0:T(8,128)(2,1)S(1)}, bf16[8,16,256]{2,1,0:T(8,128)(2,1)S(1)}, u32[]{:S(2)}, u32[]{:S(2)}) collective-permute-start(bf16[8,16,256]{2,1,0:T(8,128)(2,1)S(1)} %get-tuple-element.29), channel_id=1, source_target_pairs={{0,2},{2,0},{4,6},{6,4},{8,10},{10,8},{12,14},{14,12},{1,3},{3,1},... | collective-permute-start | bytes 196616 | tf_op jit(solution)/shard_map/ppermute | solution.py:320
  38.7 6.6 %collective-permute-start.15 = (bf16[8,16,256]{2,1,0:T(8,128)(2,1)S(1)}, bf16[8,16,256]{2,1,0:T(8,128)(2,1)S(1)}, u32[]{:S(2)}, u32[]{:S(2)}) collective-permute-start(bf16[8,16,256]{2,1,0:T(8,128)(2,1)S(1)} %get-tuple-element.30), channel_id=1, source_target_pairs={{0,6},{2,4},{4,2},{6,0},{8,14},{10,12},{12,10},{14,8},{1,7},{3,5},... | collective-permute-start | bytes 196616 | tf_op jit(solution)/shard_map/ppermute | solution.py:320
  39.9 6.8 %collective-permute-start.16 = (bf16[8,16,256]{2,1,0:T(8,128)(2,1)S(1)}, bf16[8,16,256]{2,1,0:T(8,128)(2,1)S(1)}, u32[]{:S(2)}, u32[]{:S(2)}) collective-permute-start(bf16[8,16,256]{2,1,0:T(8,128)(2,1)S(1)} %get-tuple-element.31), channel_id=1, source_target_pairs={{0,10},{2,8},{4,14},{6,12},{8,2},{10,0},{12,6},{14,4},{1,11},{3,9}... | collective-permute-start | bytes 196616 | tf_op jit(solution)/shard_map/ppermute | solution.py:320
  43.1 7.0 %collective-permute-start.17 = (bf16[8,16,256]{2,1,0:T(8,128)(2,1)S(1)}, bf16[8,16,256]{2,1,0:T(8,128)(2,1)S(1)}, u32[]{:S(2)}, u32[]{:S(2)}) collective-permute-start(bf16[8,16,256]{2,1,0:T(8,128)(2,1)S(1)} %get-tuple-element.32), channel_id=1, source_target_pairs={{0,14},{2,12},{4,10},{6,8},{8,6},{10,4},{12,2},{14,0},{1,15},{3,13... | collective-permute-start | bytes 196616 | tf_op jit(solution)/shard_map/ppermute | solution.py:320

commit v2 on v1

--- a/solution.py
+++ b/solution.py
@@ -151,6 +151,7 @@
             out_specs=jax.tree.map(lambda _: vmem, outs),
             scratch_shapes=list(scratch),
             compiler_params=pltpu.CompilerParams(vmem_limit_bytes=VMEM_BYTES),
+            cost_estimate=pl.CostEstimate(flops=1000, bytes_accessed=1000, transcendentals=0),
         )(*args)
 
     return run
@@ -250,7 +251,7 @@
 
 
 def conv_body(pos, mine, sibling, diag, lower, blend, *refs):
-    own, sends, (stacked, summed, blocks) = refs[0], refs[1:8], refs[8:]
+    own, sends, kept, passed, (stacked, summed, blocks) = refs[0], refs[1:4], refs[4], refs[5], refs[6:]
     z, x = pos[0], pos[1]
     col = lax.broadcasted_iota(jnp.int32, (24, 128), 0)
     for p in range(2):
@@ -292,19 +293,23 @@
     own[...] = blocks[x, z]
     for k in range(1, 4):
         sends[k - 1][...] = blocks[x, z ^ k].astype(jnp.bfloat16)
-    for k in range(4):
-        sends[3 + k][...] = blocks[1 - x, z ^ k].astype(jnp.bfloat16)
+    for i, k in enumerate((0, 2)):
+        kept[i] = blocks[1 - x, z ^ k]
+        passed[i] = blocks[1 - x, z ^ k ^ 1].astype(jnp.bfloat16)
+
+
+def add_body(pos, kept, came, *sums):
+    for i in range(2):
+        sums[i][...] = (kept[i] + came[i].astype(jnp.float32)).astype(jnp.bfloat16)
 
 
 def join_body(pos, bias, own, *refs):
-    same, far, out = refs[:3], refs[3:7], refs[7]
+    same, far, out = refs[:3], refs[3:5], refs[5]
     x = pos[1]
     near_sum = own[...]
     for part in same:
         near_sum = near_sum + part[...].astype(jnp.float32)
-    far_sum = far[0][...].astype(jnp.float32)
-    for part in far[1:]:
-        far_sum = far_sum + part[...].astype(jnp.float32)
+    far_sum = far[0][...].astype(jnp.float32) + far[1][...].astype(jnp.float32)
     low = jnp.where(x == 0, near_sum, far_sum)
     high = jnp.where(x == 0, far_sum, near_sum)
     for f in range(2):
@@ -332,18 +337,20 @@
     block = jax.ShapeDtypeStruct((8, 16, 128), bf16)
     wide = jax.ShapeDtypeStruct((8, 16, 256), bf16)
 
-    packed = call(pack_body, [block] * 4)(pos, latent)
-    near = [packed[0]] + [exchanged(packed[k], k, 0) for k in (1, 2, 3)]
-    far = [exchanged(packed[k], k, 1) for k in range(4)]
-
     def quarter(core, frame_block):
         start = core * 256 + frame_block * 128
         return lax.dynamic_slice_in_dim(kernel, start, 128, axis=4)
 
-    same = quarter(c, x)
-    other = across(quarter(1 - c, x), 0)
-    same_far = exchanged(quarter(c, 1 - x), 0, 1)
-    other_far = across(quarter(1 - c, 1 - x), 1)
+    quarters = (quarter(c, x), quarter(1 - c, x), quarter(c, 1 - x), quarter(1 - c, 1 - x))
+    latent, quarters = lax.optimization_barrier((latent, quarters))
+    same = quarters[0]
+    other = across(quarters[1], 0)
+    same_far = exchanged(quarters[2], 0, 1)
+    other_far = across(quarters[3], 1)
+    packed = call(pack_body, [block] * 4)(pos, latent)
+    near = [packed[0]] + [exchanged(packed[k], k, 0) for k in (1, 2, 3)]
+    same_far, near[2] = lax.optimization_barrier((same_far, near[2]))
+    far = [exchanged(part, 0, 1) for part in near]
     matrix = jax.ShapeDtypeStruct((TAPS, 768, 256), bf16)
     diag, lower = call(weights_body, [matrix] * 2)(pos, same, other, same_far, other_far)
 
@@ -361,17 +368,22 @@
     offsets = jnp.arange(2 * RIM, dtype=jnp.int32)
     ramps = ramp_weight(blend_profile[:3, None], offsets[None, :], RIM)
     blend = jnp.broadcast_to(ramps[:, :, None], (3, 2 * RIM, 256))
-    own, *sends = call(
+    own, *sends, kept, leaving = call(
         conv_body,
-        [jax.ShapeDtypeStruct((8, 16, 256), f32)] + [wide] * 7,
+        [jax.ShapeDtypeStruct((8, 16, 256), f32)]
+        + [wide] * 3
+        + [jax.ShapeDtypeStruct((2, 8, 16, 256), t) for t in (f32, bf16)],
         [
             pltpu.VMEM((2, 960, 768), bf16),
             pltpu.VMEM((8, 72, 256), f32),
             pltpu.VMEM((2, 4, 8, 16, 256), f32),
         ],
     )(pos, acts, sibling, diag, lower, blend)
-    near_sums = [exchanged(sends[k - 1], k, 0) for k in (1, 2, 3)]
-    far_sums = [exchanged(sends[3 + k], k, 1) for k in range(4)]
+    came = exchanged(leaving, 1, 0)
+    came, sends[0] = lax.optimization_barrier((came, sends[0]))
+    sums = call(add_body, [wide] * 2)(pos, kept, came)
+    far_sums = [exchanged(sums[1], 2, 1), exchanged(sums[0], 0, 1)]
+    near_sums = [exchanged(sends[k - 1], k, 0) for k in (2, 3, 1)]
     return call(join_body, jax.ShapeDtypeStruct(latent.shape, bf16))(
         pos, conv_bias[None], own, *near_sums, *far_sums
     )

time: 51.5 us -> 43.9 us (0.85)
  starting transfers between devices: 24.4 us -> 17.6 us
  local copies, waits for them, and re-layouts: 2.49 us -> 1.61 us
  Pallas kernels: 8.27 us -> 8.83 us
    ppermute x15 -> x14, starting transfers between devices: 24.3 us -> 17.5 us  [exchanged(): return lax.ppermute(block, ('tile', 'tm'), route)]
    ppermute x2, waiting for transfers between devices: 1.25 us -> 0.01 us  [across(): return lax.ppermute(block, ('tm', 'ch'), route)]
    unnamed x10, local copies, waits for them, and re-layouts: 0.92 us -> 0.02 us
    ppermute x1, waiting for transfers between devices: 0.01 us -> 0.71 us  [resident_plan(): sibling = lax.ppermute(acts, 'ch', [(0, 1), (1, 0)])]
    pallas_call x5 -> x6, Pallas kernels: 8.27 us -> 8.83 us  [run(): pl.pallas_call(body, out_shape=outs, in_specs=specs, out_specs=jax.tree.m...]
    ppermute x15 -> x14, waiting for transfers between devices: 14.6 us -> 14.6 us  [exchanged(): return lax.ppermute(block, ('tile', 'tm'), route)]
  transfers between devices with their start and end apart: 18 -> 17, of which waited for: 6 -> 8; matrix products, arithmetic and copies ran while one was open for 3% -> 1% of each run, Pallas kernels for 5% -> 9%
where the time goes in v2:
time: 43.9 us; the launch traced here: 43.8 us
  starting transfers between devices  17.6 us (40%)
  waiting for transfers between devices  15.3 us (35%)
  Pallas kernels  8.83 us (20%)
  local copies, waits for them, and re-layouts  1.61 us (4%)
    ppermute x14, starting transfers between devices, exchanged(): return lax.ppermute(block, ('tile', 'tm'), route)  17.5 us
    ppermute x14, waiting for transfers between devices, exchanged(): return lax.ppermute(block, ('tile', 'tm'), route)  14.6 us
    pallas_call x6, Pallas kernels, run(): pl.pallas_call(body, out_shape=outs, in_specs=specs, out_specs=jax.tree.m...  8.83 us
    dynamic_slice x1, local copies, waits for them, and re-layouts, quarter(): return lax.dynamic_slice_in_dim(kernel, start, 128, axis=4)  1.37 us
  transfers between devices with their start and end apart: 17, of which 8 were waited for; matrix products, arithmetic and copies ran while one was open for 1% of the time, Pallas kernels for 9%

profile of v2, /device:TPU:0, one launch (start us, length us, event | category | flops | bytes accessed | tf_op | source)
XLA Modules:
  0.0 43.8 jit_solution(3701356604381291513)
XLA Ops:
  0.0 0.0 copy-start
  0.0 0.0 copy-start.2
  0.0 0.0 copy-start.3
  0.0 0.0 copy-start.4
  0.0 1.4 %constant_dynamic-slice_fusion = (bf16[3,3,3,32,128]{4,3,2,1,0:T(8,128)(2,1)S(1)}, bf16[3,3,3,32,128]{4,3,2,1,0:T(8,128)(2,1)S(1)}, bf16[3,3,3,32,128]{4,3,2,1,0:T(8,128)(2,1)S(1)}, bf16[3,3,3,32,128]{4,3,2,1,0:T(8,128)(2,1)S(1)}) fusion(bf16[3,3,3,32,512]{4,3,2,1,0:T(8,128)(2,1)} %param.9, s32[]{:T(128)S(6)} %select_n.20, s32[]{:T(128)S(6)} %select_n.18, ...), kind=kLoop, calls=%fused_computation.1 | loop fusion | bytes 1769488 | tf_op jit(solution)/shard_map/dynamic_slice | solution.py:342
  1.4 3.1 %collective-permute-start.1 = (bf16[3,3,3,32,128]{4,3,2,1,0:T(8,128)(2,1)S(1)}, bf16[3,3,3,32,128]{4,3,2,1,0:T(8,128)(2,1)S(1)}, u32[]{:S(2)}, u32[]{:S(2)}) collective-permute-start(bf16[3,3,3,32,128]{4,3,2,1,0:T(8,128)(2,1)S(1)} %get-tuple-element.31), channel_id=1, source_target_pairs={{0,2},{2,0},{4,6},{6,4},{8,10},{10,8},{12,14},{14,12},{1,3},{3,1},... | collective-permute-start | bytes 663560 | tf_op jit(solution)/shard_map/ppermute | solution.py:325
  4.5 0.1 pad_add_fusion.pos
  4.5 0.0 copy-done
  4.5 0.9 %shard_map.64 = (bf16[8,16,128]{2,1,0:T(8,128)(2,1)S(1)}, bf16[8,16,128]{2,1,0:T(8,128)(2,1)S(1)}, bf16[8,16,128]{2,1,0:T(8,128)(2,1)S(1)}, bf16[8,16,128]{2,1,0:T(8,128)(2,1)S(1)}) custom-call(s32[2]{0:T(128)S(1)} %pad_add_fusion.pos, bf16[2,8,16,256]{3,2,1,0:T(8,128)(2,1)S(1)} %copy-done), custom_call_target="tpu_custom_call" | custom-call | flops 1000 | bytes 1000 | tf_op jit(solution)/shard_map/pallas_call | solution.py:147
  5.4 2.6 %collective-permute-start.2 = (bf16[8,16,128]{2,1,0:T(8,128)(2,1)S(1)}, bf16[8,16,128]{2,1,0:T(8,128)(2,1)S(1)}, u32[]{:S(2)}, u32[]{:S(2)}) collective-permute-start(bf16[8,16,128]{2,1,0:T(8,128)(2,1)S(1)} %get-tuple-element.32), channel_id=1, source_target_pairs={{0,8},{2,10},{4,12},{6,14},{8,0},{10,2},{12,4},{14,6},{1,9},{3,11}... | collective-permute-start | bytes 98312 | tf_op jit(solution)/shard_map/ppermute | solution.py:325
  8.0 0.0 collective-permute-start.10
  8.1 1.6 %collective-permute-start = (bf16[8,16,128]{2,1,0:T(8,128)(2,1)S(1)}, bf16[8,16,128]{2,1,0:T(8,128)(2,1)S(1)}, u32[]{:S(2)}, u32[]{:S(2)}) collective-permute-start(bf16[8,16,128]{2,1,0:T(8,128)(2,1)S(1)} %get-tuple-element.30), channel_id=1, source_target_pairs={{0,4},{2,6},{4,0},{6,2},{8,12},{10,14},{12,8},{14,10},{1,5},{3,7},... | collective-permute-start | bytes 98312 | tf_op jit(solution)/shard_map/ppermute | solution.py:325
  9.6 0.3 collective-permute-start.3
  9.9 0.0 copy-done.2
  9.9 0.1 dynamic_slice.18
  10.0 0.0 copy-done.3
  10.0 0.1 dynamic_slice.19
  10.0 0.2 collective-permute-done.2.refs_2_
  10.3 0.7 %collective-permute-start.4 = (bf16[8,16,128]{2,1,0:T(8,128)(2,1)S(1)}, bf16[8,16,128]{2,1,0:T(8,128)(2,1)S(1)}, u32[]{:S(2)}, u32[]{:S(2)}) collective-permute-start(bf16[8,16,128]{2,1,0:T(8,128)(2,1)S(1)} %get-tuple-element.29.refs_0_), channel_id=1, source_target_pairs={{0,2},{2,0},{4,6},{6,4},{8,10},{10,8},{12,14},{14,12},{1,3},{3,1},... | collective-permute-start | bytes 98312 | tf_op jit(solution)/shard_map/ppermute | solution.py:325
  10.9 1.0 %collective-permute-done.refs_1_ = bf16[8,16,128]{2,1,0:T(8,128)(2,1)S(1)} collective-permute-done((bf16[8,16,128]{2,1,0:T(8,128)(2,1)S(1)}, bf16[8,16,128]{2,1,0:T(8,128)(2,1)S(1)}, u32[]{:S(2)}, u32[]{:S(2)}) %collective-permute-start) | collective-permute-done | bytes 32800 | tf_op jit(solution)/shard_map/ppermute | solution.py:325
  12.0 1.0 %collective-permute-start.5 = (bf16[8,16,128]{2,1,0:T(8,128)(2,1)S(1)}, bf16[8,16,128]{2,1,0:T(8,128)(2,1)S(1)}, u32[]{:S(2)}, u32[]{:S(2)}) collective-permute-start(bf16[8,16,128]{2,1,0:T(8,128)(2,1)S(1)} %collective-permute-done.refs_1_), channel_id=1, source_target_pairs={{0,2},{2,0},{4,6},{6,4},{8,10},{10,8},{12,14},{14,12},{1,3},{3,1},... | collective-permute-start | bytes 98312 | tf_op jit(solution)/shard_map/ppermute | solution.py:325
  13.0 2.4 %collective-permute-done.3.refs_3_ = bf16[8,16,128]{2,1,0:T(8,128)(2,1)S(1)} collective-permute-done((bf16[8,16,128]{2,1,0:T(8,128)(2,1)S(1)}, bf16[8,16,128]{2,1,0:T(8,128)(2,1)S(1)}, u32[]{:S(2)}, u32[]{:S(2)}) %collective-permute-start.3) | collective-permute-done | bytes 32800 | tf_op jit(solution)/shard_map/ppermute | solution.py:325
  15.3 1.2 %collective-permute-start.7 = (bf16[8,16,128]{2,1,0:T(8,128)(2,1)S(1)}, bf16[8,16,128]{2,1,0:T(8,128)(2,1)S(1)}, u32[]{:S(2)}, u32[]{:S(2)}) collective-permute-start(bf16[8,16,128]{2,1,0:T(8,128)(2,1)S(1)} %collective-permute-done.3.refs_3_), channel_id=1, source_target_pairs={{0,2},{2,0},{4,6},{6,4},{8,10},{10,8},{12,14},{14,12},{1,3},{3,1},... | collective-permute-start | bytes 98312 | tf_op jit(solution)/shard_map/ppermute | solution.py:325
  16.6 0.0 collective-permute-done.1.same_far
  16.6 0.8 %collective-permute-start.6 = (bf16[8,16,128]{2,1,0:T(8,128)(2,1)S(1)}, bf16[8,16,128]{2,1,0:T(8,128)(2,1)S(1)}, u32[]{:S(2)}, u32[]{:S(2)}) collective-permute-start(bf16[8,16,128]{2,1,0:T(8,128)(2,1)S(1)} %collective-permute-done.2.refs_2_), channel_id=1, source_target_pairs={{0,2},{2,0},{4,6},{6,4},{8,10},{10,8},{12,14},{14,12},{1,3},{3,1},... | collective-permute-start | bytes 98312 | tf_op jit(solution)/shard_map/ppermute | solution.py:325
  17.4 0.1 maximum_bitcast_fusion
  17.5 0.0 collective-permute-done.4.refs_4_
  17.5 0.0 collective-permute-start.9
  17.5 0.0 collective-permute-done.5.refs_5_
  17.5 2.0 %collective-permute-done.7.refs_7_ = bf16[8,16,128]{2,1,0:T(8,128)(2,1)S(1)} collective-permute-done((bf16[8,16,128]{2,1,0:T(8,128)(2,1)S(1)}, bf16[8,16,128]{2,1,0:T(8,128)(2,1)S(1)}, u32[]{:S(2)}, u32[]{:S(2)}) %collective-permute-start.7) | collective-permute-done | bytes 32800 | tf_op jit(solution)/shard_map/ppermute | solution.py:325
  19.5 1.0 %collective-permute-done.6.refs_6_ = bf16[8,16,128]{2,1,0:T(8,128)(2,1)S(1)} collective-permute-done((bf16[8,16,128]{2,1,0:T(8,128)(2,1)S(1)}, bf16[8,16,128]{2,1,0:T(8,128)(2,1)S(1)}, u32[]{:S(2)}, u32[]{:S(2)}) %collective-permute-start.6) | collective-permute-done | bytes 32800 | tf_op jit(solution)/shard_map/ppermute | solution.py:325
  20.5 1.5 %shard_map.65.mine = bf16[2,8,96,128]{3,2,1,0:T(8,128)(2,1)S(1)} custom-call(s32[2]{0:T(128)S(1)} %pad_add_fusion.pos, f32[1,128]{1,0:T(1,128)S(1)} %get-tuple-element.55.gain, f32[1,128]{1,0:T(1,128)S(1)} %get-tuple-element.56.shift, bf16[8,16,128]{2,1,0:T(8,128)(2,1)S(1)} %get-tuple-element.29.refs_0_, ...), custom_call_target="tpu_custom_call" | custom-call | flops 1000 | bytes 1000 | tf_op jit(solution)/shard_map/pallas_call | solution.py:147
  22.0 0.1 collective-permute-start.8
  22.1 0.0 copy-done.4
  22.1 0.1 add_divide_fusion
  22.2 0.0 collective-permute-done.10.other_far
  22.2 0.0 collective-permute-done.9.other
  22.2 0.9 %shard_map.66 = (bf16[3,768,256]{2,1,0:T(8,128)(2,1)S(1)}, bf16[3,768,256]{2,1,0:T(8,128)(2,1)S(1)}) custom-call(s32[2]{0:T(128)S(1)} %pad_add_fusion.pos, bf16[3,3,3,32,128]{4,3,2,1,0:T(8,128)(2,1)S(1)} %get-tuple-element.35.same, bf16[3,3,3,32,128]{4,3,2,1,0:T(8,128)(2,1)S(1)} %collective-permute-done.9.other, ...), custom_call_target="tpu_custom_call" | custom-call | flops 1000 | bytes 1000 | tf_op jit(solution)/shard_map/pallas_call | solution.py:147
  23.1 0.7 %collective-permute-done.8.sibling = bf16[2,8,96,128]{3,2,1,0:T(8,128)(2,1)S(1)} collective-permute-done((bf16[2,8,96,128]{3,2,1,0:T(8,128)(2,1)S(1)}, bf16[2,8,96,128]{3,2,1,0:T(8,128)(2,1)S(1)}, u32[]{:S(2)}, u32[]{:S(2)}) %collective-permute-start.8) | collective-permute-done | bytes 393248 | tf_op jit(solution)/shard_map/ppermute | solution.py:366
  23.8 0.1 broadcast_in_dim.20.blend
  23.9 0.0 copy-start.1
  23.9 3.8 %shard_map.67 = (f32[8,16,256]{2,1,0:T(8,128)S(1)}, bf16[8,16,256]{2,1,0:T(8,128)(2,1)S(1)}, bf16[8,16,256]{2,1,0:T(8,128)(2,1)S(1)}, bf16[8,16,256]{2,1,0:T(8,1...) custom-call(s32[2]{0:T(128)S(1)} %pad_add_fusion.pos, ...), custom_call_target="tpu_custom_call" | custom-call | flops 1000 | bytes 1000 | tf_op jit(solution)/shard_map/pallas_call | solution.py:147
  27.6 0.1 collective-permute-start.13
  27.7 1.3 %collective-permute-start.11 = (bf16[8,16,256]{2,1,0:T(8,128)(2,1)S(1)}, bf16[8,16,256]{2,1,0:T(8,128)(2,1)S(1)}, u32[]{:S(2)}, u32[]{:S(2)}) collective-permute-start(bf16[8,16,256]{2,1,0:T(8,128)(2,1)S(1)} %get-tuple-element.42), channel_id=1, source_target_pairs={{0,8},{2,10},{4,12},{6,14},{8,0},{10,2},{12,4},{14,6},{1,9},{3,11}... | collective-permute-start | bytes 196616 | tf_op jit(solution)/shard_map/ppermute | solution.py:325
  29.1 3.0 %collective-permute-start.12 = (bf16[8,16,256]{2,1,0:T(8,128)(2,1)S(1)}, bf16[8,16,256]{2,1,0:T(8,128)(2,1)S(1)}, u32[]{:S(2)}, u32[]{:S(2)}) collective-permute-start(bf16[8,16,256]{2,1,0:T(8,128)(2,1)S(1)} %get-tuple-element.43), channel_id=1, source_target_pairs={{0,12},{2,14},{4,8},{6,10},{8,4},{10,6},{12,0},{14,2},{1,13},{3,15... | collective-permute-start | bytes 196616 | tf_op jit(solution)/shard_map/ppermute | solution.py:325
  32.1 3.6 %collective-permute-done.13.came = bf16[2,8,16,256]{3,2,1,0:T(8,128)(2,1)S(1)} collective-permute-done((bf16[2,8,16,256]{3,2,1,0:T(8,128)(2,1)S(1)}, bf16[2,8,16,256]{3,2,1,0:T(8,128)(2,1)S(1)}, u32[]{:S(2)}, u32[]{:S(2)}) %collective-permute-start.13) | collective-permute-done | bytes 131104 | tf_op jit(solution)/shard_map/ppermute | solution.py:325
  35.7 0.6 %shard_map.68 = (bf16[8,16,256]{2,1,0:T(8,128)(2,1)S(1)}, bf16[8,16,256]{2,1,0:T(8,128)(2,1)S(1)}) custom-call(s32[2]{0:T(128)S(1)} %pad_add_fusion.pos, f32[2,8,16,256]{3,2,1,0:T(8,128)S(1)} %get-tuple-element.47.kept, bf16[2,8,16,256]{3,2,1,0:T(8,128)(2,1)S(1)} %collective-permute-done.13.came), custom_call_target="tpu_custom_call" | custom-call | flops 1000 | bytes 1000 | tf_op jit(solution)/shard_map/pallas_call | solution.py:147
  36.2 0.1 collective-permute-start.15
  36.3 0.1 collective-permute-start.16
  36.4 1.7 %collective-permute-start.14 = (bf16[8,16,256]{2,1,0:T(8,128)(2,1)S(1)}, bf16[8,16,256]{2,1,0:T(8,128)(2,1)S(1)}, u32[]{:S(2)}, u32[]{:S(2)}) collective-permute-start(bf16[8,16,256]{2,1,0:T(8,128)(2,1)S(1)} %get-tuple-element.46), channel_id=1, source_target_pairs={{0,4},{2,6},{4,0},{6,2},{8,12},{10,14},{12,8},{14,10},{1,5},{3,7},... | collective-permute-start | bytes 196616 | tf_op jit(solution)/shard_map/ppermute | solution.py:325
  38.1 0.0 collective-permute-done.11.refs_0_
  38.1 0.0 collective-permute-done.12.refs_1_
  38.1 4.4 %collective-permute-done.15.refs_3_ = bf16[8,16,256]{2,1,0:T(8,128)(2,1)S(1)} collective-permute-done((bf16[8,16,256]{2,1,0:T(8,128)(2,1)S(1)}, bf16[8,16,256]{2,1,0:T(8,128)(2,1)S(1)}, u32[]{:S(2)}, u32[]{:S(2)}) %collective-permute-start.15) | collective-permute-done | bytes 65568 | tf_op jit(solution)/shard_map/ppermute | solution.py:325
  42.5 0.0 collective-permute-done.16.refs_4_
  42.5 0.0 collective-permute-done.14.refs_2_
  42.5 0.0 copy-done.1
  42.5 1.3 %shard_map.69 = bf16[2,8,16,256]{3,2,1,0:T(8,128)(2,1)} custom-call(s32[2]{0:T(128)S(1)} %pad_add_fusion.pos, f32[1,256]{1,0:T(1,128)S(1)} %bitcast.7, f32[8,16,256]{2,1,0:T(8,128)S(1)} %get-tuple-element.41.own, bf16[8,16,256]{2,1,0:T(8,128)(2,1)S(1)} %collective-permute-done.11.refs_0_, bf16[8,16,256]{2,1,0:T(8,128)(2,1)S(1)} %collective-permute-done.12.refs_1_, ...), custom_call_target="tpu_custom_call" | custom-call | flops 1000 | bytes 1000 | tf_op jit(solution)/shard_map/pallas_call | solution.py:147
  (2 shorter events, 0.0 us)
Async XLA Ops:
  0.0 4.5 %copy-start = (bf16[2,8,16,256]{3,2,1,0:T(8,128)(2,1)S(1)}, bf16[2,8,16,256]{3,2,1,0:T(8,128)(2,1)}, u32[]{:S(2)}) copy-start(bf16[2,8,16,256]{3,2,1,0:T(8,128)(2,1)} %latent) | copy-start | bytes 393220
  0.0 9.9 %copy-start.2 = (f32[256]{0:T(256)S(1)}, f32[256]{0:T(256)}, u32[]{:S(2)}) copy-start(f32[256]{0:T(256)} %param.7) | copy-start | bytes 3076
  0.0 10.0 %copy-start.3 = (f32[256]{0:T(256)S(1)}, f32[256]{0:T(256)}, u32[]{:S(2)}) copy-start(f32[256]{0:T(256)} %param.8) | copy-start | bytes 3076
  0.0 22.1 %copy-start.4 = (s32[4]{0:T(128)S(1)}, s32[4]{0:T(128)}, u32[]{:S(2)}) copy-start(s32[4]{0:T(128)} %param.11) | copy-start | bytes 52
  1.4 15.2 %collective-permute-start.1 = (bf16[3,3,3,32,128]{4,3,2,1,0:T(8,128)(2,1)S(1)}, bf16[3,3,3,32,128]{4,3,2,1,0:T(8,128)(2,1)S(1)}, u32[]{:S(2)}, u32[]{:S(2)}) collective-permute-start(bf16[3,3,3,32,128]{4,3,2,1,0:T(8,128)(2,1)S(1)} %get-tuple-element.31), channel_id=1, source_target_pairs={{0,2},{2,0},{4,6},{6,4},{8,10},{10,8},{12,14},{14,12},{1,3},{3,1},... | collective-permute-start | bytes 663560 | tf_op jit(solution)/shard_map/ppermute | solution.py:325
  5.4 4.9 %collective-permute-start.2 = (bf16[8,16,128]{2,1,0:T(8,128)(2,1)S(1)}, bf16[8,16,128]{2,1,0:T(8,128)(2,1)S(1)}, u32[]{:S(2)}, u32[]{:S(2)}) collective-permute-start(bf16[8,16,128]{2,1,0:T(8,128)(2,1)S(1)} %get-tuple-element.32), channel_id=1, source_target_pairs={{0,8},{2,10},{4,12},{6,14},{8,0},{10,2},{12,4},{14,6},{1,9},{3,11}... | collective-permute-start | bytes 98312 | tf_op jit(solution)/shard_map/ppermute | solution.py:325
  8.0 14.2 %collective-permute-start.10 = (bf16[3,3,3,32,128]{4,3,2,1,0:T(8,128)(2,1)S(1)}, bf16[3,3,3,32,128]{4,3,2,1,0:T(8,128)(2,1)S(1)}, u32[]{:S(2)}, u32[]{:S(2)}) collective-permute-start(bf16[3,3,3,32,128]{4,3,2,1,0:T(8,128)(2,1)S(1)} %get-tuple-element.38), channel_id=1, source_target_pairs={{0,3},{1,2},{2,1},{3,0},{4,7},{5,6},{6,5},{7,4},{8,11},{9,10},{10,... | collective-permute-start | bytes 663560 | tf_op jit(solution)/shard_map/ppermute | solution.py:330
  8.1 3.9 %collective-permute-start = (bf16[8,16,128]{2,1,0:T(8,128)(2,1)S(1)}, bf16[8,16,128]{2,1,0:T(8,128)(2,1)S(1)}, u32[]{:S(2)}, u32[]{:S(2)}) collective-permute-start(bf16[8,16,128]{2,1,0:T(8,128)(2,1)S(1)} %get-tuple-element.30), channel_id=1, source_target_pairs={{0,4},{2,6},{4,0},{6,2},{8,12},{10,14},{12,8},{14,10},{1,5},{3,7},... | collective-permute-start | bytes 98312 | tf_op jit(solution)/shard_map/ppermute | solution.py:325
  9.6 5.7 %collective-permute-start.3 = (bf16[8,16,128]{2,1,0:T(8,128)(2,1)S(1)}, bf16[8,16,128]{2,1,0:T(8,128)(2,1)S(1)}, u32[]{:S(2)}, u32[]{:S(2)}) collective-permute-start(bf16[8,16,128]{2,1,0:T(8,128)(2,1)S(1)} %get-tuple-element.34), channel_id=1, source_target_pairs={{0,12},{2,14},{4,8},{6,10},{8,4},{10,6},{12,0},{14,2},{1,13},{3,15... | collective-permute-start | bytes 98312 | tf_op jit(solution)/shard_map/ppermute | solution.py:325
  10.3 7.2 %collective-permute-start.4 = (bf16[8,16,128]{2,1,0:T(8,128)(2,1)S(1)}, bf16[8,16,128]{2,1,0:T(8,128)(2,1)S(1)}, u32[]{:S(2)}, u32[]{:S(2)}) collective-permute-start(bf16[8,16,128]{2,1,0:T(8,128)(2,1)S(1)} %get-tuple-element.29.refs_0_), channel_id=1, source_target_pairs={{0,2},{2,0},{4,6},{6,4},{8,10},{10,8},{12,14},{14,12},{1,3},{3,1},... | collective-permute-start | bytes 98312 | tf_op jit(solution)/shard_map/ppermute | solution.py:325
  12.0 5.5 %collective-permute-start.5 = (bf16[8,16,128]{2,1,0:T(8,128)(2,1)S(1)}, bf16[8,16,128]{2,1,0:T(8,128)(2,1)S(1)}, u32[]{:S(2)}, u32[]{:S(2)}) collective-permute-start(bf16[8,16,128]{2,1,0:T(8,128)(2,1)S(1)} %collective-permute-done.refs_1_), channel_id=1, source_target_pairs={{0,2},{2,0},{4,6},{6,4},{8,10},{10,8},{12,14},{14,12},{1,3},{3,1},... | collective-permute-start | bytes 98312 | tf_op jit(solution)/shard_map/ppermute | solution.py:325
  15.3 4.2 %collective-permute-start.7 = (bf16[8,16,128]{2,1,0:T(8,128)(2,1)S(1)}, bf16[8,16,128]{2,1,0:T(8,128)(2,1)S(1)}, u32[]{:S(2)}, u32[]{:S(2)}) collective-permute-start(bf16[8,16,128]{2,1,0:T(8,128)(2,1)S(1)} %collective-permute-done.3.refs_3_), channel_id=1, source_target_pairs={{0,2},{2,0},{4,6},{6,4},{8,10},{10,8},{12,14},{14,12},{1,3},{3,1},... | collective-permute-start | bytes 98312 | tf_op jit(solution)/shard_map/ppermute | solution.py:325
  16.6 3.9 %collective-permute-start.6 = (bf16[8,16,128]{2,1,0:T(8,128)(2,1)S(1)}, bf16[8,16,128]{2,1,0:T(8,128)(2,1)S(1)}, u32[]{:S(2)}, u32[]{:S(2)}) collective-permute-start(bf16[8,16,128]{2,1,0:T(8,128)(2,1)S(1)} %collective-permute-done.2.refs_2_), channel_id=1, source_target_pairs={{0,2},{2,0},{4,6},{6,4},{8,10},{10,8},{12,14},{14,12},{1,3},{3,1},... | collective-permute-start | bytes 98312 | tf_op jit(solution)/shard_map/ppermute | solution.py:325
  17.5 4.8 %collective-permute-start.9 = (bf16[3,3,3,32,128]{4,3,2,1,0:T(8,128)(2,1)S(1)}, bf16[3,3,3,32,128]{4,3,2,1,0:T(8,128)(2,1)S(1)}, u32[]{:S(2)}, u32[]{:S(2)}) collective-permute-start(bf16[3,3,3,32,128]{4,3,2,1,0:T(8,128)(2,1)S(1)} %get-tuple-element.36), channel_id=1, source_target_pairs={{0,1},{1,0},{2,3},{3,2},{4,5},{5,4},{6,7},{7,6},{8,9},{9,8},{10,11... | collective-permute-start | bytes 663560 | tf_op jit(solution)/shard_map/ppermute | solution.py:330
  22.0 1.8 %collective-permute-start.8 = (bf16[2,8,96,128]{3,2,1,0:T(8,128)(2,1)S(1)}, bf16[2,8,96,128]{3,2,1,0:T(8,128)(2,1)S(1)}, u32[]{:S(2)}, u32[]{:S(2)}) collective-permute-start(bf16[2,8,96,128]{3,2,1,0:T(8,128)(2,1)S(1)} %shard_map.65.mine), channel_id=1, source_target_pairs={{0,1},{1,0},{2,3},{3,2},{4,5},{5,4},{6,7},{7,6},{8,9},{9,8},{10,11... | collective-permute-start | bytes 1179656 | tf_op jit(solution)/shard_map/ppermute | solution.py:366
  23.9 18.6 %copy-start.1 = (f32[256]{0:T(256)S(1)}, f32[256]{0:T(256)}, u32[]{:S(2)}) copy-start(f32[256]{0:T(256)} %param.10) | copy-start | bytes 3076
  27.6 8.0 %collective-permute-start.13 = (bf16[2,8,16,256]{3,2,1,0:T(8,128)(2,1)S(1)}, bf16[2,8,16,256]{3,2,1,0:T(8,128)(2,1)S(1)}, u32[]{:S(2)}, u32[]{:S(2)}) collective-permute-start(bf16[2,8,16,256]{3,2,1,0:T(8,128)(2,1)S(1)} %get-tuple-element.44), channel_id=1, source_target_pairs={{0,4},{2,6},{4,0},{6,2},{8,12},{10,14},{12,8},{14,10},{1,5},{3,7},... | collective-permute-start | bytes 393224 | tf_op jit(solution)/shard_map/ppermute | solution.py:325
  27.7 10.4 %collective-permute-start.11 = (bf16[8,16,256]{2,1,0:T(8,128)(2,1)S(1)}, bf16[8,16,256]{2,1,0:T(8,128)(2,1)S(1)}, u32[]{:S(2)}, u32[]{:S(2)}) collective-permute-start(bf16[8,16,256]{2,1,0:T(8,128)(2,1)S(1)} %get-tuple-element.42), channel_id=1, source_target_pairs={{0,8},{2,10},{4,12},{6,14},{8,0},{10,2},{12,4},{14,6},{1,9},{3,11}... | collective-permute-start | bytes 196616 | tf_op jit(solution)/shard_map/ppermute | solution.py:325
  29.1 9.1 %collective-permute-start.12 = (bf16[8,16,256]{2,1,0:T(8,128)(2,1)S(1)}, bf16[8,16,256]{2,1,0:T(8,128)(2,1)S(1)}, u32[]{:S(2)}, u32[]{:S(2)}) collective-permute-start(bf16[8,16,256]{2,1,0:T(8,128)(2,1)S(1)} %get-tuple-element.43), channel_id=1, source_target_pairs={{0,12},{2,14},{4,8},{6,10},{8,4},{10,6},{12,0},{14,2},{1,13},{3,15... | collective-permute-start | bytes 196616 | tf_op jit(solution)/shard_map/ppermute | solution.py:325
  36.2 6.2 %collective-permute-start.15 = (bf16[8,16,256]{2,1,0:T(8,128)(2,1)S(1)}, bf16[8,16,256]{2,1,0:T(8,128)(2,1)S(1)}, u32[]{:S(2)}, u32[]{:S(2)}) collective-permute-start(bf16[8,16,256]{2,1,0:T(8,128)(2,1)S(1)} %get-tuple-element.49), channel_id=1, source_target_pairs={{0,10},{2,8},{4,14},{6,12},{8,2},{10,0},{12,6},{14,4},{1,11},{3,9}... | collective-permute-start | bytes 196616 | tf_op jit(solution)/shard_map/ppermute | solution.py:325
  36.3 6.2 %collective-permute-start.16 = (bf16[8,16,256]{2,1,0:T(8,128)(2,1)S(1)}, bf16[8,16,256]{2,1,0:T(8,128)(2,1)S(1)}, u32[]{:S(2)}, u32[]{:S(2)}) collective-permute-start(bf16[8,16,256]{2,1,0:T(8,128)(2,1)S(1)} %get-tuple-element.50), channel_id=1, source_target_pairs={{0,2},{2,0},{4,6},{6,4},{8,10},{10,8},{12,14},{14,12},{1,3},{3,1},... | collective-permute-start | bytes 196616 | tf_op jit(solution)/shard_map/ppermute | solution.py:325
  36.4 6.1 %collective-permute-start.14 = (bf16[8,16,256]{2,1,0:T(8,128)(2,1)S(1)}, bf16[8,16,256]{2,1,0:T(8,128)(2,1)S(1)}, u32[]{:S(2)}, u32[]{:S(2)}) collective-permute-start(bf16[8,16,256]{2,1,0:T(8,128)(2,1)S(1)} %get-tuple-element.46), channel_id=1, source_target_pairs={{0,4},{2,6},{4,0},{6,2},{8,12},{10,14},{12,8},{14,10},{1,5},{3,7},... | collective-permute-start | bytes 196616 | tf_op jit(solution)/shard_map/ppermute | solution.py:325

commit v3 on v2

--- a/solution.py
+++ b/solution.py
@@ -173,12 +173,18 @@
 
 
 def group_sum(rows):
-    lane = lax.broadcasted_iota(jnp.int32, rows.shape, 1)
-    for step in (1, 2, 4, 8):
-        ahead = pltpu.roll(rows, 128 - step, 1)
-        behind = pltpu.roll(rows, step, 1)
-        rows = rows + jnp.where((lane & step) == 0, ahead, behind)
-    return rows
+    count = rows.shape[0]
+    row = lax.broadcasted_iota(jnp.int32, (128, 128), 0)
+    lane = lax.broadcasted_iota(jnp.int32, (128, 128), 1)
+    same = (row >> 4 == lane >> 4).astype(jnp.bfloat16)
+    terms = []
+    for _ in range(3):
+        term = rows.astype(jnp.bfloat16)
+        terms.append(term.astype(jnp.float32))
+        rows = rows - term.astype(jnp.float32)
+    terms = jnp.concatenate(terms, axis=0).astype(jnp.bfloat16)
+    sums = jnp.dot(terms, same, preferred_element_type=jnp.float32)
+    return sums[:count] + sums[count : 2 * count] + sums[2 * count :]
 
 
 def norm_body(pos, gain, shift, *refs):
@@ -349,7 +355,7 @@
     other_far = across(quarters[3], 1)
     packed = call(pack_body, [block] * 4)(pos, latent)
     near = [packed[0]] + [exchanged(packed[k], k, 0) for k in (1, 2, 3)]
-    same_far, near[2] = lax.optimization_barrier((same_far, near[2]))
+    other_far, near[3] = lax.optimization_barrier((other_far, near[3]))
     far = [exchanged(part, 0, 1) for part in near]
     matrix = jax.ShapeDtypeStruct((TAPS, 768, 256), bf16)
     diag, lower = call(weights_body, [matrix] * 2)(pos, same, other, same_far, other_far)

time: 43.9 us -> 42.3 us (0.964)
  waiting for transfers between devices: 15.3 us -> 10.3 us
  starting transfers between devices: 17.6 us -> 21.3 us
    ppermute x14, waiting for transfers between devices: 14.6 us -> 9.58 us  [exchanged(): return lax.ppermute(block, ('tile', 'tm'), route)]
    ppermute x2, starting transfers between devices: 0.02 us -> 2.51 us  [across(): return lax.ppermute(block, ('tm', 'ch'), route)]
    ppermute x14, starting transfers between devices: 17.5 us -> 18.8 us  [exchanged(): return lax.ppermute(block, ('tile', 'tm'), route)]
  transfers between devices with their start and end apart: 17 -> 17, of which waited for: 8 -> 11; matrix products, arithmetic and copies ran while one was open for 1% -> 1% of each run, Pallas kernels for 9% -> 8%
where the time goes in v3:
time: 42.3 us; the launch traced here: 42.1 us
  starting transfers between devices  21.3 us (50%)
  waiting for transfers between devices  10.3 us (24%)
  Pallas kernels  8.52 us (20%)
  local copies, waits for them, and re-layouts  1.61 us (4%)
    ppermute x14, starting transfers between devices, exchanged(): return lax.ppermute(block, ('tile', 'tm'), route)  18.8 us
    ppermute x14, waiting for transfers between devices, exchanged(): return lax.ppermute(block, ('tile', 'tm'), route)  9.58 us
    pallas_call x6, Pallas kernels, run(): pl.pallas_call(body, out_shape=outs, in_specs=specs, out_specs=jax.tree.m...  8.52 us
    ppermute x2, starting transfers between devices, across(): return lax.ppermute(block, ('tm', 'ch'), route)  2.51 us
    dynamic_slice x1, local copies, waits for them, and re-layouts, quarter(): return lax.dynamic_slice_in_dim(kernel, start, 128, axis=4)  1.37 us
  transfers between devices with their start and end apart: 17, of which 11 were waited for; matrix products, arithmetic and copies ran while one was open for 1% of the time, Pallas kernels for 8%

profile of v3, /device:TPU:0, one launch (start us, length us, event | category | flops | bytes accessed | tf_op | source)
XLA Modules:
  0.0 42.1 jit_solution(18127453718589695907)
XLA Ops:
  0.0 0.0 copy-start
  0.0 0.0 copy-start.2
  0.0 0.0 copy-start.3
  0.0 0.0 copy-start.4
  0.0 1.4 %constant_dynamic-slice_fusion = (bf16[3,3,3,32,128]{4,3,2,1,0:T(8,128)(2,1)S(1)}, bf16[3,3,3,32,128]{4,3,2,1,0:T(8,128)(2,1)S(1)}, bf16[3,3,3,32,128]{4,3,2,1,0:T(8,128)(2,1)S(1)}, bf16[3,3,3,32,128]{4,3,2,1,0:T(8,128)(2,1)S(1)}) fusion(bf16[3,3,3,32,512]{4,3,2,1,0:T(8,128)(2,1)} %param.9, s32[]{:T(128)S(6)} %select_n.20, s32[]{:T(128)S(6)} %select_n.18, ...), kind=kLoop, calls=%fused_computation.1 | loop fusion | bytes 1769488 | tf_op jit(solution)/shard_map/dynamic_slice | solution.py:348
  1.4 2.5 %collective-permute-start.2 = (bf16[3,3,3,32,128]{4,3,2,1,0:T(8,128)(2,1)S(1)}, bf16[3,3,3,32,128]{4,3,2,1,0:T(8,128)(2,1)S(1)}, u32[]{:S(2)}, u32[]{:S(2)}) collective-permute-start(bf16[3,3,3,32,128]{4,3,2,1,0:T(8,128)(2,1)S(1)} %get-tuple-element.32), channel_id=1, source_target_pairs={{0,3},{1,2},{2,1},{3,0},{4,7},{5,6},{6,5},{7,4},{8,11},{9,10},{10,... | collective-permute-start | bytes 663560 | tf_op jit(solution)/shard_map/ppermute | solution.py:336
  3.9 0.1 pad_add_fusion.pos
  4.0 0.0 copy-done
  4.0 0.9 %shard_map.64 = (bf16[8,16,128]{2,1,0:T(8,128)(2,1)S(1)}, bf16[8,16,128]{2,1,0:T(8,128)(2,1)S(1)}, bf16[8,16,128]{2,1,0:T(8,128)(2,1)S(1)}, bf16[8,16,128]{2,1,0:T(8,128)(2,1)S(1)}) custom-call(s32[2]{0:T(128)S(1)} %pad_add_fusion.pos, bf16[2,8,16,256]{3,2,1,0:T(8,128)(2,1)S(1)} %copy-done), custom_call_target="tpu_custom_call" | custom-call | flops 1000 | bytes 1000 | tf_op jit(solution)/shard_map/pallas_call | solution.py:147
  4.8 3.6 %collective-permute-start.3 = (bf16[8,16,128]{2,1,0:T(8,128)(2,1)S(1)}, bf16[8,16,128]{2,1,0:T(8,128)(2,1)S(1)}, u32[]{:S(2)}, u32[]{:S(2)}) collective-permute-start(bf16[8,16,128]{2,1,0:T(8,128)(2,1)S(1)} %get-tuple-element.33), channel_id=1, source_target_pairs={{0,12},{2,14},{4,8},{6,10},{8,4},{10,6},{12,0},{14,2},{1,13},{3,15... | collective-permute-start | bytes 98312 | tf_op jit(solution)/shard_map/ppermute | solution.py:331
  8.5 0.6 %collective-permute-start.10 = (bf16[3,3,3,32,128]{4,3,2,1,0:T(8,128)(2,1)S(1)}, bf16[3,3,3,32,128]{4,3,2,1,0:T(8,128)(2,1)S(1)}, u32[]{:S(2)}, u32[]{:S(2)}) collective-permute-start(bf16[3,3,3,32,128]{4,3,2,1,0:T(8,128)(2,1)S(1)} %get-tuple-element.37), channel_id=1, source_target_pairs={{0,2},{2,0},{4,6},{6,4},{8,10},{10,8},{12,14},{14,12},{1,3},{3,1},... | collective-permute-start | bytes 663560 | tf_op jit(solution)/shard_map/ppermute | solution.py:331
  9.1 0.0 collective-permute-start
  9.1 0.8 %collective-permute-start.1 = (bf16[8,16,128]{2,1,0:T(8,128)(2,1)S(1)}, bf16[8,16,128]{2,1,0:T(8,128)(2,1)S(1)}, u32[]{:S(2)}, u32[]{:S(2)}) collective-permute-start(bf16[8,16,128]{2,1,0:T(8,128)(2,1)S(1)} %get-tuple-element.31), channel_id=1, source_target_pairs={{0,8},{2,10},{4,12},{6,14},{8,0},{10,2},{12,4},{14,6},{1,9},{3,11}... | collective-permute-start | bytes 98312 | tf_op jit(solution)/shard_map/ppermute | solution.py:331
  9.9 0.0 copy-done.2
  9.9 0.1 dynamic_slice.18
  10.0 0.0 copy-done.3
  10.0 0.1 dynamic_slice.19
  10.0 0.8 %collective-permute-done.3.refs_3_ = bf16[8,16,128]{2,1,0:T(8,128)(2,1)S(1)} collective-permute-done((bf16[8,16,128]{2,1,0:T(8,128)(2,1)S(1)}, bf16[8,16,128]{2,1,0:T(8,128)(2,1)S(1)}, u32[]{:S(2)}, u32[]{:S(2)}) %collective-permute-start.3) | collective-permute-done | bytes 32800 | tf_op jit(solution)/shard_map/ppermute | solution.py:331
  10.8 0.7 %collective-permute-start.4 = (bf16[8,16,128]{2,1,0:T(8,128)(2,1)S(1)}, bf16[8,16,128]{2,1,0:T(8,128)(2,1)S(1)}, u32[]{:S(2)}, u32[]{:S(2)}) collective-permute-start(bf16[8,16,128]{2,1,0:T(8,128)(2,1)S(1)} %get-tuple-element.29.refs_0_), channel_id=1, source_target_pairs={{0,2},{2,0},{4,6},{6,4},{8,10},{10,8},{12,14},{14,12},{1,3},{3,1},... | collective-permute-start | bytes 98312 | tf_op jit(solution)/shard_map/ppermute | solution.py:331
  11.5 1.8 %collective-permute-done.refs_1_ = bf16[8,16,128]{2,1,0:T(8,128)(2,1)S(1)} collective-permute-done((bf16[8,16,128]{2,1,0:T(8,128)(2,1)S(1)}, bf16[8,16,128]{2,1,0:T(8,128)(2,1)S(1)}, u32[]{:S(2)}, u32[]{:S(2)}) %collective-permute-start) | collective-permute-done | bytes 32800 | tf_op jit(solution)/shard_map/ppermute | solution.py:331
  13.3 1.4 %collective-permute-start.5 = (bf16[8,16,128]{2,1,0:T(8,128)(2,1)S(1)}, bf16[8,16,128]{2,1,0:T(8,128)(2,1)S(1)}, u32[]{:S(2)}, u32[]{:S(2)}) collective-permute-start(bf16[8,16,128]{2,1,0:T(8,128)(2,1)S(1)} %collective-permute-done.refs_1_), channel_id=1, source_target_pairs={{0,2},{2,0},{4,6},{6,4},{8,10},{10,8},{12,14},{14,12},{1,3},{3,1},... | collective-permute-start | bytes 98312 | tf_op jit(solution)/shard_map/ppermute | solution.py:331
  14.8 0.0 collective-permute-done.1.refs_2_
  14.8 0.6 %collective-permute-start.6 = (bf16[8,16,128]{2,1,0:T(8,128)(2,1)S(1)}, bf16[8,16,128]{2,1,0:T(8,128)(2,1)S(1)}, u32[]{:S(2)}, u32[]{:S(2)}) collective-permute-start(bf16[8,16,128]{2,1,0:T(8,128)(2,1)S(1)} %collective-permute-done.1.refs_2_), channel_id=1, source_target_pairs={{0,2},{2,0},{4,6},{6,4},{8,10},{10,8},{12,14},{14,12},{1,3},{3,1},... | collective-permute-start | bytes 98312 | tf_op jit(solution)/shard_map/ppermute | solution.py:331
  15.4 0.0 collective-permute-done.2.other_far
  15.4 1.4 %collective-permute-start.7 = (bf16[8,16,128]{2,1,0:T(8,128)(2,1)S(1)}, bf16[8,16,128]{2,1,0:T(8,128)(2,1)S(1)}, u32[]{:S(2)}, u32[]{:S(2)}) collective-permute-start(bf16[8,16,128]{2,1,0:T(8,128)(2,1)S(1)} %collective-permute-done.3.refs_3_), channel_id=1, source_target_pairs={{0,2},{2,0},{4,6},{6,4},{8,10},{10,8},{12,14},{14,12},{1,3},{3,1},... | collective-permute-start | bytes 98312 | tf_op jit(solution)/shard_map/ppermute | solution.py:331
  16.8 0.1 maximum_bitcast_fusion
  16.9 0.5 %collective-permute-done.4.refs_4_ = bf16[8,16,128]{2,1,0:T(8,128)(2,1)S(1)} collective-permute-done((bf16[8,16,128]{2,1,0:T(8,128)(2,1)S(1)}, bf16[8,16,128]{2,1,0:T(8,128)(2,1)S(1)}, u32[]{:S(2)}, u32[]{:S(2)}) %collective-permute-start.4) | collective-permute-done | bytes 32800 | tf_op jit(solution)/shard_map/ppermute | solution.py:331
  17.4 0.0 collective-permute-start.9
  17.4 0.7 %collective-permute-done.5.refs_5_ = bf16[8,16,128]{2,1,0:T(8,128)(2,1)S(1)} collective-permute-done((bf16[8,16,128]{2,1,0:T(8,128)(2,1)S(1)}, bf16[8,16,128]{2,1,0:T(8,128)(2,1)S(1)}, u32[]{:S(2)}, u32[]{:S(2)}) %collective-permute-start.5) | collective-permute-done | bytes 32800 | tf_op jit(solution)/shard_map/ppermute | solution.py:331
  18.1 0.6 %collective-permute-done.6.refs_6_ = bf16[8,16,128]{2,1,0:T(8,128)(2,1)S(1)} collective-permute-done((bf16[8,16,128]{2,1,0:T(8,128)(2,1)S(1)}, bf16[8,16,128]{2,1,0:T(8,128)(2,1)S(1)}, u32[]{:S(2)}, u32[]{:S(2)}) %collective-permute-start.6) | collective-permute-done | bytes 32800 | tf_op jit(solution)/shard_map/ppermute | solution.py:331
  18.7 0.6 %collective-permute-done.7.refs_7_ = bf16[8,16,128]{2,1,0:T(8,128)(2,1)S(1)} collective-permute-done((bf16[8,16,128]{2,1,0:T(8,128)(2,1)S(1)}, bf16[8,16,128]{2,1,0:T(8,128)(2,1)S(1)}, u32[]{:S(2)}, u32[]{:S(2)}) %collective-permute-start.7) | collective-permute-done | bytes 32800 | tf_op jit(solution)/shard_map/ppermute | solution.py:331
  19.3 1.2 %shard_map.65.mine = bf16[2,8,96,128]{3,2,1,0:T(8,128)(2,1)S(1)} custom-call(s32[2]{0:T(128)S(1)} %pad_add_fusion.pos, f32[1,128]{1,0:T(1,128)S(1)} %get-tuple-element.55.gain, f32[1,128]{1,0:T(1,128)S(1)} %get-tuple-element.56.shift, bf16[8,16,128]{2,1,0:T(8,128)(2,1)S(1)} %get-tuple-element.29.refs_0_, ...), custom_call_target="tpu_custom_call" | custom-call | flops 1000 | bytes 1000 | tf_op jit(solution)/shard_map/pallas_call | solution.py:147
  20.5 0.1 collective-permute-start.8
  20.6 0.0 copy-done.4
  20.6 0.1 add_divide_fusion
  20.7 0.0 collective-permute-done.10.same_far
  20.7 0.0 collective-permute-done.9.other
  20.7 0.9 %shard_map.66 = (bf16[3,768,256]{2,1,0:T(8,128)(2,1)S(1)}, bf16[3,768,256]{2,1,0:T(8,128)(2,1)S(1)}) custom-call(s32[2]{0:T(128)S(1)} %pad_add_fusion.pos, bf16[3,3,3,32,128]{4,3,2,1,0:T(8,128)(2,1)S(1)} %get-tuple-element.35.same, bf16[3,3,3,32,128]{4,3,2,1,0:T(8,128)(2,1)S(1)} %collective-permute-done.9.other, ...), custom_call_target="tpu_custom_call" | custom-call | flops 1000 | bytes 1000 | tf_op jit(solution)/shard_map/pallas_call | solution.py:147
  21.6 0.7 %collective-permute-done.8.sibling = bf16[2,8,96,128]{3,2,1,0:T(8,128)(2,1)S(1)} collective-permute-done((bf16[2,8,96,128]{3,2,1,0:T(8,128)(2,1)S(1)}, bf16[2,8,96,128]{3,2,1,0:T(8,128)(2,1)S(1)}, u32[]{:S(2)}, u32[]{:S(2)}) %collective-permute-start.8) | collective-permute-done | bytes 393248 | tf_op jit(solution)/shard_map/ppermute | solution.py:372
  22.3 0.1 broadcast_in_dim.20.blend
  22.4 0.0 copy-start.1
  22.4 3.8 %shard_map.67 = (f32[8,16,256]{2,1,0:T(8,128)S(1)}, bf16[8,16,256]{2,1,0:T(8,128)(2,1)S(1)}, bf16[8,16,256]{2,1,0:T(8,128)(2,1)S(1)}, bf16[8,16,256]{2,1,0:T(8,1...) custom-call(s32[2]{0:T(128)S(1)} %pad_add_fusion.pos, ...), custom_call_target="tpu_custom_call" | custom-call | flops 1000 | bytes 1000 | tf_op jit(solution)/shard_map/pallas_call | solution.py:147
  26.1 2.1 %collective-permute-start.13 = (bf16[2,8,16,256]{3,2,1,0:T(8,128)(2,1)S(1)}, bf16[2,8,16,256]{3,2,1,0:T(8,128)(2,1)S(1)}, u32[]{:S(2)}, u32[]{:S(2)}) collective-permute-start(bf16[2,8,16,256]{3,2,1,0:T(8,128)(2,1)S(1)} %get-tuple-element.44), channel_id=1, source_target_pairs={{0,4},{2,6},{4,0},{6,2},{8,12},{10,14},{12,8},{14,10},{1,5},{3,7},... | collective-permute-start | bytes 393224 | tf_op jit(solution)/shard_map/ppermute | solution.py:331
  28.2 1.1 %collective-permute-start.11 = (bf16[8,16,256]{2,1,0:T(8,128)(2,1)S(1)}, bf16[8,16,256]{2,1,0:T(8,128)(2,1)S(1)}, u32[]{:S(2)}, u32[]{:S(2)}) collective-permute-start(bf16[8,16,256]{2,1,0:T(8,128)(2,1)S(1)} %get-tuple-element.42), channel_id=1, source_target_pairs={{0,8},{2,10},{4,12},{6,14},{8,0},{10,2},{12,4},{14,6},{1,9},{3,11}... | collective-permute-start | bytes 196616 | tf_op jit(solution)/shard_map/ppermute | solution.py:331
  29.3 1.3 %collective-permute-start.12 = (bf16[8,16,256]{2,1,0:T(8,128)(2,1)S(1)}, bf16[8,16,256]{2,1,0:T(8,128)(2,1)S(1)}, u32[]{:S(2)}, u32[]{:S(2)}) collective-permute-start(bf16[8,16,256]{2,1,0:T(8,128)(2,1)S(1)} %get-tuple-element.43), channel_id=1, source_target_pairs={{0,12},{2,14},{4,8},{6,10},{8,4},{10,6},{12,0},{14,2},{1,13},{3,15... | collective-permute-start | bytes 196616 | tf_op jit(solution)/shard_map/ppermute | solution.py:331
  30.6 2.1 %collective-permute-done.13.came = bf16[2,8,16,256]{3,2,1,0:T(8,128)(2,1)S(1)} collective-permute-done((bf16[2,8,16,256]{3,2,1,0:T(8,128)(2,1)S(1)}, bf16[2,8,16,256]{3,2,1,0:T(8,128)(2,1)S(1)}, u32[]{:S(2)}, u32[]{:S(2)}) %collective-permute-start.13) | collective-permute-done | bytes 131104 | tf_op jit(solution)/shard_map/ppermute | solution.py:331
  32.7 0.6 %shard_map.68 = (bf16[8,16,256]{2,1,0:T(8,128)(2,1)S(1)}, bf16[8,16,256]{2,1,0:T(8,128)(2,1)S(1)}) custom-call(s32[2]{0:T(128)S(1)} %pad_add_fusion.pos, f32[2,8,16,256]{3,2,1,0:T(8,128)S(1)} %get-tuple-element.47.kept, bf16[2,8,16,256]{3,2,1,0:T(8,128)(2,1)S(1)} %collective-permute-done.13.came), custom_call_target="tpu_custom_call" | custom-call | flops 1000 | bytes 1000 | tf_op jit(solution)/shard_map/pallas_call | solution.py:147
  33.3 2.4 %collective-permute-start.15 = (bf16[8,16,256]{2,1,0:T(8,128)(2,1)S(1)}, bf16[8,16,256]{2,1,0:T(8,128)(2,1)S(1)}, u32[]{:S(2)}, u32[]{:S(2)}) collective-permute-start(bf16[8,16,256]{2,1,0:T(8,128)(2,1)S(1)} %get-tuple-element.49), channel_id=1, source_target_pairs={{0,10},{2,8},{4,14},{6,12},{8,2},{10,0},{12,6},{14,4},{1,11},{3,9}... | collective-permute-start | bytes 196616 | tf_op jit(solution)/shard_map/ppermute | solution.py:331
  35.6 0.5 %collective-permute-start.16 = (bf16[8,16,256]{2,1,0:T(8,128)(2,1)S(1)}, bf16[8,16,256]{2,1,0:T(8,128)(2,1)S(1)}, u32[]{:S(2)}, u32[]{:S(2)}) collective-permute-start(bf16[8,16,256]{2,1,0:T(8,128)(2,1)S(1)} %get-tuple-element.50), channel_id=1, source_target_pairs={{0,2},{2,0},{4,6},{6,4},{8,10},{10,8},{12,14},{14,12},{1,3},{3,1},... | collective-permute-start | bytes 196616 | tf_op jit(solution)/shard_map/ppermute | solution.py:331
  36.2 2.2 %collective-permute-start.14 = (bf16[8,16,256]{2,1,0:T(8,128)(2,1)S(1)}, bf16[8,16,256]{2,1,0:T(8,128)(2,1)S(1)}, u32[]{:S(2)}, u32[]{:S(2)}) collective-permute-start(bf16[8,16,256]{2,1,0:T(8,128)(2,1)S(1)} %get-tuple-element.46), channel_id=1, source_target_pairs={{0,4},{2,6},{4,0},{6,2},{8,12},{10,14},{12,8},{14,10},{1,5},{3,7},... | collective-permute-start | bytes 196616 | tf_op jit(solution)/shard_map/ppermute | solution.py:331
  38.4 0.0 collective-permute-done.11.refs_0_
  38.4 0.0 collective-permute-done.12.refs_1_
  38.4 1.1 %collective-permute-done.15.refs_3_ = bf16[8,16,256]{2,1,0:T(8,128)(2,1)S(1)} collective-permute-done((bf16[8,16,256]{2,1,0:T(8,128)(2,1)S(1)}, bf16[8,16,256]{2,1,0:T(8,128)(2,1)S(1)}, u32[]{:S(2)}, u32[]{:S(2)}) %collective-permute-start.15) | collective-permute-done | bytes 65568 | tf_op jit(solution)/shard_map/ppermute | solution.py:331
  39.5 0.7 %collective-permute-done.16.refs_4_ = bf16[8,16,256]{2,1,0:T(8,128)(2,1)S(1)} collective-permute-done((bf16[8,16,256]{2,1,0:T(8,128)(2,1)S(1)}, bf16[8,16,256]{2,1,0:T(8,128)(2,1)S(1)}, u32[]{:S(2)}, u32[]{:S(2)}) %collective-permute-start.16) | collective-permute-done | bytes 65568 | tf_op jit(solution)/shard_map/ppermute | solution.py:331
  40.1 0.7 %collective-permute-done.14.refs_2_ = bf16[8,16,256]{2,1,0:T(8,128)(2,1)S(1)} collective-permute-done((bf16[8,16,256]{2,1,0:T(8,128)(2,1)S(1)}, bf16[8,16,256]{2,1,0:T(8,128)(2,1)S(1)}, u32[]{:S(2)}, u32[]{:S(2)}) %collective-permute-start.14) | collective-permute-done | bytes 65568 | tf_op jit(solution)/shard_map/ppermute | solution.py:331
  40.9 0.0 copy-done.1
  40.9 1.3 %shard_map.69 = bf16[2,8,16,256]{3,2,1,0:T(8,128)(2,1)} custom-call(s32[2]{0:T(128)S(1)} %pad_add_fusion.pos, f32[1,256]{1,0:T(1,128)S(1)} %bitcast.7, f32[8,16,256]{2,1,0:T(8,128)S(1)} %get-tuple-element.41.own, bf16[8,16,256]{2,1,0:T(8,128)(2,1)S(1)} %collective-permute-done.11.refs_0_, bf16[8,16,256]{2,1,0:T(8,128)(2,1)S(1)} %collective-permute-done.12.refs_1_, ...), custom_call_target="tpu_custom_call" | custom-call | flops 1000 | bytes 1000 | tf_op jit(solution)/shard_map/pallas_call | solution.py:147
  (2 shorter events, 0.0 us)
Async XLA Ops:
  0.0 4.0 %copy-start = (bf16[2,8,16,256]{3,2,1,0:T(8,128)(2,1)S(1)}, bf16[2,8,16,256]{3,2,1,0:T(8,128)(2,1)}, u32[]{:S(2)}) copy-start(bf16[2,8,16,256]{3,2,1,0:T(8,128)(2,1)} %latent) | copy-start | bytes 393220
  0.0 9.9 %copy-start.2 = (f32[256]{0:T(256)S(1)}, f32[256]{0:T(256)}, u32[]{:S(2)}) copy-start(f32[256]{0:T(256)} %param.7) | copy-start | bytes 3076
  0.0 10.0 %copy-start.3 = (f32[256]{0:T(256)S(1)}, f32[256]{0:T(256)}, u32[]{:S(2)}) copy-start(f32[256]{0:T(256)} %param.8) | copy-start | bytes 3076
  0.0 20.6 %copy-start.4 = (s32[4]{0:T(128)S(1)}, s32[4]{0:T(128)}, u32[]{:S(2)}) copy-start(s32[4]{0:T(128)} %param.11) | copy-start | bytes 52
  1.4 14.0 %collective-permute-start.2 = (bf16[3,3,3,32,128]{4,3,2,1,0:T(8,128)(2,1)S(1)}, bf16[3,3,3,32,128]{4,3,2,1,0:T(8,128)(2,1)S(1)}, u32[]{:S(2)}, u32[]{:S(2)}) collective-permute-start(bf16[3,3,3,32,128]{4,3,2,1,0:T(8,128)(2,1)S(1)} %get-tuple-element.32), channel_id=1, source_target_pairs={{0,3},{1,2},{2,1},{3,0},{4,7},{5,6},{6,5},{7,4},{8,11},{9,10},{10,... | collective-permute-start | bytes 663560 | tf_op jit(solution)/shard_map/ppermute | solution.py:336
  4.8 6.0 %collective-permute-start.3 = (bf16[8,16,128]{2,1,0:T(8,128)(2,1)S(1)}, bf16[8,16,128]{2,1,0:T(8,128)(2,1)S(1)}, u32[]{:S(2)}, u32[]{:S(2)}) collective-permute-start(bf16[8,16,128]{2,1,0:T(8,128)(2,1)S(1)} %get-tuple-element.33), channel_id=1, source_target_pairs={{0,12},{2,14},{4,8},{6,10},{8,4},{10,6},{12,0},{14,2},{1,13},{3,15... | collective-permute-start | bytes 98312 | tf_op jit(solution)/shard_map/ppermute | solution.py:331
  8.5 12.2 %collective-permute-start.10 = (bf16[3,3,3,32,128]{4,3,2,1,0:T(8,128)(2,1)S(1)}, bf16[3,3,3,32,128]{4,3,2,1,0:T(8,128)(2,1)S(1)}, u32[]{:S(2)}, u32[]{:S(2)}) collective-permute-start(bf16[3,3,3,32,128]{4,3,2,1,0:T(8,128)(2,1)S(1)} %get-tuple-element.37), channel_id=1, source_target_pairs={{0,2},{2,0},{4,6},{6,4},{8,10},{10,8},{12,14},{14,12},{1,3},{3,1},... | collective-permute-start | bytes 663560 | tf_op jit(solution)/shard_map/ppermute | solution.py:331
  9.1 4.3 %collective-permute-start = (bf16[8,16,128]{2,1,0:T(8,128)(2,1)S(1)}, bf16[8,16,128]{2,1,0:T(8,128)(2,1)S(1)}, u32[]{:S(2)}, u32[]{:S(2)}) collective-permute-start(bf16[8,16,128]{2,1,0:T(8,128)(2,1)S(1)} %get-tuple-element.30), channel_id=1, source_target_pairs={{0,4},{2,6},{4,0},{6,2},{8,12},{10,14},{12,8},{14,10},{1,5},{3,7},... | collective-permute-start | bytes 98312 | tf_op jit(solution)/shard_map/ppermute | solution.py:331
  9.1 5.7 %collective-permute-start.1 = (bf16[8,16,128]{2,1,0:T(8,128)(2,1)S(1)}, bf16[8,16,128]{2,1,0:T(8,128)(2,1)S(1)}, u32[]{:S(2)}, u32[]{:S(2)}) collective-permute-start(bf16[8,16,128]{2,1,0:T(8,128)(2,1)S(1)} %get-tuple-element.31), channel_id=1, source_target_pairs={{0,8},{2,10},{4,12},{6,14},{8,0},{10,2},{12,4},{14,6},{1,9},{3,11}... | collective-permute-start | bytes 98312 | tf_op jit(solution)/shard_map/ppermute | solution.py:331
  10.8 6.6 %collective-permute-start.4 = (bf16[8,16,128]{2,1,0:T(8,128)(2,1)S(1)}, bf16[8,16,128]{2,1,0:T(8,128)(2,1)S(1)}, u32[]{:S(2)}, u32[]{:S(2)}) collective-permute-start(bf16[8,16,128]{2,1,0:T(8,128)(2,1)S(1)} %get-tuple-element.29.refs_0_), channel_id=1, source_target_pairs={{0,2},{2,0},{4,6},{6,4},{8,10},{10,8},{12,14},{14,12},{1,3},{3,1},... | collective-permute-start | bytes 98312 | tf_op jit(solution)/shard_map/ppermute | solution.py:331
  13.3 4.8 %collective-permute-start.5 = (bf16[8,16,128]{2,1,0:T(8,128)(2,1)S(1)}, bf16[8,16,128]{2,1,0:T(8,128)(2,1)S(1)}, u32[]{:S(2)}, u32[]{:S(2)}) collective-permute-start(bf16[8,16,128]{2,1,0:T(8,128)(2,1)S(1)} %collective-permute-done.refs_1_), channel_id=1, source_target_pairs={{0,2},{2,0},{4,6},{6,4},{8,10},{10,8},{12,14},{14,12},{1,3},{3,1},... | collective-permute-start | bytes 98312 | tf_op jit(solution)/shard_map/ppermute | solution.py:331
  14.8 3.9 %collective-permute-start.6 = (bf16[8,16,128]{2,1,0:T(8,128)(2,1)S(1)}, bf16[8,16,128]{2,1,0:T(8,128)(2,1)S(1)}, u32[]{:S(2)}, u32[]{:S(2)}) collective-permute-start(bf16[8,16,128]{2,1,0:T(8,128)(2,1)S(1)} %collective-permute-done.1.refs_2_), channel_id=1, source_target_pairs={{0,2},{2,0},{4,6},{6,4},{8,10},{10,8},{12,14},{14,12},{1,3},{3,1},... | collective-permute-start | bytes 98312 | tf_op jit(solution)/shard_map/ppermute | solution.py:331
  15.4 3.9 %collective-permute-start.7 = (bf16[8,16,128]{2,1,0:T(8,128)(2,1)S(1)}, bf16[8,16,128]{2,1,0:T(8,128)(2,1)S(1)}, u32[]{:S(2)}, u32[]{:S(2)}) collective-permute-start(bf16[8,16,128]{2,1,0:T(8,128)(2,1)S(1)} %collective-permute-done.3.refs_3_), channel_id=1, source_target_pairs={{0,2},{2,0},{4,6},{6,4},{8,10},{10,8},{12,14},{14,12},{1,3},{3,1},... | collective-permute-start | bytes 98312 | tf_op jit(solution)/shard_map/ppermute | solution.py:331
  17.4 3.3 %collective-permute-start.9 = (bf16[3,3,3,32,128]{4,3,2,1,0:T(8,128)(2,1)S(1)}, bf16[3,3,3,32,128]{4,3,2,1,0:T(8,128)(2,1)S(1)}, u32[]{:S(2)}, u32[]{:S(2)}) collective-permute-start(bf16[3,3,3,32,128]{4,3,2,1,0:T(8,128)(2,1)S(1)} %get-tuple-element.36), channel_id=1, source_target_pairs={{0,1},{1,0},{2,3},{3,2},{4,5},{5,4},{6,7},{7,6},{8,9},{9,8},{10,11... | collective-permute-start | bytes 663560 | tf_op jit(solution)/shard_map/ppermute | solution.py:336
  20.5 1.8 %collective-permute-start.8 = (bf16[2,8,96,128]{3,2,1,0:T(8,128)(2,1)S(1)}, bf16[2,8,96,128]{3,2,1,0:T(8,128)(2,1)S(1)}, u32[]{:S(2)}, u32[]{:S(2)}) collective-permute-start(bf16[2,8,96,128]{3,2,1,0:T(8,128)(2,1)S(1)} %shard_map.65.mine), channel_id=1, source_target_pairs={{0,1},{1,0},{2,3},{3,2},{4,5},{5,4},{6,7},{7,6},{8,9},{9,8},{10,11... | collective-permute-start | bytes 1179656 | tf_op jit(solution)/shard_map/ppermute | solution.py:372
  22.4 18.5 %copy-start.1 = (f32[256]{0:T(256)S(1)}, f32[256]{0:T(256)}, u32[]{:S(2)}) copy-start(f32[256]{0:T(256)} %param.10) | copy-start | bytes 3076
  26.1 6.6 %collective-permute-start.13 = (bf16[2,8,16,256]{3,2,1,0:T(8,128)(2,1)S(1)}, bf16[2,8,16,256]{3,2,1,0:T(8,128)(2,1)S(1)}, u32[]{:S(2)}, u32[]{:S(2)}) collective-permute-start(bf16[2,8,16,256]{3,2,1,0:T(8,128)(2,1)S(1)} %get-tuple-element.44), channel_id=1, source_target_pairs={{0,4},{2,6},{4,0},{6,2},{8,12},{10,14},{12,8},{14,10},{1,5},{3,7},... | collective-permute-start | bytes 393224 | tf_op jit(solution)/shard_map/ppermute | solution.py:331
  28.2 10.2 %collective-permute-start.11 = (bf16[8,16,256]{2,1,0:T(8,128)(2,1)S(1)}, bf16[8,16,256]{2,1,0:T(8,128)(2,1)S(1)}, u32[]{:S(2)}, u32[]{:S(2)}) collective-permute-start(bf16[8,16,256]{2,1,0:T(8,128)(2,1)S(1)} %get-tuple-element.42), channel_id=1, source_target_pairs={{0,8},{2,10},{4,12},{6,14},{8,0},{10,2},{12,4},{14,6},{1,9},{3,11}... | collective-permute-start | bytes 196616 | tf_op jit(solution)/shard_map/ppermute | solution.py:331
  29.3 9.0 %collective-permute-start.12 = (bf16[8,16,256]{2,1,0:T(8,128)(2,1)S(1)}, bf16[8,16,256]{2,1,0:T(8,128)(2,1)S(1)}, u32[]{:S(2)}, u32[]{:S(2)}) collective-permute-start(bf16[8,16,256]{2,1,0:T(8,128)(2,1)S(1)} %get-tuple-element.43), channel_id=1, source_target_pairs={{0,12},{2,14},{4,8},{6,10},{8,4},{10,6},{12,0},{14,2},{1,13},{3,15... | collective-permute-start | bytes 196616 | tf_op jit(solution)/shard_map/ppermute | solution.py:331
  33.3 6.2 %collective-permute-start.15 = (bf16[8,16,256]{2,1,0:T(8,128)(2,1)S(1)}, bf16[8,16,256]{2,1,0:T(8,128)(2,1)S(1)}, u32[]{:S(2)}, u32[]{:S(2)}) collective-permute-start(bf16[8,16,256]{2,1,0:T(8,128)(2,1)S(1)} %get-tuple-element.49), channel_id=1, source_target_pairs={{0,10},{2,8},{4,14},{6,12},{8,2},{10,0},{12,6},{14,4},{1,11},{3,9}... | collective-permute-start | bytes 196616 | tf_op jit(solution)/shard_map/ppermute | solution.py:331
  35.6 4.5 %collective-permute-start.16 = (bf16[8,16,256]{2,1,0:T(8,128)(2,1)S(1)}, bf16[8,16,256]{2,1,0:T(8,128)(2,1)S(1)}, u32[]{:S(2)}, u32[]{:S(2)}) collective-permute-start(bf16[8,16,256]{2,1,0:T(8,128)(2,1)S(1)} %get-tuple-element.50), channel_id=1, source_target_pairs={{0,2},{2,0},{4,6},{6,4},{8,10},{10,8},{12,14},{14,12},{1,3},{3,1},... | collective-permute-start | bytes 196616 | tf_op jit(solution)/shard_map/ppermute | solution.py:331
  36.2 4.7 %collective-permute-start.14 = (bf16[8,16,256]{2,1,0:T(8,128)(2,1)S(1)}, bf16[8,16,256]{2,1,0:T(8,128)(2,1)S(1)}, u32[]{:S(2)}, u32[]{:S(2)}) collective-permute-start(bf16[8,16,256]{2,1,0:T(8,128)(2,1)S(1)} %get-tuple-element.46), channel_id=1, source_target_pairs={{0,4},{2,6},{4,0},{6,2},{8,12},{10,14},{12,8},{14,10},{1,5},{3,7},... | collective-permute-start | bytes 196616 | tf_op jit(solution)/shard_map/ppermute | solution.py:331

commit v4 on v3

--- a/solution.py
+++ b/solution.py
@@ -389,7 +389,7 @@
     came, sends[0] = lax.optimization_barrier((came, sends[0]))
     sums = call(add_body, [wide] * 2)(pos, kept, came)
     far_sums = [exchanged(sums[1], 2, 1), exchanged(sums[0], 0, 1)]
-    near_sums = [exchanged(sends[k - 1], k, 0) for k in (2, 3, 1)]
+    near_sums = [exchanged(sends[k - 1], k, 0) for k in (3, 2, 1)]
     return call(join_body, jax.ShapeDtypeStruct(latent.shape, bf16))(
         pos, conv_bias[None], own, *near_sums, *far_sums
     )

time: 42.3 us -> 41.5 us (0.981)
  starting transfers between devices: 21.3 us -> 20.1 us
    ppermute x14, starting transfers between devices: 18.8 us -> 17.5 us  [exchanged(): return lax.ppermute(block, ('tile', 'tm'), route)]
    ppermute x14, waiting for transfers between devices: 9.58 us -> 10 us  [exchanged(): return lax.ppermute(block, ('tile', 'tm'), route)]
where the time goes in v4:
time: 41.5 us; the launch traced here: 41.4 us
  starting transfers between devices  20.1 us (48%)
  waiting for transfers between devices  10.7 us (26%)
  Pallas kernels  8.52 us (21%)
  local copies, waits for them, and re-layouts  1.61 us (4%)
    ppermute x14, starting transfers between devices, exchanged(): return lax.ppermute(block, ('tile', 'tm'), route)  17.5 us
    ppermute x14, waiting for transfers between devices, exchanged(): return lax.ppermute(block, ('tile', 'tm'), route)  10 us
    pallas_call x6, Pallas kernels, run(): pl.pallas_call(body, out_shape=outs, in_specs=specs, out_specs=jax.tree.m...  8.52 us
    ppermute x2, starting transfers between devices, across(): return lax.ppermute(block, ('tm', 'ch'), route)  2.51 us
    dynamic_slice x1, local copies, waits for them, and re-layouts, quarter(): return lax.dynamic_slice_in_dim(kernel, start, 128, axis=4)  1.37 us
  transfers between devices with their start and end apart: 17, of which 11 were waited for; matrix products, arithmetic and copies ran while one was open for 1% of the time, Pallas kernels for 8%

profile of v4, /device:TPU:0, one launch (start us, length us, event | category | flops | bytes accessed | tf_op | source)
XLA Modules:
  0.0 41.4 jit_solution(13729150612074036386)
XLA Ops:
  0.0 0.0 copy-start
  0.0 0.0 copy-start.2
  0.0 0.0 copy-start.3
  0.0 0.0 copy-start.4
  0.0 1.4 %constant_dynamic-slice_fusion = (bf16[3,3,3,32,128]{4,3,2,1,0:T(8,128)(2,1)S(1)}, bf16[3,3,3,32,128]{4,3,2,1,0:T(8,128)(2,1)S(1)}, bf16[3,3,3,32,128]{4,3,2,1,0:T(8,128)(2,1)S(1)}, bf16[3,3,3,32,128]{4,3,2,1,0:T(8,128)(2,1)S(1)}) fusion(bf16[3,3,3,32,512]{4,3,2,1,0:T(8,128)(2,1)} %param.9, s32[]{:T(128)S(6)} %select_n.20, s32[]{:T(128)S(6)} %select_n.18, ...), kind=kLoop, calls=%fused_computation.1 | loop fusion | bytes 1769488 | tf_op jit(solution)/shard_map/dynamic_slice | solution.py:348
  1.4 2.5 %collective-permute-start.2 = (bf16[3,3,3,32,128]{4,3,2,1,0:T(8,128)(2,1)S(1)}, bf16[3,3,3,32,128]{4,3,2,1,0:T(8,128)(2,1)S(1)}, u32[]{:S(2)}, u32[]{:S(2)}) collective-permute-start(bf16[3,3,3,32,128]{4,3,2,1,0:T(8,128)(2,1)S(1)} %get-tuple-element.32), channel_id=1, source_target_pairs={{0,3},{1,2},{2,1},{3,0},{4,7},{5,6},{6,5},{7,4},{8,11},{9,10},{10,... | collective-permute-start | bytes 663560 | tf_op jit(solution)/shard_map/ppermute | solution.py:336
  3.9 0.1 pad_add_fusion.pos
  4.0 0.0 copy-done
  4.0 0.9 %shard_map.64 = (bf16[8,16,128]{2,1,0:T(8,128)(2,1)S(1)}, bf16[8,16,128]{2,1,0:T(8,128)(2,1)S(1)}, bf16[8,16,128]{2,1,0:T(8,128)(2,1)S(1)}, bf16[8,16,128]{2,1,0:T(8,128)(2,1)S(1)}) custom-call(s32[2]{0:T(128)S(1)} %pad_add_fusion.pos, bf16[2,8,16,256]{3,2,1,0:T(8,128)(2,1)S(1)} %copy-done), custom_call_target="tpu_custom_call" | custom-call | flops 1000 | bytes 1000 | tf_op jit(solution)/shard_map/pallas_call | solution.py:147
  4.8 3.6 %collective-permute-start.3 = (bf16[8,16,128]{2,1,0:T(8,128)(2,1)S(1)}, bf16[8,16,128]{2,1,0:T(8,128)(2,1)S(1)}, u32[]{:S(2)}, u32[]{:S(2)}) collective-permute-start(bf16[8,16,128]{2,1,0:T(8,128)(2,1)S(1)} %get-tuple-element.33), channel_id=1, source_target_pairs={{0,12},{2,14},{4,8},{6,10},{8,4},{10,6},{12,0},{14,2},{1,13},{3,15... | collective-permute-start | bytes 98312 | tf_op jit(solution)/shard_map/ppermute | solution.py:331
  8.5 0.6 %collective-permute-start.10 = (bf16[3,3,3,32,128]{4,3,2,1,0:T(8,128)(2,1)S(1)}, bf16[3,3,3,32,128]{4,3,2,1,0:T(8,128)(2,1)S(1)}, u32[]{:S(2)}, u32[]{:S(2)}) collective-permute-start(bf16[3,3,3,32,128]{4,3,2,1,0:T(8,128)(2,1)S(1)} %get-tuple-element.37), channel_id=1, source_target_pairs={{0,2},{2,0},{4,6},{6,4},{8,10},{10,8},{12,14},{14,12},{1,3},{3,1},... | collective-permute-start | bytes 663560 | tf_op jit(solution)/shard_map/ppermute | solution.py:331
  9.1 0.0 collective-permute-start
  9.1 0.8 %collective-permute-start.1 = (bf16[8,16,128]{2,1,0:T(8,128)(2,1)S(1)}, bf16[8,16,128]{2,1,0:T(8,128)(2,1)S(1)}, u32[]{:S(2)}, u32[]{:S(2)}) collective-permute-start(bf16[8,16,128]{2,1,0:T(8,128)(2,1)S(1)} %get-tuple-element.31), channel_id=1, source_target_pairs={{0,8},{2,10},{4,12},{6,14},{8,0},{10,2},{12,4},{14,6},{1,9},{3,11}... | collective-permute-start | bytes 98312 | tf_op jit(solution)/shard_map/ppermute | solution.py:331
  9.9 0.0 copy-done.2
  9.9 0.1 dynamic_slice.18
  10.0 0.0 copy-done.3
  10.0 0.1 dynamic_slice.19
  10.0 0.8 %collective-permute-done.3.refs_3_ = bf16[8,16,128]{2,1,0:T(8,128)(2,1)S(1)} collective-permute-done((bf16[8,16,128]{2,1,0:T(8,128)(2,1)S(1)}, bf16[8,16,128]{2,1,0:T(8,128)(2,1)S(1)}, u32[]{:S(2)}, u32[]{:S(2)}) %collective-permute-start.3) | collective-permute-done | bytes 32800 | tf_op jit(solution)/shard_map/ppermute | solution.py:331
  10.8 0.7 %collective-permute-start.4 = (bf16[8,16,128]{2,1,0:T(8,128)(2,1)S(1)}, bf16[8,16,128]{2,1,0:T(8,128)(2,1)S(1)}, u32[]{:S(2)}, u32[]{:S(2)}) collective-permute-start(bf16[8,16,128]{2,1,0:T(8,128)(2,1)S(1)} %get-tuple-element.29.refs_0_), channel_id=1, source_target_pairs={{0,2},{2,0},{4,6},{6,4},{8,10},{10,8},{12,14},{14,12},{1,3},{3,1},... | collective-permute-start | bytes 98312 | tf_op jit(solution)/shard_map/ppermute | solution.py:331
  11.5 1.8 %collective-permute-done.refs_1_ = bf16[8,16,128]{2,1,0:T(8,128)(2,1)S(1)} collective-permute-done((bf16[8,16,128]{2,1,0:T(8,128)(2,1)S(1)}, bf16[8,16,128]{2,1,0:T(8,128)(2,1)S(1)}, u32[]{:S(2)}, u32[]{:S(2)}) %collective-permute-start) | collective-permute-done | bytes 32800 | tf_op jit(solution)/shard_map/ppermute | solution.py:331
  13.3 1.4 %collective-permute-start.5 = (bf16[8,16,128]{2,1,0:T(8,128)(2,1)S(1)}, bf16[8,16,128]{2,1,0:T(8,128)(2,1)S(1)}, u32[]{:S(2)}, u32[]{:S(2)}) collective-permute-start(bf16[8,16,128]{2,1,0:T(8,128)(2,1)S(1)} %collective-permute-done.refs_1_), channel_id=1, source_target_pairs={{0,2},{2,0},{4,6},{6,4},{8,10},{10,8},{12,14},{14,12},{1,3},{3,1},... | collective-permute-start | bytes 98312 | tf_op jit(solution)/shard_map/ppermute | solution.py:331
  14.8 0.0 collective-permute-done.1.refs_2_
  14.8 0.6 %collective-permute-start.6 = (bf16[8,16,128]{2,1,0:T(8,128)(2,1)S(1)}, bf16[8,16,128]{2,1,0:T(8,128)(2,1)S(1)}, u32[]{:S(2)}, u32[]{:S(2)}) collective-permute-start(bf16[8,16,128]{2,1,0:T(8,128)(2,1)S(1)} %collective-permute-done.1.refs_2_), channel_id=1, source_target_pairs={{0,2},{2,0},{4,6},{6,4},{8,10},{10,8},{12,14},{14,12},{1,3},{3,1},... | collective-permute-start | bytes 98312 | tf_op jit(solution)/shard_map/ppermute | solution.py:331
  15.4 0.0 collective-permute-done.2.other_far
  15.4 1.4 %collective-permute-start.7 = (bf16[8,16,128]{2,1,0:T(8,128)(2,1)S(1)}, bf16[8,16,128]{2,1,0:T(8,128)(2,1)S(1)}, u32[]{:S(2)}, u32[]{:S(2)}) collective-permute-start(bf16[8,16,128]{2,1,0:T(8,128)(2,1)S(1)} %collective-permute-done.3.refs_3_), channel_id=1, source_target_pairs={{0,2},{2,0},{4,6},{6,4},{8,10},{10,8},{12,14},{14,12},{1,3},{3,1},... | collective-permute-start | bytes 98312 | tf_op jit(solution)/shard_map/ppermute | solution.py:331
  16.8 0.1 maximum_bitcast_fusion
  16.9 0.5 %collective-permute-done.4.refs_4_ = bf16[8,16,128]{2,1,0:T(8,128)(2,1)S(1)} collective-permute-done((bf16[8,16,128]{2,1,0:T(8,128)(2,1)S(1)}, bf16[8,16,128]{2,1,0:T(8,128)(2,1)S(1)}, u32[]{:S(2)}, u32[]{:S(2)}) %collective-permute-start.4) | collective-permute-done | bytes 32800 | tf_op jit(solution)/shard_map/ppermute | solution.py:331
  17.4 0.0 collective-permute-start.9
  17.4 0.7 %collective-permute-done.5.refs_5_ = bf16[8,16,128]{2,1,0:T(8,128)(2,1)S(1)} collective-permute-done((bf16[8,16,128]{2,1,0:T(8,128)(2,1)S(1)}, bf16[8,16,128]{2,1,0:T(8,128)(2,1)S(1)}, u32[]{:S(2)}, u32[]{:S(2)}) %collective-permute-start.5) | collective-permute-done | bytes 32800 | tf_op jit(solution)/shard_map/ppermute | solution.py:331
  18.1 0.6 %collective-permute-done.6.refs_6_ = bf16[8,16,128]{2,1,0:T(8,128)(2,1)S(1)} collective-permute-done((bf16[8,16,128]{2,1,0:T(8,128)(2,1)S(1)}, bf16[8,16,128]{2,1,0:T(8,128)(2,1)S(1)}, u32[]{:S(2)}, u32[]{:S(2)}) %collective-permute-start.6) | collective-permute-done | bytes 32800 | tf_op jit(solution)/shard_map/ppermute | solution.py:331
  18.7 0.6 %collective-permute-done.7.refs_7_ = bf16[8,16,128]{2,1,0:T(8,128)(2,1)S(1)} collective-permute-done((bf16[8,16,128]{2,1,0:T(8,128)(2,1)S(1)}, bf16[8,16,128]{2,1,0:T(8,128)(2,1)S(1)}, u32[]{:S(2)}, u32[]{:S(2)}) %collective-permute-start.7) | collective-permute-done | bytes 32800 | tf_op jit(solution)/shard_map/ppermute | solution.py:331
  19.3 1.2 %shard_map.65.mine = bf16[2,8,96,128]{3,2,1,0:T(8,128)(2,1)S(1)} custom-call(s32[2]{0:T(128)S(1)} %pad_add_fusion.pos, f32[1,128]{1,0:T(1,128)S(1)} %get-tuple-element.55.gain, f32[1,128]{1,0:T(1,128)S(1)} %get-tuple-element.56.shift, bf16[8,16,128]{2,1,0:T(8,128)(2,1)S(1)} %get-tuple-element.29.refs_0_, ...), custom_call_target="tpu_custom_call" | custom-call | flops 1000 | bytes 1000 | tf_op jit(solution)/shard_map/pallas_call | solution.py:147
  20.5 0.1 collective-permute-start.8
  20.6 0.0 copy-done.4
  20.6 0.1 add_divide_fusion
  20.7 0.0 collective-permute-done.10.same_far
  20.7 0.0 collective-permute-done.9.other
  20.7 0.9 %shard_map.66 = (bf16[3,768,256]{2,1,0:T(8,128)(2,1)S(1)}, bf16[3,768,256]{2,1,0:T(8,128)(2,1)S(1)}) custom-call(s32[2]{0:T(128)S(1)} %pad_add_fusion.pos, bf16[3,3,3,32,128]{4,3,2,1,0:T(8,128)(2,1)S(1)} %get-tuple-element.35.same, bf16[3,3,3,32,128]{4,3,2,1,0:T(8,128)(2,1)S(1)} %collective-permute-done.9.other, ...), custom_call_target="tpu_custom_call" | custom-call | flops 1000 | bytes 1000 | tf_op jit(solution)/shard_map/pallas_call | solution.py:147
  21.6 0.7 %collective-permute-done.8.sibling = bf16[2,8,96,128]{3,2,1,0:T(8,128)(2,1)S(1)} collective-permute-done((bf16[2,8,96,128]{3,2,1,0:T(8,128)(2,1)S(1)}, bf16[2,8,96,128]{3,2,1,0:T(8,128)(2,1)S(1)}, u32[]{:S(2)}, u32[]{:S(2)}) %collective-permute-start.8) | collective-permute-done | bytes 393248 | tf_op jit(solution)/shard_map/ppermute | solution.py:372
  22.3 0.1 broadcast_in_dim.20.blend
  22.4 0.0 copy-start.1
  22.4 3.8 %shard_map.67 = (f32[8,16,256]{2,1,0:T(8,128)S(1)}, bf16[8,16,256]{2,1,0:T(8,128)(2,1)S(1)}, bf16[8,16,256]{2,1,0:T(8,128)(2,1)S(1)}, bf16[8,16,256]{2,1,0:T(8,1...) custom-call(s32[2]{0:T(128)S(1)} %pad_add_fusion.pos, ...), custom_call_target="tpu_custom_call" | custom-call | flops 1000 | bytes 1000 | tf_op jit(solution)/shard_map/pallas_call | solution.py:147
  26.1 2.1 %collective-permute-start.13 = (bf16[2,8,16,256]{3,2,1,0:T(8,128)(2,1)S(1)}, bf16[2,8,16,256]{3,2,1,0:T(8,128)(2,1)S(1)}, u32[]{:S(2)}, u32[]{:S(2)}) collective-permute-start(bf16[2,8,16,256]{3,2,1,0:T(8,128)(2,1)S(1)} %get-tuple-element.44), channel_id=1, source_target_pairs={{0,4},{2,6},{4,0},{6,2},{8,12},{10,14},{12,8},{14,10},{1,5},{3,7},... | collective-permute-start | bytes 393224 | tf_op jit(solution)/shard_map/ppermute | solution.py:331
  28.2 1.0 %collective-permute-start.11 = (bf16[8,16,256]{2,1,0:T(8,128)(2,1)S(1)}, bf16[8,16,256]{2,1,0:T(8,128)(2,1)S(1)}, u32[]{:S(2)}, u32[]{:S(2)}) collective-permute-start(bf16[8,16,256]{2,1,0:T(8,128)(2,1)S(1)} %get-tuple-element.42), channel_id=1, source_target_pairs={{0,12},{2,14},{4,8},{6,10},{8,4},{10,6},{12,0},{14,2},{1,13},{3,15... | collective-permute-start | bytes 196616 | tf_op jit(solution)/shard_map/ppermute | solution.py:331
  29.2 0.5 %collective-permute-start.12 = (bf16[8,16,256]{2,1,0:T(8,128)(2,1)S(1)}, bf16[8,16,256]{2,1,0:T(8,128)(2,1)S(1)}, u32[]{:S(2)}, u32[]{:S(2)}) collective-permute-start(bf16[8,16,256]{2,1,0:T(8,128)(2,1)S(1)} %get-tuple-element.43), channel_id=1, source_target_pairs={{0,8},{2,10},{4,12},{6,14},{8,0},{10,2},{12,4},{14,6},{1,9},{3,11}... | collective-permute-start | bytes 196616 | tf_op jit(solution)/shard_map/ppermute | solution.py:331
  29.7 2.3 %collective-permute-done.13.came = bf16[2,8,16,256]{3,2,1,0:T(8,128)(2,1)S(1)} collective-permute-done((bf16[2,8,16,256]{3,2,1,0:T(8,128)(2,1)S(1)}, bf16[2,8,16,256]{3,2,1,0:T(8,128)(2,1)S(1)}, u32[]{:S(2)}, u32[]{:S(2)}) %collective-permute-start.13) | collective-permute-done | bytes 131104 | tf_op jit(solution)/shard_map/ppermute | solution.py:331
  32.0 0.6 %shard_map.68 = (bf16[8,16,256]{2,1,0:T(8,128)(2,1)S(1)}, bf16[8,16,256]{2,1,0:T(8,128)(2,1)S(1)}) custom-call(s32[2]{0:T(128)S(1)} %pad_add_fusion.pos, f32[2,8,16,256]{3,2,1,0:T(8,128)S(1)} %get-tuple-element.47.kept, bf16[2,8,16,256]{3,2,1,0:T(8,128)(2,1)S(1)} %collective-permute-done.13.came), custom_call_target="tpu_custom_call" | custom-call | flops 1000 | bytes 1000 | tf_op jit(solution)/shard_map/pallas_call | solution.py:147
  32.6 3.0 %collective-permute-start.15 = (bf16[8,16,256]{2,1,0:T(8,128)(2,1)S(1)}, bf16[8,16,256]{2,1,0:T(8,128)(2,1)S(1)}, u32[]{:S(2)}, u32[]{:S(2)}) collective-permute-start(bf16[8,16,256]{2,1,0:T(8,128)(2,1)S(1)} %get-tuple-element.49), channel_id=1, source_target_pairs={{0,10},{2,8},{4,14},{6,12},{8,2},{10,0},{12,6},{14,4},{1,11},{3,9}... | collective-permute-start | bytes 196616 | tf_op jit(solution)/shard_map/ppermute | solution.py:331
  35.6 0.0 collective-permute-start.16
  35.6 1.7 %collective-permute-start.14 = (bf16[8,16,256]{2,1,0:T(8,128)(2,1)S(1)}, bf16[8,16,256]{2,1,0:T(8,128)(2,1)S(1)}, u32[]{:S(2)}, u32[]{:S(2)}) collective-permute-start(bf16[8,16,256]{2,1,0:T(8,128)(2,1)S(1)} %get-tuple-element.46), channel_id=1, source_target_pairs={{0,4},{2,6},{4,0},{6,2},{8,12},{10,14},{12,8},{14,10},{1,5},{3,7},... | collective-permute-start | bytes 196616 | tf_op jit(solution)/shard_map/ppermute | solution.py:331
  37.4 0.0 collective-permute-done.11.refs_0_
  37.4 0.2 collective-permute-done.12.refs_1_
  37.6 1.8 %collective-permute-done.15.refs_3_ = bf16[8,16,256]{2,1,0:T(8,128)(2,1)S(1)} collective-permute-done((bf16[8,16,256]{2,1,0:T(8,128)(2,1)S(1)}, bf16[8,16,256]{2,1,0:T(8,128)(2,1)S(1)}, u32[]{:S(2)}, u32[]{:S(2)}) %collective-permute-start.15) | collective-permute-done | bytes 65568 | tf_op jit(solution)/shard_map/ppermute | solution.py:331
  39.4 0.7 %collective-permute-done.16.refs_4_ = bf16[8,16,256]{2,1,0:T(8,128)(2,1)S(1)} collective-permute-done((bf16[8,16,256]{2,1,0:T(8,128)(2,1)S(1)}, bf16[8,16,256]{2,1,0:T(8,128)(2,1)S(1)}, u32[]{:S(2)}, u32[]{:S(2)}) %collective-permute-start.16) | collective-permute-done | bytes 65568 | tf_op jit(solution)/shard_map/ppermute | solution.py:331
  40.1 0.0 collective-permute-done.14.refs_2_
  40.1 0.0 copy-done.1
  40.1 1.3 %shard_map.69 = bf16[2,8,16,256]{3,2,1,0:T(8,128)(2,1)} custom-call(s32[2]{0:T(128)S(1)} %pad_add_fusion.pos, f32[1,256]{1,0:T(1,128)S(1)} %bitcast.7, f32[8,16,256]{2,1,0:T(8,128)S(1)} %get-tuple-element.41.own, bf16[8,16,256]{2,1,0:T(8,128)(2,1)S(1)} %collective-permute-done.11.refs_0_, bf16[8,16,256]{2,1,0:T(8,128)(2,1)S(1)} %collective-permute-done.12.refs_1_, ...), custom_call_target="tpu_custom_call" | custom-call | flops 1000 | bytes 1000 | tf_op jit(solution)/shard_map/pallas_call | solution.py:147
  (2 shorter events, 0.0 us)
Async XLA Ops:
  0.0 4.0 %copy-start = (bf16[2,8,16,256]{3,2,1,0:T(8,128)(2,1)S(1)}, bf16[2,8,16,256]{3,2,1,0:T(8,128)(2,1)}, u32[]{:S(2)}) copy-start(bf16[2,8,16,256]{3,2,1,0:T(8,128)(2,1)} %latent) | copy-start | bytes 393220
  0.0 9.9 %copy-start.2 = (f32[256]{0:T(256)S(1)}, f32[256]{0:T(256)}, u32[]{:S(2)}) copy-start(f32[256]{0:T(256)} %param.7) | copy-start | bytes 3076
  0.0 10.0 %copy-start.3 = (f32[256]{0:T(256)S(1)}, f32[256]{0:T(256)}, u32[]{:S(2)}) copy-start(f32[256]{0:T(256)} %param.8) | copy-start | bytes 3076
  0.0 20.6 %copy-start.4 = (s32[4]{0:T(128)S(1)}, s32[4]{0:T(128)}, u32[]{:S(2)}) copy-start(s32[4]{0:T(128)} %param.11) | copy-start | bytes 52
  1.4 14.0 %collective-permute-start.2 = (bf16[3,3,3,32,128]{4,3,2,1,0:T(8,128)(2,1)S(1)}, bf16[3,3,3,32,128]{4,3,2,1,0:T(8,128)(2,1)S(1)}, u32[]{:S(2)}, u32[]{:S(2)}) collective-permute-start(bf16[3,3,3,32,128]{4,3,2,1,0:T(8,128)(2,1)S(1)} %get-tuple-element.32), channel_id=1, source_target_pairs={{0,3},{1,2},{2,1},{3,0},{4,7},{5,6},{6,5},{7,4},{8,11},{9,10},{10,... | collective-permute-start | bytes 663560 | tf_op jit(solution)/shard_map/ppermute | solution.py:336
  4.8 6.0 %collective-permute-start.3 = (bf16[8,16,128]{2,1,0:T(8,128)(2,1)S(1)}, bf16[8,16,128]{2,1,0:T(8,128)(2,1)S(1)}, u32[]{:S(2)}, u32[]{:S(2)}) collective-permute-start(bf16[8,16,128]{2,1,0:T(8,128)(2,1)S(1)} %get-tuple-element.33), channel_id=1, source_target_pairs={{0,12},{2,14},{4,8},{6,10},{8,4},{10,6},{12,0},{14,2},{1,13},{3,15... | collective-permute-start | bytes 98312 | tf_op jit(solution)/shard_map/ppermute | solution.py:331
  8.5 12.2 %collective-permute-start.10 = (bf16[3,3,3,32,128]{4,3,2,1,0:T(8,128)(2,1)S(1)}, bf16[3,3,3,32,128]{4,3,2,1,0:T(8,128)(2,1)S(1)}, u32[]{:S(2)}, u32[]{:S(2)}) collective-permute-start(bf16[3,3,3,32,128]{4,3,2,1,0:T(8,128)(2,1)S(1)} %get-tuple-element.37), channel_id=1, source_target_pairs={{0,2},{2,0},{4,6},{6,4},{8,10},{10,8},{12,14},{14,12},{1,3},{3,1},... | collective-permute-start | bytes 663560 | tf_op jit(solution)/shard_map/ppermute | solution.py:331
  9.1 4.3 %collective-permute-start = (bf16[8,16,128]{2,1,0:T(8,128)(2,1)S(1)}, bf16[8,16,128]{2,1,0:T(8,128)(2,1)S(1)}, u32[]{:S(2)}, u32[]{:S(2)}) collective-permute-start(bf16[8,16,128]{2,1,0:T(8,128)(2,1)S(1)} %get-tuple-element.30), channel_id=1, source_target_pairs={{0,4},{2,6},{4,0},{6,2},{8,12},{10,14},{12,8},{14,10},{1,5},{3,7},... | collective-permute-start | bytes 98312 | tf_op jit(solution)/shard_map/ppermute | solution.py:331
  9.1 5.7 %collective-permute-start.1 = (bf16[8,16,128]{2,1,0:T(8,128)(2,1)S(1)}, bf16[8,16,128]{2,1,0:T(8,128)(2,1)S(1)}, u32[]{:S(2)}, u32[]{:S(2)}) collective-permute-start(bf16[8,16,128]{2,1,0:T(8,128)(2,1)S(1)} %get-tuple-element.31), channel_id=1, source_target_pairs={{0,8},{2,10},{4,12},{6,14},{8,0},{10,2},{12,4},{14,6},{1,9},{3,11}... | collective-permute-start | bytes 98312 | tf_op jit(solution)/shard_map/ppermute | solution.py:331
  10.8 6.6 %collective-permute-start.4 = (bf16[8,16,128]{2,1,0:T(8,128)(2,1)S(1)}, bf16[8,16,128]{2,1,0:T(8,128)(2,1)S(1)}, u32[]{:S(2)}, u32[]{:S(2)}) collective-permute-start(bf16[8,16,128]{2,1,0:T(8,128)(2,1)S(1)} %get-tuple-element.29.refs_0_), channel_id=1, source_target_pairs={{0,2},{2,0},{4,6},{6,4},{8,10},{10,8},{12,14},{14,12},{1,3},{3,1},... | collective-permute-start | bytes 98312 | tf_op jit(solution)/shard_map/ppermute | solution.py:331
  13.3 4.8 %collective-permute-start.5 = (bf16[8,16,128]{2,1,0:T(8,128)(2,1)S(1)}, bf16[8,16,128]{2,1,0:T(8,128)(2,1)S(1)}, u32[]{:S(2)}, u32[]{:S(2)}) collective-permute-start(bf16[8,16,128]{2,1,0:T(8,128)(2,1)S(1)} %collective-permute-done.refs_1_), channel_id=1, source_target_pairs={{0,2},{2,0},{4,6},{6,4},{8,10},{10,8},{12,14},{14,12},{1,3},{3,1},... | collective-permute-start | bytes 98312 | tf_op jit(solution)/shard_map/ppermute | solution.py:331
  14.8 3.9 %collective-permute-start.6 = (bf16[8,16,128]{2,1,0:T(8,128)(2,1)S(1)}, bf16[8,16,128]{2,1,0:T(8,128)(2,1)S(1)}, u32[]{:S(2)}, u32[]{:S(2)}) collective-permute-start(bf16[8,16,128]{2,1,0:T(8,128)(2,1)S(1)} %collective-permute-done.1.refs_2_), channel_id=1, source_target_pairs={{0,2},{2,0},{4,6},{6,4},{8,10},{10,8},{12,14},{14,12},{1,3},{3,1},... | collective-permute-start | bytes 98312 | tf_op jit(solution)/shard_map/ppermute | solution.py:331
  15.4 3.9 %collective-permute-start.7 = (bf16[8,16,128]{2,1,0:T(8,128)(2,1)S(1)}, bf16[8,16,128]{2,1,0:T(8,128)(2,1)S(1)}, u32[]{:S(2)}, u32[]{:S(2)}) collective-permute-start(bf16[8,16,128]{2,1,0:T(8,128)(2,1)S(1)} %collective-permute-done.3.refs_3_), channel_id=1, source_target_pairs={{0,2},{2,0},{4,6},{6,4},{8,10},{10,8},{12,14},{14,12},{1,3},{3,1},... | collective-permute-start | bytes 98312 | tf_op jit(solution)/shard_map/ppermute | solution.py:331
  17.4 3.3 %collective-permute-start.9 = (bf16[3,3,3,32,128]{4,3,2,1,0:T(8,128)(2,1)S(1)}, bf16[3,3,3,32,128]{4,3,2,1,0:T(8,128)(2,1)S(1)}, u32[]{:S(2)}, u32[]{:S(2)}) collective-permute-start(bf16[3,3,3,32,128]{4,3,2,1,0:T(8,128)(2,1)S(1)} %get-tuple-element.36), channel_id=1, source_target_pairs={{0,1},{1,0},{2,3},{3,2},{4,5},{5,4},{6,7},{7,6},{8,9},{9,8},{10,11... | collective-permute-start | bytes 663560 | tf_op jit(solution)/shard_map/ppermute | solution.py:336
  20.5 1.8 %collective-permute-start.8 = (bf16[2,8,96,128]{3,2,1,0:T(8,128)(2,1)S(1)}, bf16[2,8,96,128]{3,2,1,0:T(8,128)(2,1)S(1)}, u32[]{:S(2)}, u32[]{:S(2)}) collective-permute-start(bf16[2,8,96,128]{3,2,1,0:T(8,128)(2,1)S(1)} %shard_map.65.mine), channel_id=1, source_target_pairs={{0,1},{1,0},{2,3},{3,2},{4,5},{5,4},{6,7},{7,6},{8,9},{9,8},{10,11... | collective-permute-start | bytes 1179656 | tf_op jit(solution)/shard_map/ppermute | solution.py:372
  22.4 17.7 %copy-start.1 = (f32[256]{0:T(256)S(1)}, f32[256]{0:T(256)}, u32[]{:S(2)}) copy-start(f32[256]{0:T(256)} %param.10) | copy-start | bytes 3076
  26.1 5.9 %collective-permute-start.13 = (bf16[2,8,16,256]{3,2,1,0:T(8,128)(2,1)S(1)}, bf16[2,8,16,256]{3,2,1,0:T(8,128)(2,1)S(1)}, u32[]{:S(2)}, u32[]{:S(2)}) collective-permute-start(bf16[2,8,16,256]{3,2,1,0:T(8,128)(2,1)S(1)} %get-tuple-element.44), channel_id=1, source_target_pairs={{0,4},{2,6},{4,0},{6,2},{8,12},{10,14},{12,8},{14,10},{1,5},{3,7},... | collective-permute-start | bytes 393224 | tf_op jit(solution)/shard_map/ppermute | solution.py:331
  28.2 9.2 %collective-permute-start.11 = (bf16[8,16,256]{2,1,0:T(8,128)(2,1)S(1)}, bf16[8,16,256]{2,1,0:T(8,128)(2,1)S(1)}, u32[]{:S(2)}, u32[]{:S(2)}) collective-permute-start(bf16[8,16,256]{2,1,0:T(8,128)(2,1)S(1)} %get-tuple-element.42), channel_id=1, source_target_pairs={{0,12},{2,14},{4,8},{6,10},{8,4},{10,6},{12,0},{14,2},{1,13},{3,15... | collective-permute-start | bytes 196616 | tf_op jit(solution)/shard_map/ppermute | solution.py:331
  29.2 8.4 %collective-permute-start.12 = (bf16[8,16,256]{2,1,0:T(8,128)(2,1)S(1)}, bf16[8,16,256]{2,1,0:T(8,128)(2,1)S(1)}, u32[]{:S(2)}, u32[]{:S(2)}) collective-permute-start(bf16[8,16,256]{2,1,0:T(8,128)(2,1)S(1)} %get-tuple-element.43), channel_id=1, source_target_pairs={{0,8},{2,10},{4,12},{6,14},{8,0},{10,2},{12,4},{14,6},{1,9},{3,11}... | collective-permute-start | bytes 196616 | tf_op jit(solution)/shard_map/ppermute | solution.py:331
  32.6 6.8 %collective-permute-start.15 = (bf16[8,16,256]{2,1,0:T(8,128)(2,1)S(1)}, bf16[8,16,256]{2,1,0:T(8,128)(2,1)S(1)}, u32[]{:S(2)}, u32[]{:S(2)}) collective-permute-start(bf16[8,16,256]{2,1,0:T(8,128)(2,1)S(1)} %get-tuple-element.49), channel_id=1, source_target_pairs={{0,10},{2,8},{4,14},{6,12},{8,2},{10,0},{12,6},{14,4},{1,11},{3,9}... | collective-permute-start | bytes 196616 | tf_op jit(solution)/shard_map/ppermute | solution.py:331
  35.6 4.4 %collective-permute-start.16 = (bf16[8,16,256]{2,1,0:T(8,128)(2,1)S(1)}, bf16[8,16,256]{2,1,0:T(8,128)(2,1)S(1)}, u32[]{:S(2)}, u32[]{:S(2)}) collective-permute-start(bf16[8,16,256]{2,1,0:T(8,128)(2,1)S(1)} %get-tuple-element.50), channel_id=1, source_target_pairs={{0,2},{2,0},{4,6},{6,4},{8,10},{10,8},{12,14},{14,12},{1,3},{3,1},... | collective-permute-start | bytes 196616 | tf_op jit(solution)/shard_map/ppermute | solution.py:331
  35.6 4.4 %collective-permute-start.14 = (bf16[8,16,256]{2,1,0:T(8,128)(2,1)S(1)}, bf16[8,16,256]{2,1,0:T(8,128)(2,1)S(1)}, u32[]{:S(2)}, u32[]{:S(2)}) collective-permute-start(bf16[8,16,256]{2,1,0:T(8,128)(2,1)S(1)} %get-tuple-element.46), channel_id=1, source_target_pairs={{0,4},{2,6},{4,0},{6,2},{8,12},{10,14},{12,8},{14,10},{1,5},{3,7},... | collective-permute-start | bytes 196616 | tf_op jit(solution)/shard_map/ppermute | solution.py:331

commit v5 on v4

--- a/solution.py
+++ b/solution.py
@@ -257,7 +257,7 @@
 
 
 def conv_body(pos, mine, sibling, diag, lower, blend, *refs):
-    own, sends, kept, passed, (stacked, summed, blocks) = refs[0], refs[1:4], refs[4], refs[5], refs[6:]
+    sends, kept, passed, (stacked, summed, blocks) = refs[:4], refs[4], refs[5], refs[6:]
     z, x = pos[0], pos[1]
     col = lax.broadcasted_iota(jnp.int32, (24, 128), 0)
     for p in range(2):
@@ -296,26 +296,25 @@
         summed[:, 64:72, :] = total[:, 88:96]
         for t in range(4):
             blocks[p, t] = summed[:, 4 + 16 * t : 20 + 16 * t, :]
-    own[...] = blocks[x, z]
-    for k in range(1, 4):
-        sends[k - 1][...] = blocks[x, z ^ k].astype(jnp.bfloat16)
+    for k in range(4):
+        sends[k][...] = blocks[1 - x, z ^ k].astype(jnp.bfloat16)
     for i, k in enumerate((0, 2)):
-        kept[i] = blocks[1 - x, z ^ k]
-        passed[i] = blocks[1 - x, z ^ k ^ 1].astype(jnp.bfloat16)
+        kept[i] = blocks[x, z ^ k]
+        passed[i] = blocks[x, z ^ k ^ 1].astype(jnp.bfloat16)
 
 
 def add_body(pos, kept, came, *sums):
     for i in range(2):
-        sums[i][...] = (kept[i] + came[i].astype(jnp.float32)).astype(jnp.bfloat16)
-
-
-def join_body(pos, bias, own, *refs):
-    same, far, out = refs[:3], refs[3:5], refs[5]
+        sums[i][...] = (kept[i] + came[i].astype(jnp.float32)).astype(sums[i].dtype)
+
+
+def join_body(pos, bias, own, same, *refs):
+    far, out = refs[:4], refs[4]
     x = pos[1]
-    near_sum = own[...]
-    for part in same:
-        near_sum = near_sum + part[...].astype(jnp.float32)
-    far_sum = far[0][...].astype(jnp.float32) + far[1][...].astype(jnp.float32)
+    near_sum = own[...] + same[...].astype(jnp.float32)
+    far_sum = far[0][...].astype(jnp.float32)
+    for part in far[1:]:
+        far_sum = far_sum + part[...].astype(jnp.float32)
     low = jnp.where(x == 0, near_sum, far_sum)
     high = jnp.where(x == 0, far_sum, near_sum)
     for f in range(2):
@@ -374,11 +373,9 @@
     offsets = jnp.arange(2 * RIM, dtype=jnp.int32)
     ramps = ramp_weight(blend_profile[:3, None], offsets[None, :], RIM)
     blend = jnp.broadcast_to(ramps[:, :, None], (3, 2 * RIM, 256))
-    own, *sends, kept, leaving = call(
+    *sends, kept, leaving = call(
         conv_body,
-        [jax.ShapeDtypeStruct((8, 16, 256), f32)]
-        + [wide] * 3
-        + [jax.ShapeDtypeStruct((2, 8, 16, 256), t) for t in (f32, bf16)],
+        [wide] * 4 + [jax.ShapeDtypeStruct((2, 8, 16, 256), t) for t in (f32, bf16)],
         [
             pltpu.VMEM((2, 960, 768), bf16),
             pltpu.VMEM((8, 72, 256), f32),
@@ -387,11 +384,11 @@
     )(pos, acts, sibling, diag, lower, blend)
     came = exchanged(leaving, 1, 0)
     came, sends[0] = lax.optimization_barrier((came, sends[0]))
-    sums = call(add_body, [wide] * 2)(pos, kept, came)
-    far_sums = [exchanged(sums[1], 2, 1), exchanged(sums[0], 0, 1)]
-    near_sums = [exchanged(sends[k - 1], k, 0) for k in (3, 2, 1)]
+    own, leaving = call(add_body, [jax.ShapeDtypeStruct(wide.shape, f32), wide])(pos, kept, came)
+    same = exchanged(leaving, 2, 0)
+    far = [exchanged(sends[k], k, 1) for k in (3, 2, 0, 1)]
     return call(join_body, jax.ShapeDtypeStruct(latent.shape, bf16))(
-        pos, conv_bias[None], own, *near_sums, *far_sums
+        pos, conv_bias[None], own, same, *far
     )
 
 

time: 41.5 us -> 41.4 us (level)
  starting transfers between devices: 20.1 us -> 20.9 us
  waiting for transfers between devices: 10.7 us -> 9.94 us
    ppermute x14, waiting for transfers between devices: 10 us -> 9.22 us  [exchanged(): return lax.ppermute(block, ('tile', 'tm'), route)]
    ppermute x14, starting transfers between devices: 17.5 us -> 18.3 us  [exchanged(): return lax.ppermute(block, ('tile', 'tm'), route)]
  transfers between devices with their start and end apart: 17 -> 17, of which waited for: 11 -> 10; matrix products, arithmetic and copies ran while one was open for 1% -> 1% of each run, Pallas kernels for 8% -> 8%
where the time goes in v5:
time: 41.4 us; the launch traced here: 41.3 us
  starting transfers between devices  20.9 us (50%)
  waiting for transfers between devices  9.94 us (24%)
  Pallas kernels  8.52 us (21%)
  local copies, waits for them, and re-layouts  1.61 us (4%)
    ppermute x14, starting transfers between devices, exchanged(): return lax.ppermute(block, ('tile', 'tm'), route)  18.3 us
    ppermute x14, waiting for transfers between devices, exchanged(): return lax.ppermute(block, ('tile', 'tm'), route)  9.22 us
    pallas_call x6, Pallas kernels, run(): pl.pallas_call(body, out_shape=outs, in_specs=specs, out_specs=jax.tree.m...  8.52 us
    ppermute x2, starting transfers between devices, across(): return lax.ppermute(block, ('tm', 'ch'), route)  2.51 us
    dynamic_slice x1, local copies, waits for them, and re-layouts, quarter(): return lax.dynamic_slice_in_dim(kernel, start, 128, axis=4)  1.37 us
  transfers between devices with their start and end apart: 17, of which 10 were waited for; matrix products, arithmetic and copies ran while one was open for 1% of the time, Pallas kernels for 8%

profile of v5, /device:TPU:0, one launch (start us, length us, event | category | flops | bytes accessed | tf_op | source)
XLA Modules:
  0.0 41.3 jit_solution(8130487682246309207)
XLA Ops:
  0.0 0.0 copy-start
  0.0 0.0 copy-start.2
  0.0 0.0 copy-start.3
  0.0 0.0 copy-start.4
  0.0 1.4 %constant_dynamic-slice_fusion = (bf16[3,3,3,32,128]{4,3,2,1,0:T(8,128)(2,1)S(1)}, bf16[3,3,3,32,128]{4,3,2,1,0:T(8,128)(2,1)S(1)}, bf16[3,3,3,32,128]{4,3,2,1,0:T(8,128)(2,1)S(1)}, bf16[3,3,3,32,128]{4,3,2,1,0:T(8,128)(2,1)S(1)}) fusion(bf16[3,3,3,32,512]{4,3,2,1,0:T(8,128)(2,1)} %param.9, s32[]{:T(128)S(6)} %select_n.20, s32[]{:T(128)S(6)} %select_n.18, ...), kind=kLoop, calls=%fused_computation.1 | loop fusion | bytes 1769488 | tf_op jit(solution)/shard_map/dynamic_slice | solution.py:347
  1.4 2.5 %collective-permute-start.2 = (bf16[3,3,3,32,128]{4,3,2,1,0:T(8,128)(2,1)S(1)}, bf16[3,3,3,32,128]{4,3,2,1,0:T(8,128)(2,1)S(1)}, u32[]{:S(2)}, u32[]{:S(2)}) collective-permute-start(bf16[3,3,3,32,128]{4,3,2,1,0:T(8,128)(2,1)S(1)} %get-tuple-element.32), channel_id=1, source_target_pairs={{0,3},{1,2},{2,1},{3,0},{4,7},{5,6},{6,5},{7,4},{8,11},{9,10},{10,... | collective-permute-start | bytes 663560 | tf_op jit(solution)/shard_map/ppermute | solution.py:335
  3.9 0.1 pad_add_fusion.pos
  4.0 0.0 copy-done
  4.0 0.9 %shard_map.64 = (bf16[8,16,128]{2,1,0:T(8,128)(2,1)S(1)}, bf16[8,16,128]{2,1,0:T(8,128)(2,1)S(1)}, bf16[8,16,128]{2,1,0:T(8,128)(2,1)S(1)}, bf16[8,16,128]{2,1,0:T(8,128)(2,1)S(1)}) custom-call(s32[2]{0:T(128)S(1)} %pad_add_fusion.pos, bf16[2,8,16,256]{3,2,1,0:T(8,128)(2,1)S(1)} %copy-done), custom_call_target="tpu_custom_call" | custom-call | flops 1000 | bytes 1000 | tf_op jit(solution)/shard_map/pallas_call | solution.py:147
  4.8 3.6 %collective-permute-start.3 = (bf16[8,16,128]{2,1,0:T(8,128)(2,1)S(1)}, bf16[8,16,128]{2,1,0:T(8,128)(2,1)S(1)}, u32[]{:S(2)}, u32[]{:S(2)}) collective-permute-start(bf16[8,16,128]{2,1,0:T(8,128)(2,1)S(1)} %get-tuple-element.33), channel_id=1, source_target_pairs={{0,12},{2,14},{4,8},{6,10},{8,4},{10,6},{12,0},{14,2},{1,13},{3,15... | collective-permute-start | bytes 98312 | tf_op jit(solution)/shard_map/ppermute | solution.py:330
  8.5 0.6 %collective-permute-start.10 = (bf16[3,3,3,32,128]{4,3,2,1,0:T(8,128)(2,1)S(1)}, bf16[3,3,3,32,128]{4,3,2,1,0:T(8,128)(2,1)S(1)}, u32[]{:S(2)}, u32[]{:S(2)}) collective-permute-start(bf16[3,3,3,32,128]{4,3,2,1,0:T(8,128)(2,1)S(1)} %get-tuple-element.37), channel_id=1, source_target_pairs={{0,2},{2,0},{4,6},{6,4},{8,10},{10,8},{12,14},{14,12},{1,3},{3,1},... | collective-permute-start | bytes 663560 | tf_op jit(solution)/shard_map/ppermute | solution.py:330
  9.1 0.0 collective-permute-start
  9.1 0.8 %collective-permute-start.1 = (bf16[8,16,128]{2,1,0:T(8,128)(2,1)S(1)}, bf16[8,16,128]{2,1,0:T(8,128)(2,1)S(1)}, u32[]{:S(2)}, u32[]{:S(2)}) collective-permute-start(bf16[8,16,128]{2,1,0:T(8,128)(2,1)S(1)} %get-tuple-element.31), channel_id=1, source_target_pairs={{0,8},{2,10},{4,12},{6,14},{8,0},{10,2},{12,4},{14,6},{1,9},{3,11}... | collective-permute-start | bytes 98312 | tf_op jit(solution)/shard_map/ppermute | solution.py:330
  9.9 0.0 copy-done.2
  9.9 0.1 dynamic_slice.18
  10.0 0.0 copy-done.3
  10.0 0.1 dynamic_slice.19
  10.0 0.8 %collective-permute-done.3.refs_3_ = bf16[8,16,128]{2,1,0:T(8,128)(2,1)S(1)} collective-permute-done((bf16[8,16,128]{2,1,0:T(8,128)(2,1)S(1)}, bf16[8,16,128]{2,1,0:T(8,128)(2,1)S(1)}, u32[]{:S(2)}, u32[]{:S(2)}) %collective-permute-start.3) | collective-permute-done | bytes 32800 | tf_op jit(solution)/shard_map/ppermute | solution.py:330
  10.8 0.7 %collective-permute-start.4 = (bf16[8,16,128]{2,1,0:T(8,128)(2,1)S(1)}, bf16[8,16,128]{2,1,0:T(8,128)(2,1)S(1)}, u32[]{:S(2)}, u32[]{:S(2)}) collective-permute-start(bf16[8,16,128]{2,1,0:T(8,128)(2,1)S(1)} %get-tuple-element.29.refs_0_), channel_id=1, source_target_pairs={{0,2},{2,0},{4,6},{6,4},{8,10},{10,8},{12,14},{14,12},{1,3},{3,1},... | collective-permute-start | bytes 98312 | tf_op jit(solution)/shard_map/ppermute | solution.py:330
  11.5 1.8 %collective-permute-done.refs_1_ = bf16[8,16,128]{2,1,0:T(8,128)(2,1)S(1)} collective-permute-done((bf16[8,16,128]{2,1,0:T(8,128)(2,1)S(1)}, bf16[8,16,128]{2,1,0:T(8,128)(2,1)S(1)}, u32[]{:S(2)}, u32[]{:S(2)}) %collective-permute-start) | collective-permute-done | bytes 32800 | tf_op jit(solution)/shard_map/ppermute | solution.py:330
  13.3 1.4 %collective-permute-start.5 = (bf16[8,16,128]{2,1,0:T(8,128)(2,1)S(1)}, bf16[8,16,128]{2,1,0:T(8,128)(2,1)S(1)}, u32[]{:S(2)}, u32[]{:S(2)}) collective-permute-start(bf16[8,16,128]{2,1,0:T(8,128)(2,1)S(1)} %collective-permute-done.refs_1_), channel_id=1, source_target_pairs={{0,2},{2,0},{4,6},{6,4},{8,10},{10,8},{12,14},{14,12},{1,3},{3,1},... | collective-permute-start | bytes 98312 | tf_op jit(solution)/shard_map/ppermute | solution.py:330
  14.8 0.0 collective-permute-done.1.refs_2_
  14.8 0.6 %collective-permute-start.6 = (bf16[8,16,128]{2,1,0:T(8,128)(2,1)S(1)}, bf16[8,16,128]{2,1,0:T(8,128)(2,1)S(1)}, u32[]{:S(2)}, u32[]{:S(2)}) collective-permute-start(bf16[8,16,128]{2,1,0:T(8,128)(2,1)S(1)} %collective-permute-done.1.refs_2_), channel_id=1, source_target_pairs={{0,2},{2,0},{4,6},{6,4},{8,10},{10,8},{12,14},{14,12},{1,3},{3,1},... | collective-permute-start | bytes 98312 | tf_op jit(solution)/shard_map/ppermute | solution.py:330
  15.4 0.0 collective-permute-done.2.other_far
  15.4 1.4 %collective-permute-start.7 = (bf16[8,16,128]{2,1,0:T(8,128)(2,1)S(1)}, bf16[8,16,128]{2,1,0:T(8,128)(2,1)S(1)}, u32[]{:S(2)}, u32[]{:S(2)}) collective-permute-start(bf16[8,16,128]{2,1,0:T(8,128)(2,1)S(1)} %collective-permute-done.3.refs_3_), channel_id=1, source_target_pairs={{0,2},{2,0},{4,6},{6,4},{8,10},{10,8},{12,14},{14,12},{1,3},{3,1},... | collective-permute-start | bytes 98312 | tf_op jit(solution)/shard_map/ppermute | solution.py:330
  16.8 0.1 maximum_bitcast_fusion
  16.9 0.5 %collective-permute-done.4.refs_4_ = bf16[8,16,128]{2,1,0:T(8,128)(2,1)S(1)} collective-permute-done((bf16[8,16,128]{2,1,0:T(8,128)(2,1)S(1)}, bf16[8,16,128]{2,1,0:T(8,128)(2,1)S(1)}, u32[]{:S(2)}, u32[]{:S(2)}) %collective-permute-start.4) | collective-permute-done | bytes 32800 | tf_op jit(solution)/shard_map/ppermute | solution.py:330
  17.4 0.0 collective-permute-start.9
  17.4 0.7 %collective-permute-done.5.refs_5_ = bf16[8,16,128]{2,1,0:T(8,128)(2,1)S(1)} collective-permute-done((bf16[8,16,128]{2,1,0:T(8,128)(2,1)S(1)}, bf16[8,16,128]{2,1,0:T(8,128)(2,1)S(1)}, u32[]{:S(2)}, u32[]{:S(2)}) %collective-permute-start.5) | collective-permute-done | bytes 32800 | tf_op jit(solution)/shard_map/ppermute | solution.py:330
  18.1 0.6 %collective-permute-done.6.refs_6_ = bf16[8,16,128]{2,1,0:T(8,128)(2,1)S(1)} collective-permute-done((bf16[8,16,128]{2,1,0:T(8,128)(2,1)S(1)}, bf16[8,16,128]{2,1,0:T(8,128)(2,1)S(1)}, u32[]{:S(2)}, u32[]{:S(2)}) %collective-permute-start.6) | collective-permute-done | bytes 32800 | tf_op jit(solution)/shard_map/ppermute | solution.py:330
  18.7 0.6 %collective-permute-done.7.refs_7_ = bf16[8,16,128]{2,1,0:T(8,128)(2,1)S(1)} collective-permute-done((bf16[8,16,128]{2,1,0:T(8,128)(2,1)S(1)}, bf16[8,16,128]{2,1,0:T(8,128)(2,1)S(1)}, u32[]{:S(2)}, u32[]{:S(2)}) %collective-permute-start.7) | collective-permute-done | bytes 32800 | tf_op jit(solution)/shard_map/ppermute | solution.py:330
  19.3 1.2 %shard_map.65.mine = bf16[2,8,96,128]{3,2,1,0:T(8,128)(2,1)S(1)} custom-call(s32[2]{0:T(128)S(1)} %pad_add_fusion.pos, f32[1,128]{1,0:T(1,128)S(1)} %get-tuple-element.55.gain, f32[1,128]{1,0:T(1,128)S(1)} %get-tuple-element.56.shift, bf16[8,16,128]{2,1,0:T(8,128)(2,1)S(1)} %get-tuple-element.29.refs_0_, ...), custom_call_target="tpu_custom_call" | custom-call | flops 1000 | bytes 1000 | tf_op jit(solution)/shard_map/pallas_call | solution.py:147
  20.5 0.1 collective-permute-start.8
  20.6 0.0 copy-done.4
  20.6 0.1 add_divide_fusion
  20.7 0.0 collective-permute-done.10.same_far
  20.7 0.0 collective-permute-done.9.other
  20.7 0.9 %shard_map.66 = (bf16[3,768,256]{2,1,0:T(8,128)(2,1)S(1)}, bf16[3,768,256]{2,1,0:T(8,128)(2,1)S(1)}) custom-call(s32[2]{0:T(128)S(1)} %pad_add_fusion.pos, bf16[3,3,3,32,128]{4,3,2,1,0:T(8,128)(2,1)S(1)} %get-tuple-element.35.same, bf16[3,3,3,32,128]{4,3,2,1,0:T(8,128)(2,1)S(1)} %collective-permute-done.9.other, ...), custom_call_target="tpu_custom_call" | custom-call | flops 1000 | bytes 1000 | tf_op jit(solution)/shard_map/pallas_call | solution.py:147
  21.6 0.7 %collective-permute-done.8.sibling = bf16[2,8,96,128]{3,2,1,0:T(8,128)(2,1)S(1)} collective-permute-done((bf16[2,8,96,128]{3,2,1,0:T(8,128)(2,1)S(1)}, bf16[2,8,96,128]{3,2,1,0:T(8,128)(2,1)S(1)}, u32[]{:S(2)}, u32[]{:S(2)}) %collective-permute-start.8) | collective-permute-done | bytes 393248 | tf_op jit(solution)/shard_map/ppermute | solution.py:371
  22.3 0.1 broadcast_in_dim.20.blend
  22.4 0.0 copy-start.1
  22.4 3.8 %shard_map.67 = (bf16[8,16,256]{2,1,0:T(8,128)(2,1)S(1)}, bf16[8,16,256]{2,1,0:T(8,128)(2,1)S(1)}, bf16[8,16,256]{2,1,0:T(8,128)(2,1)S(1)}, bf16[8,16,256]{2,1,0...) custom-call(s32[2]{0:T(128)S(1)} %pad_add_fusion.pos, ...), custom_call_target="tpu_custom_call" | custom-call | flops 1000 | bytes 1000 | tf_op jit(solution)/shard_map/pallas_call | solution.py:147
  26.1 2.1 %collective-permute-start.11 = (bf16[2,8,16,256]{3,2,1,0:T(8,128)(2,1)S(1)}, bf16[2,8,16,256]{3,2,1,0:T(8,128)(2,1)S(1)}, u32[]{:S(2)}, u32[]{:S(2)}) collective-permute-start(bf16[2,8,16,256]{3,2,1,0:T(8,128)(2,1)S(1)} %get-tuple-element.42), channel_id=1, source_target_pairs={{0,4},{2,6},{4,0},{6,2},{8,12},{10,14},{12,8},{14,10},{1,5},{3,7},... | collective-permute-start | bytes 393224 | tf_op jit(solution)/shard_map/ppermute | solution.py:330
  28.2 1.9 %collective-permute-start.13 = (bf16[8,16,256]{2,1,0:T(8,128)(2,1)S(1)}, bf16[8,16,256]{2,1,0:T(8,128)(2,1)S(1)}, u32[]{:S(2)}, u32[]{:S(2)}) collective-permute-start(bf16[8,16,256]{2,1,0:T(8,128)(2,1)S(1)} %get-tuple-element.47), channel_id=1, source_target_pairs={{0,14},{2,12},{4,10},{6,8},{8,6},{10,4},{12,2},{14,0},{1,15},{3,13... | collective-permute-start | bytes 196616 | tf_op jit(solution)/shard_map/ppermute | solution.py:330
  30.1 0.5 %collective-permute-start.14 = (bf16[8,16,256]{2,1,0:T(8,128)(2,1)S(1)}, bf16[8,16,256]{2,1,0:T(8,128)(2,1)S(1)}, u32[]{:S(2)}, u32[]{:S(2)}) collective-permute-start(bf16[8,16,256]{2,1,0:T(8,128)(2,1)S(1)} %get-tuple-element.48), channel_id=1, source_target_pairs={{0,10},{2,8},{4,14},{6,12},{8,2},{10,0},{12,6},{14,4},{1,11},{3,9}... | collective-permute-start | bytes 196616 | tf_op jit(solution)/shard_map/ppermute | solution.py:330
  30.6 2.9 %collective-permute-start.16 = (bf16[8,16,256]{2,1,0:T(8,128)(2,1)S(1)}, bf16[8,16,256]{2,1,0:T(8,128)(2,1)S(1)}, u32[]{:S(2)}, u32[]{:S(2)}) collective-permute-start(bf16[8,16,256]{2,1,0:T(8,128)(2,1)S(1)} %get-tuple-element.50), channel_id=1, source_target_pairs={{0,6},{2,4},{4,2},{6,0},{8,14},{10,12},{12,10},{14,8},{1,7},{3,5},... | collective-permute-start | bytes 196616 | tf_op jit(solution)/shard_map/ppermute | solution.py:330
  33.5 0.0 collective-permute-done.11.came
  33.5 0.6 %shard_map.68 = (f32[8,16,256]{2,1,0:T(8,128)S(1)}, bf16[8,16,256]{2,1,0:T(8,128)(2,1)S(1)}) custom-call(s32[2]{0:T(128)S(1)} %pad_add_fusion.pos, f32[2,8,16,256]{3,2,1,0:T(8,128)S(1)} %get-tuple-element.41.kept, bf16[2,8,16,256]{3,2,1,0:T(8,128)(2,1)S(1)} %collective-permute-done.11.came), custom_call_target="tpu_custom_call" | custom-call | flops 1000 | bytes 1000 | tf_op jit(solution)/shard_map/pallas_call | solution.py:147
  34.1 1.2 %collective-permute-start.12 = (bf16[8,16,256]{2,1,0:T(8,128)(2,1)S(1)}, bf16[8,16,256]{2,1,0:T(8,128)(2,1)S(1)}, u32[]{:S(2)}, u32[]{:S(2)}) collective-permute-start(bf16[8,16,256]{2,1,0:T(8,128)(2,1)S(1)} %get-tuple-element.46), channel_id=1, source_target_pairs={{0,8},{2,10},{4,12},{6,14},{8,0},{10,2},{12,4},{14,6},{1,9},{3,11}... | collective-permute-start | bytes 196616 | tf_op jit(solution)/shard_map/ppermute | solution.py:330
  35.3 0.5 %collective-permute-start.15 = (bf16[8,16,256]{2,1,0:T(8,128)(2,1)S(1)}, bf16[8,16,256]{2,1,0:T(8,128)(2,1)S(1)}, u32[]{:S(2)}, u32[]{:S(2)}) collective-permute-start(bf16[8,16,256]{2,1,0:T(8,128)(2,1)S(1)} %get-tuple-element.49), channel_id=1, source_target_pairs={{0,2},{2,0},{4,6},{6,4},{8,10},{10,8},{12,14},{14,12},{1,3},{3,1},... | collective-permute-start | bytes 196616 | tf_op jit(solution)/shard_map/ppermute | solution.py:330
  35.8 0.1 collective-permute-done.13.refs_0_
  35.9 2.8 %collective-permute-done.14.refs_1_ = bf16[8,16,256]{2,1,0:T(8,128)(2,1)S(1)} collective-permute-done((bf16[8,16,256]{2,1,0:T(8,128)(2,1)S(1)}, bf16[8,16,256]{2,1,0:T(8,128)(2,1)S(1)}, u32[]{:S(2)}, u32[]{:S(2)}) %collective-permute-start.14) | collective-permute-done | bytes 65568 | tf_op jit(solution)/shard_map/ppermute | solution.py:330
  38.6 0.0 collective-permute-done.16.refs_3_
  38.6 1.4 %collective-permute-done.12.same = bf16[8,16,256]{2,1,0:T(8,128)(2,1)S(1)} collective-permute-done((bf16[8,16,256]{2,1,0:T(8,128)(2,1)S(1)}, bf16[8,16,256]{2,1,0:T(8,128)(2,1)S(1)}, u32[]{:S(2)}, u32[]{:S(2)}) %collective-permute-start.12) | collective-permute-done | bytes 65568 | tf_op jit(solution)/shard_map/ppermute | solution.py:330
  40.0 0.0 collective-permute-done.15.refs_2_
  40.0 0.0 copy-done.1
  40.0 1.3 %shard_map.69 = bf16[2,8,16,256]{3,2,1,0:T(8,128)(2,1)} custom-call(s32[2]{0:T(128)S(1)} %pad_add_fusion.pos, f32[1,256]{1,0:T(1,128)S(1)} %bitcast.7, f32[8,16,256]{2,1,0:T(8,128)S(1)} %get-tuple-element.45.own, bf16[8,16,256]{2,1,0:T(8,128)(2,1)S(1)} %collective-permute-done.12.same, bf16[8,16,256]{2,1,0:T(8,128)(2,1)S(1)} %collective-permute-done.13.refs_0_, ...), custom_call_target="tpu_custom_call" | custom-call | flops 1000 | bytes 1000 | tf_op jit(solution)/shard_map/pallas_call | solution.py:147
  (2 shorter events, 0.0 us)
Async XLA Ops:
  0.0 4.0 %copy-start = (bf16[2,8,16,256]{3,2,1,0:T(8,128)(2,1)S(1)}, bf16[2,8,16,256]{3,2,1,0:T(8,128)(2,1)}, u32[]{:S(2)}) copy-start(bf16[2,8,16,256]{3,2,1,0:T(8,128)(2,1)} %latent) | copy-start | bytes 393220
  0.0 9.9 %copy-start.2 = (f32[256]{0:T(256)S(1)}, f32[256]{0:T(256)}, u32[]{:S(2)}) copy-start(f32[256]{0:T(256)} %param.7) | copy-start | bytes 3076
  0.0 10.0 %copy-start.3 = (f32[256]{0:T(256)S(1)}, f32[256]{0:T(256)}, u32[]{:S(2)}) copy-start(f32[256]{0:T(256)} %param.8) | copy-start | bytes 3076
  0.0 20.6 %copy-start.4 = (s32[4]{0:T(128)S(1)}, s32[4]{0:T(128)}, u32[]{:S(2)}) copy-start(s32[4]{0:T(128)} %param.11) | copy-start | bytes 52
  1.4 14.0 %collective-permute-start.2 = (bf16[3,3,3,32,128]{4,3,2,1,0:T(8,128)(2,1)S(1)}, bf16[3,3,3,32,128]{4,3,2,1,0:T(8,128)(2,1)S(1)}, u32[]{:S(2)}, u32[]{:S(2)}) collective-permute-start(bf16[3,3,3,32,128]{4,3,2,1,0:T(8,128)(2,1)S(1)} %get-tuple-element.32), channel_id=1, source_target_pairs={{0,3},{1,2},{2,1},{3,0},{4,7},{5,6},{6,5},{7,4},{8,11},{9,10},{10,... | collective-permute-start | bytes 663560 | tf_op jit(solution)/shard_map/ppermute | solution.py:335
  4.8 6.0 %collective-permute-start.3 = (bf16[8,16,128]{2,1,0:T(8,128)(2,1)S(1)}, bf16[8,16,128]{2,1,0:T(8,128)(2,1)S(1)}, u32[]{:S(2)}, u32[]{:S(2)}) collective-permute-start(bf16[8,16,128]{2,1,0:T(8,128)(2,1)S(1)} %get-tuple-element.33), channel_id=1, source_target_pairs={{0,12},{2,14},{4,8},{6,10},{8,4},{10,6},{12,0},{14,2},{1,13},{3,15... | collective-permute-start | bytes 98312 | tf_op jit(solution)/shard_map/ppermute | solution.py:330
  8.5 12.2 %collective-permute-start.10 = (bf16[3,3,3,32,128]{4,3,2,1,0:T(8,128)(2,1)S(1)}, bf16[3,3,3,32,128]{4,3,2,1,0:T(8,128)(2,1)S(1)}, u32[]{:S(2)}, u32[]{:S(2)}) collective-permute-start(bf16[3,3,3,32,128]{4,3,2,1,0:T(8,128)(2,1)S(1)} %get-tuple-element.37), channel_id=1, source_target_pairs={{0,2},{2,0},{4,6},{6,4},{8,10},{10,8},{12,14},{14,12},{1,3},{3,1},... | collective-permute-start | bytes 663560 | tf_op jit(solution)/shard_map/ppermute | solution.py:330
  9.1 4.3 %collective-permute-start = (bf16[8,16,128]{2,1,0:T(8,128)(2,1)S(1)}, bf16[8,16,128]{2,1,0:T(8,128)(2,1)S(1)}, u32[]{:S(2)}, u32[]{:S(2)}) collective-permute-start(bf16[8,16,128]{2,1,0:T(8,128)(2,1)S(1)} %get-tuple-element.30), channel_id=1, source_target_pairs={{0,4},{2,6},{4,0},{6,2},{8,12},{10,14},{12,8},{14,10},{1,5},{3,7},... | collective-permute-start | bytes 98312 | tf_op jit(solution)/shard_map/ppermute | solution.py:330
  9.1 5.7 %collective-permute-start.1 = (bf16[8,16,128]{2,1,0:T(8,128)(2,1)S(1)}, bf16[8,16,128]{2,1,0:T(8,128)(2,1)S(1)}, u32[]{:S(2)}, u32[]{:S(2)}) collective-permute-start(bf16[8,16,128]{2,1,0:T(8,128)(2,1)S(1)} %get-tuple-element.31), channel_id=1, source_target_pairs={{0,8},{2,10},{4,12},{6,14},{8,0},{10,2},{12,4},{14,6},{1,9},{3,11}... | collective-permute-start | bytes 98312 | tf_op jit(solution)/shard_map/ppermute | solution.py:330
  10.8 6.6 %collective-permute-start.4 = (bf16[8,16,128]{2,1,0:T(8,128)(2,1)S(1)}, bf16[8,16,128]{2,1,0:T(8,128)(2,1)S(1)}, u32[]{:S(2)}, u32[]{:S(2)}) collective-permute-start(bf16[8,16,128]{2,1,0:T(8,128)(2,1)S(1)} %get-tuple-element.29.refs_0_), channel_id=1, source_target_pairs={{0,2},{2,0},{4,6},{6,4},{8,10},{10,8},{12,14},{14,12},{1,3},{3,1},... | collective-permute-start | bytes 98312 | tf_op jit(solution)/shard_map/ppermute | solution.py:330
  13.3 4.8 %collective-permute-start.5 = (bf16[8,16,128]{2,1,0:T(8,128)(2,1)S(1)}, bf16[8,16,128]{2,1,0:T(8,128)(2,1)S(1)}, u32[]{:S(2)}, u32[]{:S(2)}) collective-permute-start(bf16[8,16,128]{2,1,0:T(8,128)(2,1)S(1)} %collective-permute-done.refs_1_), channel_id=1, source_target_pairs={{0,2},{2,0},{4,6},{6,4},{8,10},{10,8},{12,14},{14,12},{1,3},{3,1},... | collective-permute-start | bytes 98312 | tf_op jit(solution)/shard_map/ppermute | solution.py:330
  14.8 3.9 %collective-permute-start.6 = (bf16[8,16,128]{2,1,0:T(8,128)(2,1)S(1)}, bf16[8,16,128]{2,1,0:T(8,128)(2,1)S(1)}, u32[]{:S(2)}, u32[]{:S(2)}) collective-permute-start(bf16[8,16,128]{2,1,0:T(8,128)(2,1)S(1)} %collective-permute-done.1.refs_2_), channel_id=1, source_target_pairs={{0,2},{2,0},{4,6},{6,4},{8,10},{10,8},{12,14},{14,12},{1,3},{3,1},... | collective-permute-start | bytes 98312 | tf_op jit(solution)/shard_map/ppermute | solution.py:330
  15.4 3.9 %collective-permute-start.7 = (bf16[8,16,128]{2,1,0:T(8,128)(2,1)S(1)}, bf16[8,16,128]{2,1,0:T(8,128)(2,1)S(1)}, u32[]{:S(2)}, u32[]{:S(2)}) collective-permute-start(bf16[8,16,128]{2,1,0:T(8,128)(2,1)S(1)} %collective-permute-done.3.refs_3_), channel_id=1, source_target_pairs={{0,2},{2,0},{4,6},{6,4},{8,10},{10,8},{12,14},{14,12},{1,3},{3,1},... | collective-permute-start | bytes 98312 | tf_op jit(solution)/shard_map/ppermute | solution.py:330
  17.4 3.3 %collective-permute-start.9 = (bf16[3,3,3,32,128]{4,3,2,1,0:T(8,128)(2,1)S(1)}, bf16[3,3,3,32,128]{4,3,2,1,0:T(8,128)(2,1)S(1)}, u32[]{:S(2)}, u32[]{:S(2)}) collective-permute-start(bf16[3,3,3,32,128]{4,3,2,1,0:T(8,128)(2,1)S(1)} %get-tuple-element.36), channel_id=1, source_target_pairs={{0,1},{1,0},{2,3},{3,2},{4,5},{5,4},{6,7},{7,6},{8,9},{9,8},{10,11... | collective-permute-start | bytes 663560 | tf_op jit(solution)/shard_map/ppermute | solution.py:335
  20.5 1.8 %collective-permute-start.8 = (bf16[2,8,96,128]{3,2,1,0:T(8,128)(2,1)S(1)}, bf16[2,8,96,128]{3,2,1,0:T(8,128)(2,1)S(1)}, u32[]{:S(2)}, u32[]{:S(2)}) collective-permute-start(bf16[2,8,96,128]{3,2,1,0:T(8,128)(2,1)S(1)} %shard_map.65.mine), channel_id=1, source_target_pairs={{0,1},{1,0},{2,3},{3,2},{4,5},{5,4},{6,7},{7,6},{8,9},{9,8},{10,11... | collective-permute-start | bytes 1179656 | tf_op jit(solution)/shard_map/ppermute | solution.py:371
  22.4 17.6 %copy-start.1 = (f32[256]{0:T(256)S(1)}, f32[256]{0:T(256)}, u32[]{:S(2)}) copy-start(f32[256]{0:T(256)} %param.10) | copy-start | bytes 3076
  26.1 7.4 %collective-permute-start.11 = (bf16[2,8,16,256]{3,2,1,0:T(8,128)(2,1)S(1)}, bf16[2,8,16,256]{3,2,1,0:T(8,128)(2,1)S(1)}, u32[]{:S(2)}, u32[]{:S(2)}) collective-permute-start(bf16[2,8,16,256]{3,2,1,0:T(8,128)(2,1)S(1)} %get-tuple-element.42), channel_id=1, source_target_pairs={{0,4},{2,6},{4,0},{6,2},{8,12},{10,14},{12,8},{14,10},{1,5},{3,7},... | collective-permute-start | bytes 393224 | tf_op jit(solution)/shard_map/ppermute | solution.py:330
  28.2 7.7 %collective-permute-start.13 = (bf16[8,16,256]{2,1,0:T(8,128)(2,1)S(1)}, bf16[8,16,256]{2,1,0:T(8,128)(2,1)S(1)}, u32[]{:S(2)}, u32[]{:S(2)}) collective-permute-start(bf16[8,16,256]{2,1,0:T(8,128)(2,1)S(1)} %get-tuple-element.47), channel_id=1, source_target_pairs={{0,14},{2,12},{4,10},{6,8},{8,6},{10,4},{12,2},{14,0},{1,15},{3,13... | collective-permute-start | bytes 196616 | tf_op jit(solution)/shard_map/ppermute | solution.py:330
  30.1 8.5 %collective-permute-start.14 = (bf16[8,16,256]{2,1,0:T(8,128)(2,1)S(1)}, bf16[8,16,256]{2,1,0:T(8,128)(2,1)S(1)}, u32[]{:S(2)}, u32[]{:S(2)}) collective-permute-start(bf16[8,16,256]{2,1,0:T(8,128)(2,1)S(1)} %get-tuple-element.48), channel_id=1, source_target_pairs={{0,10},{2,8},{4,14},{6,12},{8,2},{10,0},{12,6},{14,4},{1,11},{3,9}... | collective-permute-start | bytes 196616 | tf_op jit(solution)/shard_map/ppermute | solution.py:330
  30.6 8.0 %collective-permute-start.16 = (bf16[8,16,256]{2,1,0:T(8,128)(2,1)S(1)}, bf16[8,16,256]{2,1,0:T(8,128)(2,1)S(1)}, u32[]{:S(2)}, u32[]{:S(2)}) collective-permute-start(bf16[8,16,256]{2,1,0:T(8,128)(2,1)S(1)} %get-tuple-element.50), channel_id=1, source_target_pairs={{0,6},{2,4},{4,2},{6,0},{8,14},{10,12},{12,10},{14,8},{1,7},{3,5},... | collective-permute-start | bytes 196616 | tf_op jit(solution)/shard_map/ppermute | solution.py:330
  34.1 5.9 %collective-permute-start.12 = (bf16[8,16,256]{2,1,0:T(8,128)(2,1)S(1)}, bf16[8,16,256]{2,1,0:T(8,128)(2,1)S(1)}, u32[]{:S(2)}, u32[]{:S(2)}) collective-permute-start(bf16[8,16,256]{2,1,0:T(8,128)(2,1)S(1)} %get-tuple-element.46), channel_id=1, source_target_pairs={{0,8},{2,10},{4,12},{6,14},{8,0},{10,2},{12,4},{14,6},{1,9},{3,11}... | collective-permute-start | bytes 196616 | tf_op jit(solution)/shard_map/ppermute | solution.py:330
  35.3 4.7 %collective-permute-start.15 = (bf16[8,16,256]{2,1,0:T(8,128)(2,1)S(1)}, bf16[8,16,256]{2,1,0:T(8,128)(2,1)S(1)}, u32[]{:S(2)}, u32[]{:S(2)}) collective-permute-start(bf16[8,16,256]{2,1,0:T(8,128)(2,1)S(1)} %get-tuple-element.49), channel_id=1, source_target_pairs={{0,2},{2,0},{4,6},{6,4},{8,10},{10,8},{12,14},{14,12},{1,3},{3,1},... | collective-permute-start | bytes 196616 | tf_op jit(solution)/shard_map/ppermute | solution.py:330

commit v6 on v5

--- a/solution.py
+++ b/solution.py
@@ -354,7 +354,7 @@
     other_far = across(quarters[3], 1)
     packed = call(pack_body, [block] * 4)(pos, latent)
     near = [packed[0]] + [exchanged(packed[k], k, 0) for k in (1, 2, 3)]
-    other_far, near[3] = lax.optimization_barrier((other_far, near[3]))
+    same_far, near[3] = lax.optimization_barrier((same_far, near[3]))
     far = [exchanged(part, 0, 1) for part in near]
     matrix = jax.ShapeDtypeStruct((TAPS, 768, 256), bf16)
     diag, lower = call(weights_body, [matrix] * 2)(pos, same, other, same_far, other_far)

time: 41.4 us -> 41.4 us (level)
    ppermute x2, starting transfers between devices: 2.51 us -> 0.91 us  [across(): return lax.ppermute(block, ('tm', 'ch'), route)]
    ppermute x14, starting transfers between devices: 18.3 us -> 19.8 us  [exchanged(): return lax.ppermute(block, ('tile', 'tm'), route)]
  transfers between devices with their start and end apart: 17 -> 17, of which waited for: 10 -> 9; matrix products, arithmetic and copies ran while one was open for 1% -> 1% of each run, Pallas kernels for 8% -> 8%
where the time goes in v6:
time: 41.4 us; the launch traced here: 41.3 us
  starting transfers between devices  20.8 us (50%)
  waiting for transfers between devices  9.97 us (24%)
  Pallas kernels  8.52 us (21%)
  local copies, waits for them, and re-layouts  1.61 us (4%)
    ppermute x14, starting transfers between devices, exchanged(): return lax.ppermute(block, ('tile', 'tm'), route)  19.8 us
    ppermute x14, waiting for transfers between devices, exchanged(): return lax.ppermute(block, ('tile', 'tm'), route)  9.25 us
    pallas_call x6, Pallas kernels, run(): pl.pallas_call(body, out_shape=outs, in_specs=specs, out_specs=jax.tree.m...  8.52 us
    dynamic_slice x1, local copies, waits for them, and re-layouts, quarter(): return lax.dynamic_slice_in_dim(kernel, start, 128, axis=4)  1.37 us
    ppermute x2, starting transfers between devices, across(): return lax.ppermute(block, ('tm', 'ch'), route)  0.91 us
  transfers between devices with their start and end apart: 17, of which 9 were waited for; matrix products, arithmetic and copies ran while one was open for 1% of the time, Pallas kernels for 8%

profile of v6, /device:TPU:0, one launch (start us, length us, event | category | flops | bytes accessed | tf_op | source)
XLA Modules:
  0.0 41.3 jit_solution(12419912876544998726)
XLA Ops:
  0.0 0.0 copy-start
  0.0 0.0 copy-start.2
  0.0 0.0 copy-start.3
  0.0 0.0 copy-start.4
  0.0 1.4 %constant_dynamic-slice_fusion = (bf16[3,3,3,32,128]{4,3,2,1,0:T(8,128)(2,1)S(1)}, bf16[3,3,3,32,128]{4,3,2,1,0:T(8,128)(2,1)S(1)}, bf16[3,3,3,32,128]{4,3,2,1,0:T(8,128)(2,1)S(1)}, bf16[3,3,3,32,128]{4,3,2,1,0:T(8,128)(2,1)S(1)}) fusion(bf16[3,3,3,32,512]{4,3,2,1,0:T(8,128)(2,1)} %param.9, s32[]{:T(128)S(6)} %select_n.20, s32[]{:T(128)S(6)} %select_n.18, ...), kind=kLoop, calls=%fused_computation.1 | loop fusion | bytes 1769488 | tf_op jit(solution)/shard_map/dynamic_slice | solution.py:347
  1.4 3.1 %collective-permute-start.2 = (bf16[3,3,3,32,128]{4,3,2,1,0:T(8,128)(2,1)S(1)}, bf16[3,3,3,32,128]{4,3,2,1,0:T(8,128)(2,1)S(1)}, u32[]{:S(2)}, u32[]{:S(2)}) collective-permute-start(bf16[3,3,3,32,128]{4,3,2,1,0:T(8,128)(2,1)S(1)} %get-tuple-element.32), channel_id=1, source_target_pairs={{0,2},{2,0},{4,6},{6,4},{8,10},{10,8},{12,14},{14,12},{1,3},{3,1},... | collective-permute-start | bytes 663560 | tf_op jit(solution)/shard_map/ppermute | solution.py:330
  4.5 0.1 pad_add_fusion.pos
  4.5 0.0 copy-done
  4.5 0.9 %shard_map.64 = (bf16[8,16,128]{2,1,0:T(8,128)(2,1)S(1)}, bf16[8,16,128]{2,1,0:T(8,128)(2,1)S(1)}, bf16[8,16,128]{2,1,0:T(8,128)(2,1)S(1)}, bf16[8,16,128]{2,1,0:T(8,128)(2,1)S(1)}) custom-call(s32[2]{0:T(128)S(1)} %pad_add_fusion.pos, bf16[2,8,16,256]{3,2,1,0:T(8,128)(2,1)S(1)} %copy-done), custom_call_target="tpu_custom_call" | custom-call | flops 1000 | bytes 1000 | tf_op jit(solution)/shard_map/pallas_call | solution.py:147
  5.4 3.6 %collective-permute-start.3 = (bf16[8,16,128]{2,1,0:T(8,128)(2,1)S(1)}, bf16[8,16,128]{2,1,0:T(8,128)(2,1)S(1)}, u32[]{:S(2)}, u32[]{:S(2)}) collective-permute-start(bf16[8,16,128]{2,1,0:T(8,128)(2,1)S(1)} %get-tuple-element.33), channel_id=1, source_target_pairs={{0,12},{2,14},{4,8},{6,10},{8,4},{10,6},{12,0},{14,2},{1,13},{3,15... | collective-permute-start | bytes 98312 | tf_op jit(solution)/shard_map/ppermute | solution.py:330
  9.1 0.0 collective-permute-start.10
  9.1 0.0 collective-permute-start
  9.1 0.8 %collective-permute-start.1 = (bf16[8,16,128]{2,1,0:T(8,128)(2,1)S(1)}, bf16[8,16,128]{2,1,0:T(8,128)(2,1)S(1)}, u32[]{:S(2)}, u32[]{:S(2)}) collective-permute-start(bf16[8,16,128]{2,1,0:T(8,128)(2,1)S(1)} %get-tuple-element.31), channel_id=1, source_target_pairs={{0,8},{2,10},{4,12},{6,14},{8,0},{10,2},{12,4},{14,6},{1,9},{3,11}... | collective-permute-start | bytes 98312 | tf_op jit(solution)/shard_map/ppermute | solution.py:330
  9.9 0.0 copy-done.2
  9.9 0.1 dynamic_slice.18
  9.9 0.0 copy-done.3
  9.9 0.1 dynamic_slice.19
  10.0 1.2 %collective-permute-done.3.refs_3_ = bf16[8,16,128]{2,1,0:T(8,128)(2,1)S(1)} collective-permute-done((bf16[8,16,128]{2,1,0:T(8,128)(2,1)S(1)}, bf16[8,16,128]{2,1,0:T(8,128)(2,1)S(1)}, u32[]{:S(2)}, u32[]{:S(2)}) %collective-permute-start.3) | collective-permute-done | bytes 32800 | tf_op jit(solution)/shard_map/ppermute | solution.py:330
  11.2 0.3 collective-permute-start.4
  11.5 1.5 %collective-permute-done.refs_1_ = bf16[8,16,128]{2,1,0:T(8,128)(2,1)S(1)} collective-permute-done((bf16[8,16,128]{2,1,0:T(8,128)(2,1)S(1)}, bf16[8,16,128]{2,1,0:T(8,128)(2,1)S(1)}, u32[]{:S(2)}, u32[]{:S(2)}) %collective-permute-start) | collective-permute-done | bytes 32800 | tf_op jit(solution)/shard_map/ppermute | solution.py:330
  13.0 1.0 %collective-permute-start.5 = (bf16[8,16,128]{2,1,0:T(8,128)(2,1)S(1)}, bf16[8,16,128]{2,1,0:T(8,128)(2,1)S(1)}, u32[]{:S(2)}, u32[]{:S(2)}) collective-permute-start(bf16[8,16,128]{2,1,0:T(8,128)(2,1)S(1)} %collective-permute-done.refs_1_), channel_id=1, source_target_pairs={{0,2},{2,0},{4,6},{6,4},{8,10},{10,8},{12,14},{14,12},{1,3},{3,1},... | collective-permute-start | bytes 98312 | tf_op jit(solution)/shard_map/ppermute | solution.py:330
  14.0 0.0 collective-permute-done.1.refs_2_
  14.0 1.0 %collective-permute-start.6 = (bf16[8,16,128]{2,1,0:T(8,128)(2,1)S(1)}, bf16[8,16,128]{2,1,0:T(8,128)(2,1)S(1)}, u32[]{:S(2)}, u32[]{:S(2)}) collective-permute-start(bf16[8,16,128]{2,1,0:T(8,128)(2,1)S(1)} %collective-permute-done.1.refs_2_), channel_id=1, source_target_pairs={{0,2},{2,0},{4,6},{6,4},{8,10},{10,8},{12,14},{14,12},{1,3},{3,1},... | collective-permute-start | bytes 98312 | tf_op jit(solution)/shard_map/ppermute | solution.py:330
  15.0 0.0 collective-permute-done.2.same_far
  15.0 1.0 %collective-permute-start.7 = (bf16[8,16,128]{2,1,0:T(8,128)(2,1)S(1)}, bf16[8,16,128]{2,1,0:T(8,128)(2,1)S(1)}, u32[]{:S(2)}, u32[]{:S(2)}) collective-permute-start(bf16[8,16,128]{2,1,0:T(8,128)(2,1)S(1)} %collective-permute-done.3.refs_3_), channel_id=1, source_target_pairs={{0,2},{2,0},{4,6},{6,4},{8,10},{10,8},{12,14},{14,12},{1,3},{3,1},... | collective-permute-start | bytes 98312 | tf_op jit(solution)/shard_map/ppermute | solution.py:330
  16.0 0.1 maximum_bitcast_fusion
  16.1 0.4 collective-permute-done.4.refs_4_
  16.5 0.9 %collective-permute-start.9 = (bf16[3,3,3,32,128]{4,3,2,1,0:T(8,128)(2,1)S(1)}, bf16[3,3,3,32,128]{4,3,2,1,0:T(8,128)(2,1)S(1)}, u32[]{:S(2)}, u32[]{:S(2)}) collective-permute-start(bf16[3,3,3,32,128]{4,3,2,1,0:T(8,128)(2,1)S(1)} %get-tuple-element.36), channel_id=1, source_target_pairs={{0,1},{1,0},{2,3},{3,2},{4,5},{5,4},{6,7},{7,6},{8,9},{9,8},{10,11... | collective-permute-start | bytes 663560 | tf_op jit(solution)/shard_map/ppermute | solution.py:335
  17.4 0.0 collective-permute-done.5.refs_5_
  17.4 0.9 %collective-permute-done.6.refs_6_ = bf16[8,16,128]{2,1,0:T(8,128)(2,1)S(1)} collective-permute-done((bf16[8,16,128]{2,1,0:T(8,128)(2,1)S(1)}, bf16[8,16,128]{2,1,0:T(8,128)(2,1)S(1)}, u32[]{:S(2)}, u32[]{:S(2)}) %collective-permute-start.6) | collective-permute-done | bytes 32800 | tf_op jit(solution)/shard_map/ppermute | solution.py:330
  18.3 0.7 %collective-permute-done.7.refs_7_ = bf16[8,16,128]{2,1,0:T(8,128)(2,1)S(1)} collective-permute-done((bf16[8,16,128]{2,1,0:T(8,128)(2,1)S(1)}, bf16[8,16,128]{2,1,0:T(8,128)(2,1)S(1)}, u32[]{:S(2)}, u32[]{:S(2)}) %collective-permute-start.7) | collective-permute-done | bytes 32800 | tf_op jit(solution)/shard_map/ppermute | solution.py:330
  19.0 1.2 %shard_map.65.mine = bf16[2,8,96,128]{3,2,1,0:T(8,128)(2,1)S(1)} custom-call(s32[2]{0:T(128)S(1)} %pad_add_fusion.pos, f32[1,128]{1,0:T(1,128)S(1)} %get-tuple-element.55.gain, f32[1,128]{1,0:T(1,128)S(1)} %get-tuple-element.56.shift, bf16[8,16,128]{2,1,0:T(8,128)(2,1)S(1)} %get-tuple-element.29.refs_0_, ...), custom_call_target="tpu_custom_call" | custom-call | flops 1000 | bytes 1000 | tf_op jit(solution)/shard_map/pallas_call | solution.py:147
  20.3 0.1 collective-permute-start.8
  20.3 0.0 copy-done.4
  20.4 0.1 add_divide_fusion
  20.4 0.0 collective-permute-done.10.other_far
  20.5 0.0 collective-permute-done.9.other
  20.5 0.9 %shard_map.66 = (bf16[3,768,256]{2,1,0:T(8,128)(2,1)S(1)}, bf16[3,768,256]{2,1,0:T(8,128)(2,1)S(1)}) custom-call(s32[2]{0:T(128)S(1)} %pad_add_fusion.pos, bf16[3,3,3,32,128]{4,3,2,1,0:T(8,128)(2,1)S(1)} %get-tuple-element.35.same, bf16[3,3,3,32,128]{4,3,2,1,0:T(8,128)(2,1)S(1)} %collective-permute-done.9.other, ...), custom_call_target="tpu_custom_call" | custom-call | flops 1000 | bytes 1000 | tf_op jit(solution)/shard_map/pallas_call | solution.py:147
  21.3 0.7 %collective-permute-done.8.sibling = bf16[2,8,96,128]{3,2,1,0:T(8,128)(2,1)S(1)} collective-permute-done((bf16[2,8,96,128]{3,2,1,0:T(8,128)(2,1)S(1)}, bf16[2,8,96,128]{3,2,1,0:T(8,128)(2,1)S(1)}, u32[]{:S(2)}, u32[]{:S(2)}) %collective-permute-start.8) | collective-permute-done | bytes 393248 | tf_op jit(solution)/shard_map/ppermute | solution.py:371
  22.0 0.1 broadcast_in_dim.20.blend
  22.1 0.0 copy-start.1
  22.1 3.8 %shard_map.67 = (bf16[8,16,256]{2,1,0:T(8,128)(2,1)S(1)}, bf16[8,16,256]{2,1,0:T(8,128)(2,1)S(1)}, bf16[8,16,256]{2,1,0:T(8,128)(2,1)S(1)}, bf16[8,16,256]{2,1,0...) custom-call(s32[2]{0:T(128)S(1)} %pad_add_fusion.pos, ...), custom_call_target="tpu_custom_call" | custom-call | flops 1000 | bytes 1000 | tf_op jit(solution)/shard_map/pallas_call | solution.py:147
  25.9 2.1 %collective-permute-start.11 = (bf16[2,8,16,256]{3,2,1,0:T(8,128)(2,1)S(1)}, bf16[2,8,16,256]{3,2,1,0:T(8,128)(2,1)S(1)}, u32[]{:S(2)}, u32[]{:S(2)}) collective-permute-start(bf16[2,8,16,256]{3,2,1,0:T(8,128)(2,1)S(1)} %get-tuple-element.42), channel_id=1, source_target_pairs={{0,4},{2,6},{4,0},{6,2},{8,12},{10,14},{12,8},{14,10},{1,5},{3,7},... | collective-permute-start | bytes 393224 | tf_op jit(solution)/shard_map/ppermute | solution.py:330
  28.0 1.7 %collective-permute-start.13 = (bf16[8,16,256]{2,1,0:T(8,128)(2,1)S(1)}, bf16[8,16,256]{2,1,0:T(8,128)(2,1)S(1)}, u32[]{:S(2)}, u32[]{:S(2)}) collective-permute-start(bf16[8,16,256]{2,1,0:T(8,128)(2,1)S(1)} %get-tuple-element.47), channel_id=1, source_target_pairs={{0,14},{2,12},{4,10},{6,8},{8,6},{10,4},{12,2},{14,0},{1,15},{3,13... | collective-permute-start | bytes 196616 | tf_op jit(solution)/shard_map/ppermute | solution.py:330
  29.6 0.8 %collective-permute-start.14 = (bf16[8,16,256]{2,1,0:T(8,128)(2,1)S(1)}, bf16[8,16,256]{2,1,0:T(8,128)(2,1)S(1)}, u32[]{:S(2)}, u32[]{:S(2)}) collective-permute-start(bf16[8,16,256]{2,1,0:T(8,128)(2,1)S(1)} %get-tuple-element.48), channel_id=1, source_target_pairs={{0,10},{2,8},{4,14},{6,12},{8,2},{10,0},{12,6},{14,4},{1,11},{3,9}... | collective-permute-start | bytes 196616 | tf_op jit(solution)/shard_map/ppermute | solution.py:330
  30.4 3.1 %collective-permute-start.16 = (bf16[8,16,256]{2,1,0:T(8,128)(2,1)S(1)}, bf16[8,16,256]{2,1,0:T(8,128)(2,1)S(1)}, u32[]{:S(2)}, u32[]{:S(2)}) collective-permute-start(bf16[8,16,256]{2,1,0:T(8,128)(2,1)S(1)} %get-tuple-element.50), channel_id=1, source_target_pairs={{0,6},{2,4},{4,2},{6,0},{8,14},{10,12},{12,10},{14,8},{1,7},{3,5},... | collective-permute-start | bytes 196616 | tf_op jit(solution)/shard_map/ppermute | solution.py:330
  33.5 0.0 collective-permute-done.11.came
  33.5 0.6 %shard_map.68 = (f32[8,16,256]{2,1,0:T(8,128)S(1)}, bf16[8,16,256]{2,1,0:T(8,128)(2,1)S(1)}) custom-call(s32[2]{0:T(128)S(1)} %pad_add_fusion.pos, f32[2,8,16,256]{3,2,1,0:T(8,128)S(1)} %get-tuple-element.41.kept, bf16[2,8,16,256]{3,2,1,0:T(8,128)(2,1)S(1)} %collective-permute-done.11.came), custom_call_target="tpu_custom_call" | custom-call | flops 1000 | bytes 1000 | tf_op jit(solution)/shard_map/pallas_call | solution.py:147
  34.1 1.1 %collective-permute-start.12 = (bf16[8,16,256]{2,1,0:T(8,128)(2,1)S(1)}, bf16[8,16,256]{2,1,0:T(8,128)(2,1)S(1)}, u32[]{:S(2)}, u32[]{:S(2)}) collective-permute-start(bf16[8,16,256]{2,1,0:T(8,128)(2,1)S(1)} %get-tuple-element.46), channel_id=1, source_target_pairs={{0,8},{2,10},{4,12},{6,14},{8,0},{10,2},{12,4},{14,6},{1,9},{3,11}... | collective-permute-start | bytes 196616 | tf_op jit(solution)/shard_map/ppermute | solution.py:330
  35.1 0.3 collective-permute-start.15
  35.5 0.1 collective-permute-done.13.refs_0_
  35.6 2.7 %collective-permute-done.14.refs_1_ = bf16[8,16,256]{2,1,0:T(8,128)(2,1)S(1)} collective-permute-done((bf16[8,16,256]{2,1,0:T(8,128)(2,1)S(1)}, bf16[8,16,256]{2,1,0:T(8,128)(2,1)S(1)}, u32[]{:S(2)}, u32[]{:S(2)}) %collective-permute-start.14) | collective-permute-done | bytes 65568 | tf_op jit(solution)/shard_map/ppermute | solution.py:330
  38.3 0.0 collective-permute-done.16.refs_3_
  38.3 1.6 %collective-permute-done.12.same = bf16[8,16,256]{2,1,0:T(8,128)(2,1)S(1)} collective-permute-done((bf16[8,16,256]{2,1,0:T(8,128)(2,1)S(1)}, bf16[8,16,256]{2,1,0:T(8,128)(2,1)S(1)}, u32[]{:S(2)}, u32[]{:S(2)}) %collective-permute-start.12) | collective-permute-done | bytes 65568 | tf_op jit(solution)/shard_map/ppermute | solution.py:330
  40.0 0.0 collective-permute-done.15.refs_2_
  40.0 0.0 copy-done.1
  40.0 1.3 %shard_map.69 = bf16[2,8,16,256]{3,2,1,0:T(8,128)(2,1)} custom-call(s32[2]{0:T(128)S(1)} %pad_add_fusion.pos, f32[1,256]{1,0:T(1,128)S(1)} %bitcast.7, f32[8,16,256]{2,1,0:T(8,128)S(1)} %get-tuple-element.45.own, bf16[8,16,256]{2,1,0:T(8,128)(2,1)S(1)} %collective-permute-done.12.same, bf16[8,16,256]{2,1,0:T(8,128)(2,1)S(1)} %collective-permute-done.13.refs_0_, ...), custom_call_target="tpu_custom_call" | custom-call | flops 1000 | bytes 1000 | tf_op jit(solution)/shard_map/pallas_call | solution.py:147
  (2 shorter events, 0.0 us)
Async XLA Ops:
  0.0 4.5 %copy-start = (bf16[2,8,16,256]{3,2,1,0:T(8,128)(2,1)S(1)}, bf16[2,8,16,256]{3,2,1,0:T(8,128)(2,1)}, u32[]{:S(2)}) copy-start(bf16[2,8,16,256]{3,2,1,0:T(8,128)(2,1)} %latent) | copy-start | bytes 393220
  0.0 9.9 %copy-start.2 = (f32[256]{0:T(256)S(1)}, f32[256]{0:T(256)}, u32[]{:S(2)}) copy-start(f32[256]{0:T(256)} %param.7) | copy-start | bytes 3076
  0.0 9.9 %copy-start.3 = (f32[256]{0:T(256)S(1)}, f32[256]{0:T(256)}, u32[]{:S(2)}) copy-start(f32[256]{0:T(256)} %param.8) | copy-start | bytes 3076
  0.0 20.3 %copy-start.4 = (s32[4]{0:T(128)S(1)}, s32[4]{0:T(128)}, u32[]{:S(2)}) copy-start(s32[4]{0:T(128)} %param.11) | copy-start | bytes 52
  1.4 13.6 %collective-permute-start.2 = (bf16[3,3,3,32,128]{4,3,2,1,0:T(8,128)(2,1)S(1)}, bf16[3,3,3,32,128]{4,3,2,1,0:T(8,128)(2,1)S(1)}, u32[]{:S(2)}, u32[]{:S(2)}) collective-permute-start(bf16[3,3,3,32,128]{4,3,2,1,0:T(8,128)(2,1)S(1)} %get-tuple-element.32), channel_id=1, source_target_pairs={{0,2},{2,0},{4,6},{6,4},{8,10},{10,8},{12,14},{14,12},{1,3},{3,1},... | collective-permute-start | bytes 663560 | tf_op jit(solution)/shard_map/ppermute | solution.py:330
  5.4 5.8 %collective-permute-start.3 = (bf16[8,16,128]{2,1,0:T(8,128)(2,1)S(1)}, bf16[8,16,128]{2,1,0:T(8,128)(2,1)S(1)}, u32[]{:S(2)}, u32[]{:S(2)}) collective-permute-start(bf16[8,16,128]{2,1,0:T(8,128)(2,1)S(1)} %get-tuple-element.33), channel_id=1, source_target_pairs={{0,12},{2,14},{4,8},{6,10},{8,4},{10,6},{12,0},{14,2},{1,13},{3,15... | collective-permute-start | bytes 98312 | tf_op jit(solution)/shard_map/ppermute | solution.py:330
  9.1 11.4 %collective-permute-start.10 = (bf16[3,3,3,32,128]{4,3,2,1,0:T(8,128)(2,1)S(1)}, bf16[3,3,3,32,128]{4,3,2,1,0:T(8,128)(2,1)S(1)}, u32[]{:S(2)}, u32[]{:S(2)}) collective-permute-start(bf16[3,3,3,32,128]{4,3,2,1,0:T(8,128)(2,1)S(1)} %get-tuple-element.38), channel_id=1, source_target_pairs={{0,3},{1,2},{2,1},{3,0},{4,7},{5,6},{6,5},{7,4},{8,11},{9,10},{10,... | collective-permute-start | bytes 663560 | tf_op jit(solution)/shard_map/ppermute | solution.py:335
  9.1 3.9 %collective-permute-start = (bf16[8,16,128]{2,1,0:T(8,128)(2,1)S(1)}, bf16[8,16,128]{2,1,0:T(8,128)(2,1)S(1)}, u32[]{:S(2)}, u32[]{:S(2)}) collective-permute-start(bf16[8,16,128]{2,1,0:T(8,128)(2,1)S(1)} %get-tuple-element.30), channel_id=1, source_target_pairs={{0,4},{2,6},{4,0},{6,2},{8,12},{10,14},{12,8},{14,10},{1,5},{3,7},... | collective-permute-start | bytes 98312 | tf_op jit(solution)/shard_map/ppermute | solution.py:330
  9.1 4.9 %collective-permute-start.1 = (bf16[8,16,128]{2,1,0:T(8,128)(2,1)S(1)}, bf16[8,16,128]{2,1,0:T(8,128)(2,1)S(1)}, u32[]{:S(2)}, u32[]{:S(2)}) collective-permute-start(bf16[8,16,128]{2,1,0:T(8,128)(2,1)S(1)} %get-tuple-element.31), channel_id=1, source_target_pairs={{0,8},{2,10},{4,12},{6,14},{8,0},{10,2},{12,4},{14,6},{1,9},{3,11}... | collective-permute-start | bytes 98312 | tf_op jit(solution)/shard_map/ppermute | solution.py:330
  11.2 5.3 %collective-permute-start.4 = (bf16[8,16,128]{2,1,0:T(8,128)(2,1)S(1)}, bf16[8,16,128]{2,1,0:T(8,128)(2,1)S(1)}, u32[]{:S(2)}, u32[]{:S(2)}) collective-permute-start(bf16[8,16,128]{2,1,0:T(8,128)(2,1)S(1)} %get-tuple-element.29.refs_0_), channel_id=1, source_target_pairs={{0,2},{2,0},{4,6},{6,4},{8,10},{10,8},{12,14},{14,12},{1,3},{3,1},... | collective-permute-start | bytes 98312 | tf_op jit(solution)/shard_map/ppermute | solution.py:330
  13.0 4.4 %collective-permute-start.5 = (bf16[8,16,128]{2,1,0:T(8,128)(2,1)S(1)}, bf16[8,16,128]{2,1,0:T(8,128)(2,1)S(1)}, u32[]{:S(2)}, u32[]{:S(2)}) collective-permute-start(bf16[8,16,128]{2,1,0:T(8,128)(2,1)S(1)} %collective-permute-done.refs_1_), channel_id=1, source_target_pairs={{0,2},{2,0},{4,6},{6,4},{8,10},{10,8},{12,14},{14,12},{1,3},{3,1},... | collective-permute-start | bytes 98312 | tf_op jit(solution)/shard_map/ppermute | solution.py:330
  14.0 4.3 %collective-permute-start.6 = (bf16[8,16,128]{2,1,0:T(8,128)(2,1)S(1)}, bf16[8,16,128]{2,1,0:T(8,128)(2,1)S(1)}, u32[]{:S(2)}, u32[]{:S(2)}) collective-permute-start(bf16[8,16,128]{2,1,0:T(8,128)(2,1)S(1)} %collective-permute-done.1.refs_2_), channel_id=1, source_target_pairs={{0,2},{2,0},{4,6},{6,4},{8,10},{10,8},{12,14},{14,12},{1,3},{3,1},... | collective-permute-start | bytes 98312 | tf_op jit(solution)/shard_map/ppermute | solution.py:330
  15.0 4.0 %collective-permute-start.7 = (bf16[8,16,128]{2,1,0:T(8,128)(2,1)S(1)}, bf16[8,16,128]{2,1,0:T(8,128)(2,1)S(1)}, u32[]{:S(2)}, u32[]{:S(2)}) collective-permute-start(bf16[8,16,128]{2,1,0:T(8,128)(2,1)S(1)} %collective-permute-done.3.refs_3_), channel_id=1, source_target_pairs={{0,2},{2,0},{4,6},{6,4},{8,10},{10,8},{12,14},{14,12},{1,3},{3,1},... | collective-permute-start | bytes 98312 | tf_op jit(solution)/shard_map/ppermute | solution.py:330
  16.5 4.0 %collective-permute-start.9 = (bf16[3,3,3,32,128]{4,3,2,1,0:T(8,128)(2,1)S(1)}, bf16[3,3,3,32,128]{4,3,2,1,0:T(8,128)(2,1)S(1)}, u32[]{:S(2)}, u32[]{:S(2)}) collective-permute-start(bf16[3,3,3,32,128]{4,3,2,1,0:T(8,128)(2,1)S(1)} %get-tuple-element.36), channel_id=1, source_target_pairs={{0,1},{1,0},{2,3},{3,2},{4,5},{5,4},{6,7},{7,6},{8,9},{9,8},{10,11... | collective-permute-start | bytes 663560 | tf_op jit(solution)/shard_map/ppermute | solution.py:335
  20.3 1.8 %collective-permute-start.8 = (bf16[2,8,96,128]{3,2,1,0:T(8,128)(2,1)S(1)}, bf16[2,8,96,128]{3,2,1,0:T(8,128)(2,1)S(1)}, u32[]{:S(2)}, u32[]{:S(2)}) collective-permute-start(bf16[2,8,96,128]{3,2,1,0:T(8,128)(2,1)S(1)} %shard_map.65.mine), channel_id=1, source_target_pairs={{0,1},{1,0},{2,3},{3,2},{4,5},{5,4},{6,7},{7,6},{8,9},{9,8},{10,11... | collective-permute-start | bytes 1179656 | tf_op jit(solution)/shard_map/ppermute | solution.py:371
  22.1 17.9 %copy-start.1 = (f32[256]{0:T(256)S(1)}, f32[256]{0:T(256)}, u32[]{:S(2)}) copy-start(f32[256]{0:T(256)} %param.10) | copy-start | bytes 3076
  25.9 7.6 %collective-permute-start.11 = (bf16[2,8,16,256]{3,2,1,0:T(8,128)(2,1)S(1)}, bf16[2,8,16,256]{3,2,1,0:T(8,128)(2,1)S(1)}, u32[]{:S(2)}, u32[]{:S(2)}) collective-permute-start(bf16[2,8,16,256]{3,2,1,0:T(8,128)(2,1)S(1)} %get-tuple-element.42), channel_id=1, source_target_pairs={{0,4},{2,6},{4,0},{6,2},{8,12},{10,14},{12,8},{14,10},{1,5},{3,7},... | collective-permute-start | bytes 393224 | tf_op jit(solution)/shard_map/ppermute | solution.py:330
  28.0 7.7 %collective-permute-start.13 = (bf16[8,16,256]{2,1,0:T(8,128)(2,1)S(1)}, bf16[8,16,256]{2,1,0:T(8,128)(2,1)S(1)}, u32[]{:S(2)}, u32[]{:S(2)}) collective-permute-start(bf16[8,16,256]{2,1,0:T(8,128)(2,1)S(1)} %get-tuple-element.47), channel_id=1, source_target_pairs={{0,14},{2,12},{4,10},{6,8},{8,6},{10,4},{12,2},{14,0},{1,15},{3,13... | collective-permute-start | bytes 196616 | tf_op jit(solution)/shard_map/ppermute | solution.py:330
  29.6 8.7 %collective-permute-start.14 = (bf16[8,16,256]{2,1,0:T(8,128)(2,1)S(1)}, bf16[8,16,256]{2,1,0:T(8,128)(2,1)S(1)}, u32[]{:S(2)}, u32[]{:S(2)}) collective-permute-start(bf16[8,16,256]{2,1,0:T(8,128)(2,1)S(1)} %get-tuple-element.48), channel_id=1, source_target_pairs={{0,10},{2,8},{4,14},{6,12},{8,2},{10,0},{12,6},{14,4},{1,11},{3,9}... | collective-permute-start | bytes 196616 | tf_op jit(solution)/shard_map/ppermute | solution.py:330
  30.4 7.9 %collective-permute-start.16 = (bf16[8,16,256]{2,1,0:T(8,128)(2,1)S(1)}, bf16[8,16,256]{2,1,0:T(8,128)(2,1)S(1)}, u32[]{:S(2)}, u32[]{:S(2)}) collective-permute-start(bf16[8,16,256]{2,1,0:T(8,128)(2,1)S(1)} %get-tuple-element.50), channel_id=1, source_target_pairs={{0,6},{2,4},{4,2},{6,0},{8,14},{10,12},{12,10},{14,8},{1,7},{3,5},... | collective-permute-start | bytes 196616 | tf_op jit(solution)/shard_map/ppermute | solution.py:330
  34.1 5.9 %collective-permute-start.12 = (bf16[8,16,256]{2,1,0:T(8,128)(2,1)S(1)}, bf16[8,16,256]{2,1,0:T(8,128)(2,1)S(1)}, u32[]{:S(2)}, u32[]{:S(2)}) collective-permute-start(bf16[8,16,256]{2,1,0:T(8,128)(2,1)S(1)} %get-tuple-element.46), channel_id=1, source_target_pairs={{0,8},{2,10},{4,12},{6,14},{8,0},{10,2},{12,4},{14,6},{1,9},{3,11}... | collective-permute-start | bytes 196616 | tf_op jit(solution)/shard_map/ppermute | solution.py:330
  35.1 4.9 %collective-permute-start.15 = (bf16[8,16,256]{2,1,0:T(8,128)(2,1)S(1)}, bf16[8,16,256]{2,1,0:T(8,128)(2,1)S(1)}, u32[]{:S(2)}, u32[]{:S(2)}) collective-permute-start(bf16[8,16,256]{2,1,0:T(8,128)(2,1)S(1)} %get-tuple-element.49), channel_id=1, source_target_pairs={{0,2},{2,0},{4,6},{6,4},{8,10},{10,8},{12,14},{14,12},{1,3},{3,1},... | collective-permute-start | bytes 196616 | tf_op jit(solution)/shard_map/ppermute | solution.py:330

commit v7 on v6

--- a/solution.py
+++ b/solution.py
@@ -125,7 +125,7 @@
     return jnp.concatenate([head_cols, middle, tail_cols], axis=2).astype(jnp.bfloat16)
 
 
-VMEM_BYTES = 48 * 1024 * 1024
+VMEM_BYTES = 24 * 1024 * 1024
 
 
 def resident_fits(mesh, latent, kernel):
@@ -157,19 +157,17 @@
     return run
 
 
-def pack_body(pos, latent, *outs):
+def pack_body(pos, latent, *refs):
+    outs, packed = refs[:4], refs[4]
     z = pos[0]
     first = latent[0].astype(jnp.float32)
     second = latent[1].astype(jnp.float32)
     for owner in range(4):
         lanes = slice(64 * owner, 64 * owner + 64)
         block = jnp.concatenate([first[..., lanes], second[..., lanes]], axis=-1)
-        block = block.astype(jnp.bfloat16)
-        for k in range(4):
-
-            @pl.when(z == owner ^ k)
-            def _():
-                outs[k][...] = block
+        packed[owner] = block.astype(jnp.bfloat16)
+    for k in range(4):
+        outs[k][...] = packed[z ^ k]
 
 
 def group_sum(rows):
@@ -352,7 +350,7 @@
     other = across(quarters[1], 0)
     same_far = exchanged(quarters[2], 0, 1)
     other_far = across(quarters[3], 1)
-    packed = call(pack_body, [block] * 4)(pos, latent)
+    packed = call(pack_body, [block] * 4, [pltpu.VMEM((4, 8, 16, 128), bf16)])(pos, latent)
     near = [packed[0]] + [exchanged(packed[k], k, 0) for k in (1, 2, 3)]
     same_far, near[3] = lax.optimization_barrier((same_far, near[3]))
     far = [exchanged(part, 0, 1) for part in near]

time: 41.4 us -> 41.2 us (level)
  no operation moved by 1% of the time
where the time goes in v7:
time: 41.2 us; the launch traced here: 41.1 us
  starting transfers between devices  20.8 us (50%)
  waiting for transfers between devices  9.97 us (24%)
  Pallas kernels  8.3 us (20%)
  local copies, waits for them, and re-layouts  1.61 us (4%)
    ppermute x14, starting transfers between devices, exchanged(): return lax.ppermute(block, ('tile', 'tm'), route)  19.9 us
    ppermute x14, waiting for transfers between devices, exchanged(): return lax.ppermute(block, ('tile', 'tm'), route)  9.25 us
    pallas_call x6, Pallas kernels, run(): pl.pallas_call(body, out_shape=outs, in_specs=specs, out_specs=jax.tree.m...  8.3 us
    dynamic_slice x1, local copies, waits for them, and re-layouts, quarter(): return lax.dynamic_slice_in_dim(kernel, start, 128, axis=4)  1.37 us
    ppermute x2, starting transfers between devices, across(): return lax.ppermute(block, ('tm', 'ch'), route)  0.91 us
  transfers between devices with their start and end apart: 17, of which 9 were waited for; matrix products, arithmetic and copies ran while one was open for 1% of the time, Pallas kernels for 8%

profile of v7, /device:TPU:0, one launch (start us, length us, event | category | flops | bytes accessed | tf_op | source)
XLA Modules:
  0.0 41.1 jit_solution(4691790683367330009)
XLA Ops:
  0.0 0.0 copy-start
  0.0 0.0 copy-start.2
  0.0 0.0 copy-start.3
  0.0 0.0 copy-start.4
  0.0 1.4 %constant_dynamic-slice_fusion = (bf16[3,3,3,32,128]{4,3,2,1,0:T(8,128)(2,1)S(1)}, bf16[3,3,3,32,128]{4,3,2,1,0:T(8,128)(2,1)S(1)}, bf16[3,3,3,32,128]{4,3,2,1,0:T(8,128)(2,1)S(1)}, bf16[3,3,3,32,128]{4,3,2,1,0:T(8,128)(2,1)S(1)}) fusion(bf16[3,3,3,32,512]{4,3,2,1,0:T(8,128)(2,1)} %param.9, s32[]{:T(128)S(6)} %select_n.20, s32[]{:T(128)S(6)} %select_n.18, ...), kind=kLoop, calls=%fused_computation.1 | loop fusion | bytes 1769488 | tf_op jit(solution)/shard_map/dynamic_slice | solution.py:345
  1.4 3.1 %collective-permute-start.2 = (bf16[3,3,3,32,128]{4,3,2,1,0:T(8,128)(2,1)S(1)}, bf16[3,3,3,32,128]{4,3,2,1,0:T(8,128)(2,1)S(1)}, u32[]{:S(2)}, u32[]{:S(2)}) collective-permute-start(bf16[3,3,3,32,128]{4,3,2,1,0:T(8,128)(2,1)S(1)} %get-tuple-element.32), channel_id=1, source_target_pairs={{0,2},{2,0},{4,6},{6,4},{8,10},{10,8},{12,14},{14,12},{1,3},{3,1},... | collective-permute-start | bytes 663560 | tf_op jit(solution)/shard_map/ppermute | solution.py:328
  4.5 0.1 pad_add_fusion.pos
  4.5 0.0 copy-done
  4.5 0.7 %shard_map.64 = (bf16[8,16,128]{2,1,0:T(8,128)(2,1)S(1)}, bf16[8,16,128]{2,1,0:T(8,128)(2,1)S(1)}, bf16[8,16,128]{2,1,0:T(8,128)(2,1)S(1)}, bf16[8,16,128]{2,1,0:T(8,128)(2,1)S(1)}) custom-call(s32[2]{0:T(128)S(1)} %pad_add_fusion.pos, bf16[2,8,16,256]{3,2,1,0:T(8,128)(2,1)S(1)} %copy-done), custom_call_target="tpu_custom_call" | custom-call | flops 1000 | bytes 1000 | tf_op jit(solution)/shard_map/pallas_call | solution.py:147
  5.2 3.7 %collective-permute-start.3 = (bf16[8,16,128]{2,1,0:T(8,128)(2,1)S(1)}, bf16[8,16,128]{2,1,0:T(8,128)(2,1)S(1)}, u32[]{:S(2)}, u32[]{:S(2)}) collective-permute-start(bf16[8,16,128]{2,1,0:T(8,128)(2,1)S(1)} %get-tuple-element.33), channel_id=1, source_target_pairs={{0,12},{2,14},{4,8},{6,10},{8,4},{10,6},{12,0},{14,2},{1,13},{3,15... | collective-permute-start | bytes 98312 | tf_op jit(solution)/shard_map/ppermute | solution.py:328
  8.9 0.0 collective-permute-start.10
  8.9 0.0 collective-permute-start
  8.9 0.8 %collective-permute-start.1 = (bf16[8,16,128]{2,1,0:T(8,128)(2,1)S(1)}, bf16[8,16,128]{2,1,0:T(8,128)(2,1)S(1)}, u32[]{:S(2)}, u32[]{:S(2)}) collective-permute-start(bf16[8,16,128]{2,1,0:T(8,128)(2,1)S(1)} %get-tuple-element.31), channel_id=1, source_target_pairs={{0,8},{2,10},{4,12},{6,14},{8,0},{10,2},{12,4},{14,6},{1,9},{3,11}... | collective-permute-start | bytes 98312 | tf_op jit(solution)/shard_map/ppermute | solution.py:328
  9.7 0.0 copy-done.2
  9.7 0.1 dynamic_slice.18
  9.7 0.0 copy-done.3
  9.7 0.1 dynamic_slice.19
  9.8 1.2 %collective-permute-done.3.refs_3_ = bf16[8,16,128]{2,1,0:T(8,128)(2,1)S(1)} collective-permute-done((bf16[8,16,128]{2,1,0:T(8,128)(2,1)S(1)}, bf16[8,16,128]{2,1,0:T(8,128)(2,1)S(1)}, u32[]{:S(2)}, u32[]{:S(2)}) %collective-permute-start.3) | collective-permute-done | bytes 32800 | tf_op jit(solution)/shard_map/ppermute | solution.py:328
  11.0 0.3 collective-permute-start.4
  11.3 1.5 %collective-permute-done.refs_1_ = bf16[8,16,128]{2,1,0:T(8,128)(2,1)S(1)} collective-permute-done((bf16[8,16,128]{2,1,0:T(8,128)(2,1)S(1)}, bf16[8,16,128]{2,1,0:T(8,128)(2,1)S(1)}, u32[]{:S(2)}, u32[]{:S(2)}) %collective-permute-start) | collective-permute-done | bytes 32800 | tf_op jit(solution)/shard_map/ppermute | solution.py:328
  12.8 1.0 %collective-permute-start.5 = (bf16[8,16,128]{2,1,0:T(8,128)(2,1)S(1)}, bf16[8,16,128]{2,1,0:T(8,128)(2,1)S(1)}, u32[]{:S(2)}, u32[]{:S(2)}) collective-permute-start(bf16[8,16,128]{2,1,0:T(8,128)(2,1)S(1)} %collective-permute-done.refs_1_), channel_id=1, source_target_pairs={{0,2},{2,0},{4,6},{6,4},{8,10},{10,8},{12,14},{14,12},{1,3},{3,1},... | collective-permute-start | bytes 98312 | tf_op jit(solution)/shard_map/ppermute | solution.py:328
  13.8 0.0 collective-permute-done.1.refs_2_
  13.8 1.0 %collective-permute-start.6 = (bf16[8,16,128]{2,1,0:T(8,128)(2,1)S(1)}, bf16[8,16,128]{2,1,0:T(8,128)(2,1)S(1)}, u32[]{:S(2)}, u32[]{:S(2)}) collective-permute-start(bf16[8,16,128]{2,1,0:T(8,128)(2,1)S(1)} %collective-permute-done.1.refs_2_), channel_id=1, source_target_pairs={{0,2},{2,0},{4,6},{6,4},{8,10},{10,8},{12,14},{14,12},{1,3},{3,1},... | collective-permute-start | bytes 98312 | tf_op jit(solution)/shard_map/ppermute | solution.py:328
  14.8 0.0 collective-permute-done.2.same_far
  14.8 1.0 %collective-permute-start.7 = (bf16[8,16,128]{2,1,0:T(8,128)(2,1)S(1)}, bf16[8,16,128]{2,1,0:T(8,128)(2,1)S(1)}, u32[]{:S(2)}, u32[]{:S(2)}) collective-permute-start(bf16[8,16,128]{2,1,0:T(8,128)(2,1)S(1)} %collective-permute-done.3.refs_3_), channel_id=1, source_target_pairs={{0,2},{2,0},{4,6},{6,4},{8,10},{10,8},{12,14},{14,12},{1,3},{3,1},... | collective-permute-start | bytes 98312 | tf_op jit(solution)/shard_map/ppermute | solution.py:328
  15.8 0.1 maximum_bitcast_fusion
  15.9 0.4 collective-permute-done.4.refs_4_
  16.3 0.9 %collective-permute-start.9 = (bf16[3,3,3,32,128]{4,3,2,1,0:T(8,128)(2,1)S(1)}, bf16[3,3,3,32,128]{4,3,2,1,0:T(8,128)(2,1)S(1)}, u32[]{:S(2)}, u32[]{:S(2)}) collective-permute-start(bf16[3,3,3,32,128]{4,3,2,1,0:T(8,128)(2,1)S(1)} %get-tuple-element.36), channel_id=1, source_target_pairs={{0,1},{1,0},{2,3},{3,2},{4,5},{5,4},{6,7},{7,6},{8,9},{9,8},{10,11... | collective-permute-start | bytes 663560 | tf_op jit(solution)/shard_map/ppermute | solution.py:333
  17.2 0.0 collective-permute-done.5.refs_5_
  17.2 0.9 %collective-permute-done.6.refs_6_ = bf16[8,16,128]{2,1,0:T(8,128)(2,1)S(1)} collective-permute-done((bf16[8,16,128]{2,1,0:T(8,128)(2,1)S(1)}, bf16[8,16,128]{2,1,0:T(8,128)(2,1)S(1)}, u32[]{:S(2)}, u32[]{:S(2)}) %collective-permute-start.6) | collective-permute-done | bytes 32800 | tf_op jit(solution)/shard_map/ppermute | solution.py:328
  18.1 0.7 %collective-permute-done.7.refs_7_ = bf16[8,16,128]{2,1,0:T(8,128)(2,1)S(1)} collective-permute-done((bf16[8,16,128]{2,1,0:T(8,128)(2,1)S(1)}, bf16[8,16,128]{2,1,0:T(8,128)(2,1)S(1)}, u32[]{:S(2)}, u32[]{:S(2)}) %collective-permute-start.7) | collective-permute-done | bytes 32800 | tf_op jit(solution)/shard_map/ppermute | solution.py:328
  18.8 1.2 %shard_map.65.mine = bf16[2,8,96,128]{3,2,1,0:T(8,128)(2,1)S(1)} custom-call(s32[2]{0:T(128)S(1)} %pad_add_fusion.pos, f32[1,128]{1,0:T(1,128)S(1)} %get-tuple-element.55.gain, f32[1,128]{1,0:T(1,128)S(1)} %get-tuple-element.56.shift, bf16[8,16,128]{2,1,0:T(8,128)(2,1)S(1)} %get-tuple-element.29.refs_0_, ...), custom_call_target="tpu_custom_call" | custom-call | flops 1000 | bytes 1000 | tf_op jit(solution)/shard_map/pallas_call | solution.py:147
  20.1 0.1 collective-permute-start.8
  20.1 0.0 copy-done.4
  20.2 0.1 add_divide_fusion
  20.3 0.0 collective-permute-done.10.other_far
  20.3 0.0 collective-permute-done.9.other
  20.3 0.9 %shard_map.66 = (bf16[3,768,256]{2,1,0:T(8,128)(2,1)S(1)}, bf16[3,768,256]{2,1,0:T(8,128)(2,1)S(1)}) custom-call(s32[2]{0:T(128)S(1)} %pad_add_fusion.pos, bf16[3,3,3,32,128]{4,3,2,1,0:T(8,128)(2,1)S(1)} %get-tuple-element.35.same, bf16[3,3,3,32,128]{4,3,2,1,0:T(8,128)(2,1)S(1)} %collective-permute-done.9.other, ...), custom_call_target="tpu_custom_call" | custom-call | flops 1000 | bytes 1000 | tf_op jit(solution)/shard_map/pallas_call | solution.py:147
  21.1 0.7 %collective-permute-done.8.sibling = bf16[2,8,96,128]{3,2,1,0:T(8,128)(2,1)S(1)} collective-permute-done((bf16[2,8,96,128]{3,2,1,0:T(8,128)(2,1)S(1)}, bf16[2,8,96,128]{3,2,1,0:T(8,128)(2,1)S(1)}, u32[]{:S(2)}, u32[]{:S(2)}) %collective-permute-start.8) | collective-permute-done | bytes 393248 | tf_op jit(solution)/shard_map/ppermute | solution.py:369
  21.8 0.1 broadcast_in_dim.20.blend
  21.9 0.0 copy-start.1
  21.9 3.8 %shard_map.67 = (bf16[8,16,256]{2,1,0:T(8,128)(2,1)S(1)}, bf16[8,16,256]{2,1,0:T(8,128)(2,1)S(1)}, bf16[8,16,256]{2,1,0:T(8,128)(2,1)S(1)}, bf16[8,16,256]{2,1,0...) custom-call(s32[2]{0:T(128)S(1)} %pad_add_fusion.pos, ...), custom_call_target="tpu_custom_call" | custom-call | flops 1000 | bytes 1000 | tf_op jit(solution)/shard_map/pallas_call | solution.py:147
  25.7 2.1 %collective-permute-start.11 = (bf16[2,8,16,256]{3,2,1,0:T(8,128)(2,1)S(1)}, bf16[2,8,16,256]{3,2,1,0:T(8,128)(2,1)S(1)}, u32[]{:S(2)}, u32[]{:S(2)}) collective-permute-start(bf16[2,8,16,256]{3,2,1,0:T(8,128)(2,1)S(1)} %get-tuple-element.42), channel_id=1, source_target_pairs={{0,4},{2,6},{4,0},{6,2},{8,12},{10,14},{12,8},{14,10},{1,5},{3,7},... | collective-permute-start | bytes 393224 | tf_op jit(solution)/shard_map/ppermute | solution.py:328
  27.8 1.8 %collective-permute-start.13 = (bf16[8,16,256]{2,1,0:T(8,128)(2,1)S(1)}, bf16[8,16,256]{2,1,0:T(8,128)(2,1)S(1)}, u32[]{:S(2)}, u32[]{:S(2)}) collective-permute-start(bf16[8,16,256]{2,1,0:T(8,128)(2,1)S(1)} %get-tuple-element.47), channel_id=1, source_target_pairs={{0,14},{2,12},{4,10},{6,8},{8,6},{10,4},{12,2},{14,0},{1,15},{3,13... | collective-permute-start | bytes 196616 | tf_op jit(solution)/shard_map/ppermute | solution.py:328
  29.6 0.6 %collective-permute-start.14 = (bf16[8,16,256]{2,1,0:T(8,128)(2,1)S(1)}, bf16[8,16,256]{2,1,0:T(8,128)(2,1)S(1)}, u32[]{:S(2)}, u32[]{:S(2)}) collective-permute-start(bf16[8,16,256]{2,1,0:T(8,128)(2,1)S(1)} %get-tuple-element.48), channel_id=1, source_target_pairs={{0,10},{2,8},{4,14},{6,12},{8,2},{10,0},{12,6},{14,4},{1,11},{3,9}... | collective-permute-start | bytes 196616 | tf_op jit(solution)/shard_map/ppermute | solution.py:328
  30.2 3.1 %collective-permute-start.16 = (bf16[8,16,256]{2,1,0:T(8,128)(2,1)S(1)}, bf16[8,16,256]{2,1,0:T(8,128)(2,1)S(1)}, u32[]{:S(2)}, u32[]{:S(2)}) collective-permute-start(bf16[8,16,256]{2,1,0:T(8,128)(2,1)S(1)} %get-tuple-element.50), channel_id=1, source_target_pairs={{0,6},{2,4},{4,2},{6,0},{8,14},{10,12},{12,10},{14,8},{1,7},{3,5},... | collective-permute-start | bytes 196616 | tf_op jit(solution)/shard_map/ppermute | solution.py:328
  33.3 0.0 collective-permute-done.11.came
  33.3 0.6 %shard_map.68 = (f32[8,16,256]{2,1,0:T(8,128)S(1)}, bf16[8,16,256]{2,1,0:T(8,128)(2,1)S(1)}) custom-call(s32[2]{0:T(128)S(1)} %pad_add_fusion.pos, f32[2,8,16,256]{3,2,1,0:T(8,128)S(1)} %get-tuple-element.41.kept, bf16[2,8,16,256]{3,2,1,0:T(8,128)(2,1)S(1)} %collective-permute-done.11.came), custom_call_target="tpu_custom_call" | custom-call | flops 1000 | bytes 1000 | tf_op jit(solution)/shard_map/pallas_call | solution.py:147
  33.9 1.1 %collective-permute-start.12 = (bf16[8,16,256]{2,1,0:T(8,128)(2,1)S(1)}, bf16[8,16,256]{2,1,0:T(8,128)(2,1)S(1)}, u32[]{:S(2)}, u32[]{:S(2)}) collective-permute-start(bf16[8,16,256]{2,1,0:T(8,128)(2,1)S(1)} %get-tuple-element.46), channel_id=1, source_target_pairs={{0,8},{2,10},{4,12},{6,14},{8,0},{10,2},{12,4},{14,6},{1,9},{3,11}... | collective-permute-start | bytes 196616 | tf_op jit(solution)/shard_map/ppermute | solution.py:328
  34.9 0.3 collective-permute-start.15
  35.3 0.1 collective-permute-done.13.refs_0_
  35.4 2.7 %collective-permute-done.14.refs_1_ = bf16[8,16,256]{2,1,0:T(8,128)(2,1)S(1)} collective-permute-done((bf16[8,16,256]{2,1,0:T(8,128)(2,1)S(1)}, bf16[8,16,256]{2,1,0:T(8,128)(2,1)S(1)}, u32[]{:S(2)}, u32[]{:S(2)}) %collective-permute-start.14) | collective-permute-done | bytes 65568 | tf_op jit(solution)/shard_map/ppermute | solution.py:328
  38.1 0.0 collective-permute-done.16.refs_3_
  38.1 1.6 %collective-permute-done.12.same = bf16[8,16,256]{2,1,0:T(8,128)(2,1)S(1)} collective-permute-done((bf16[8,16,256]{2,1,0:T(8,128)(2,1)S(1)}, bf16[8,16,256]{2,1,0:T(8,128)(2,1)S(1)}, u32[]{:S(2)}, u32[]{:S(2)}) %collective-permute-start.12) | collective-permute-done | bytes 65568 | tf_op jit(solution)/shard_map/ppermute | solution.py:328
  39.8 0.0 collective-permute-done.15.refs_2_
  39.8 0.0 copy-done.1
  39.8 1.3 %shard_map.69 = bf16[2,8,16,256]{3,2,1,0:T(8,128)(2,1)} custom-call(s32[2]{0:T(128)S(1)} %pad_add_fusion.pos, f32[1,256]{1,0:T(1,128)S(1)} %bitcast.7, f32[8,16,256]{2,1,0:T(8,128)S(1)} %get-tuple-element.45.own, bf16[8,16,256]{2,1,0:T(8,128)(2,1)S(1)} %collective-permute-done.12.same, bf16[8,16,256]{2,1,0:T(8,128)(2,1)S(1)} %collective-permute-done.13.refs_0_, ...), custom_call_target="tpu_custom_call" | custom-call | flops 1000 | bytes 1000 | tf_op jit(solution)/shard_map/pallas_call | solution.py:147
  (2 shorter events, 0.0 us)
Async XLA Ops:
  0.0 4.5 %copy-start = (bf16[2,8,16,256]{3,2,1,0:T(8,128)(2,1)S(1)}, bf16[2,8,16,256]{3,2,1,0:T(8,128)(2,1)}, u32[]{:S(2)}) copy-start(bf16[2,8,16,256]{3,2,1,0:T(8,128)(2,1)} %latent) | copy-start | bytes 393220
  0.0 9.7 %copy-start.2 = (f32[256]{0:T(256)S(1)}, f32[256]{0:T(256)}, u32[]{:S(2)}) copy-start(f32[256]{0:T(256)} %param.7) | copy-start | bytes 3076
  0.0 9.7 %copy-start.3 = (f32[256]{0:T(256)S(1)}, f32[256]{0:T(256)}, u32[]{:S(2)}) copy-start(f32[256]{0:T(256)} %param.8) | copy-start | bytes 3076
  0.0 20.1 %copy-start.4 = (s32[4]{0:T(128)S(1)}, s32[4]{0:T(128)}, u32[]{:S(2)}) copy-start(s32[4]{0:T(128)} %param.11) | copy-start | bytes 52
  1.4 13.4 %collective-permute-start.2 = (bf16[3,3,3,32,128]{4,3,2,1,0:T(8,128)(2,1)S(1)}, bf16[3,3,3,32,128]{4,3,2,1,0:T(8,128)(2,1)S(1)}, u32[]{:S(2)}, u32[]{:S(2)}) collective-permute-start(bf16[3,3,3,32,128]{4,3,2,1,0:T(8,128)(2,1)S(1)} %get-tuple-element.32), channel_id=1, source_target_pairs={{0,2},{2,0},{4,6},{6,4},{8,10},{10,8},{12,14},{14,12},{1,3},{3,1},... | collective-permute-start | bytes 663560 | tf_op jit(solution)/shard_map/ppermute | solution.py:328
  5.2 5.8 %collective-permute-start.3 = (bf16[8,16,128]{2,1,0:T(8,128)(2,1)S(1)}, bf16[8,16,128]{2,1,0:T(8,128)(2,1)S(1)}, u32[]{:S(2)}, u32[]{:S(2)}) collective-permute-start(bf16[8,16,128]{2,1,0:T(8,128)(2,1)S(1)} %get-tuple-element.33), channel_id=1, source_target_pairs={{0,12},{2,14},{4,8},{6,10},{8,4},{10,6},{12,0},{14,2},{1,13},{3,15... | collective-permute-start | bytes 98312 | tf_op jit(solution)/shard_map/ppermute | solution.py:328
  8.9 11.4 %collective-permute-start.10 = (bf16[3,3,3,32,128]{4,3,2,1,0:T(8,128)(2,1)S(1)}, bf16[3,3,3,32,128]{4,3,2,1,0:T(8,128)(2,1)S(1)}, u32[]{:S(2)}, u32[]{:S(2)}) collective-permute-start(bf16[3,3,3,32,128]{4,3,2,1,0:T(8,128)(2,1)S(1)} %get-tuple-element.38), channel_id=1, source_target_pairs={{0,3},{1,2},{2,1},{3,0},{4,7},{5,6},{6,5},{7,4},{8,11},{9,10},{10,... | collective-permute-start | bytes 663560 | tf_op jit(solution)/shard_map/ppermute | solution.py:333
  8.9 3.9 %collective-permute-start = (bf16[8,16,128]{2,1,0:T(8,128)(2,1)S(1)}, bf16[8,16,128]{2,1,0:T(8,128)(2,1)S(1)}, u32[]{:S(2)}, u32[]{:S(2)}) collective-permute-start(bf16[8,16,128]{2,1,0:T(8,128)(2,1)S(1)} %get-tuple-element.30), channel_id=1, source_target_pairs={{0,4},{2,6},{4,0},{6,2},{8,12},{10,14},{12,8},{14,10},{1,5},{3,7},... | collective-permute-start | bytes 98312 | tf_op jit(solution)/shard_map/ppermute | solution.py:328
  8.9 4.9 %collective-permute-start.1 = (bf16[8,16,128]{2,1,0:T(8,128)(2,1)S(1)}, bf16[8,16,128]{2,1,0:T(8,128)(2,1)S(1)}, u32[]{:S(2)}, u32[]{:S(2)}) collective-permute-start(bf16[8,16,128]{2,1,0:T(8,128)(2,1)S(1)} %get-tuple-element.31), channel_id=1, source_target_pairs={{0,8},{2,10},{4,12},{6,14},{8,0},{10,2},{12,4},{14,6},{1,9},{3,11}... | collective-permute-start | bytes 98312 | tf_op jit(solution)/shard_map/ppermute | solution.py:328
  11.0 5.3 %collective-permute-start.4 = (bf16[8,16,128]{2,1,0:T(8,128)(2,1)S(1)}, bf16[8,16,128]{2,1,0:T(8,128)(2,1)S(1)}, u32[]{:S(2)}, u32[]{:S(2)}) collective-permute-start(bf16[8,16,128]{2,1,0:T(8,128)(2,1)S(1)} %get-tuple-element.29.refs_0_), channel_id=1, source_target_pairs={{0,2},{2,0},{4,6},{6,4},{8,10},{10,8},{12,14},{14,12},{1,3},{3,1},... | collective-permute-start | bytes 98312 | tf_op jit(solution)/shard_map/ppermute | solution.py:328
  12.8 4.4 %collective-permute-start.5 = (bf16[8,16,128]{2,1,0:T(8,128)(2,1)S(1)}, bf16[8,16,128]{2,1,0:T(8,128)(2,1)S(1)}, u32[]{:S(2)}, u32[]{:S(2)}) collective-permute-start(bf16[8,16,128]{2,1,0:T(8,128)(2,1)S(1)} %collective-permute-done.refs_1_), channel_id=1, source_target_pairs={{0,2},{2,0},{4,6},{6,4},{8,10},{10,8},{12,14},{14,12},{1,3},{3,1},... | collective-permute-start | bytes 98312 | tf_op jit(solution)/shard_map/ppermute | solution.py:328
  13.8 4.3 %collective-permute-start.6 = (bf16[8,16,128]{2,1,0:T(8,128)(2,1)S(1)}, bf16[8,16,128]{2,1,0:T(8,128)(2,1)S(1)}, u32[]{:S(2)}, u32[]{:S(2)}) collective-permute-start(bf16[8,16,128]{2,1,0:T(8,128)(2,1)S(1)} %collective-permute-done.1.refs_2_), channel_id=1, source_target_pairs={{0,2},{2,0},{4,6},{6,4},{8,10},{10,8},{12,14},{14,12},{1,3},{3,1},... | collective-permute-start | bytes 98312 | tf_op jit(solution)/shard_map/ppermute | solution.py:328
  14.8 4.0 %collective-permute-start.7 = (bf16[8,16,128]{2,1,0:T(8,128)(2,1)S(1)}, bf16[8,16,128]{2,1,0:T(8,128)(2,1)S(1)}, u32[]{:S(2)}, u32[]{:S(2)}) collective-permute-start(bf16[8,16,128]{2,1,0:T(8,128)(2,1)S(1)} %collective-permute-done.3.refs_3_), channel_id=1, source_target_pairs={{0,2},{2,0},{4,6},{6,4},{8,10},{10,8},{12,14},{14,12},{1,3},{3,1},... | collective-permute-start | bytes 98312 | tf_op jit(solution)/shard_map/ppermute | solution.py:328
  16.3 4.0 %collective-permute-start.9 = (bf16[3,3,3,32,128]{4,3,2,1,0:T(8,128)(2,1)S(1)}, bf16[3,3,3,32,128]{4,3,2,1,0:T(8,128)(2,1)S(1)}, u32[]{:S(2)}, u32[]{:S(2)}) collective-permute-start(bf16[3,3,3,32,128]{4,3,2,1,0:T(8,128)(2,1)S(1)} %get-tuple-element.36), channel_id=1, source_target_pairs={{0,1},{1,0},{2,3},{3,2},{4,5},{5,4},{6,7},{7,6},{8,9},{9,8},{10,11... | collective-permute-start | bytes 663560 | tf_op jit(solution)/shard_map/ppermute | solution.py:333
  20.1 1.8 %collective-permute-start.8 = (bf16[2,8,96,128]{3,2,1,0:T(8,128)(2,1)S(1)}, bf16[2,8,96,128]{3,2,1,0:T(8,128)(2,1)S(1)}, u32[]{:S(2)}, u32[]{:S(2)}) collective-permute-start(bf16[2,8,96,128]{3,2,1,0:T(8,128)(2,1)S(1)} %shard_map.65.mine), channel_id=1, source_target_pairs={{0,1},{1,0},{2,3},{3,2},{4,5},{5,4},{6,7},{7,6},{8,9},{9,8},{10,11... | collective-permute-start | bytes 1179656 | tf_op jit(solution)/shard_map/ppermute | solution.py:369
  21.9 17.9 %copy-start.1 = (f32[256]{0:T(256)S(1)}, f32[256]{0:T(256)}, u32[]{:S(2)}) copy-start(f32[256]{0:T(256)} %param.10) | copy-start | bytes 3076
  25.7 7.6 %collective-permute-start.11 = (bf16[2,8,16,256]{3,2,1,0:T(8,128)(2,1)S(1)}, bf16[2,8,16,256]{3,2,1,0:T(8,128)(2,1)S(1)}, u32[]{:S(2)}, u32[]{:S(2)}) collective-permute-start(bf16[2,8,16,256]{3,2,1,0:T(8,128)(2,1)S(1)} %get-tuple-element.42), channel_id=1, source_target_pairs={{0,4},{2,6},{4,0},{6,2},{8,12},{10,14},{12,8},{14,10},{1,5},{3,7},... | collective-permute-start | bytes 393224 | tf_op jit(solution)/shard_map/ppermute | solution.py:328
  27.8 7.7 %collective-permute-start.13 = (bf16[8,16,256]{2,1,0:T(8,128)(2,1)S(1)}, bf16[8,16,256]{2,1,0:T(8,128)(2,1)S(1)}, u32[]{:S(2)}, u32[]{:S(2)}) collective-permute-start(bf16[8,16,256]{2,1,0:T(8,128)(2,1)S(1)} %get-tuple-element.47), channel_id=1, source_target_pairs={{0,14},{2,12},{4,10},{6,8},{8,6},{10,4},{12,2},{14,0},{1,15},{3,13... | collective-permute-start | bytes 196616 | tf_op jit(solution)/shard_map/ppermute | solution.py:328
  29.6 8.6 %collective-permute-start.14 = (bf16[8,16,256]{2,1,0:T(8,128)(2,1)S(1)}, bf16[8,16,256]{2,1,0:T(8,128)(2,1)S(1)}, u32[]{:S(2)}, u32[]{:S(2)}) collective-permute-start(bf16[8,16,256]{2,1,0:T(8,128)(2,1)S(1)} %get-tuple-element.48), channel_id=1, source_target_pairs={{0,10},{2,8},{4,14},{6,12},{8,2},{10,0},{12,6},{14,4},{1,11},{3,9}... | collective-permute-start | bytes 196616 | tf_op jit(solution)/shard_map/ppermute | solution.py:328
  30.2 7.9 %collective-permute-start.16 = (bf16[8,16,256]{2,1,0:T(8,128)(2,1)S(1)}, bf16[8,16,256]{2,1,0:T(8,128)(2,1)S(1)}, u32[]{:S(2)}, u32[]{:S(2)}) collective-permute-start(bf16[8,16,256]{2,1,0:T(8,128)(2,1)S(1)} %get-tuple-element.50), channel_id=1, source_target_pairs={{0,6},{2,4},{4,2},{6,0},{8,14},{10,12},{12,10},{14,8},{1,7},{3,5},... | collective-permute-start | bytes 196616 | tf_op jit(solution)/shard_map/ppermute | solution.py:328
  33.9 5.9 %collective-permute-start.12 = (bf16[8,16,256]{2,1,0:T(8,128)(2,1)S(1)}, bf16[8,16,256]{2,1,0:T(8,128)(2,1)S(1)}, u32[]{:S(2)}, u32[]{:S(2)}) collective-permute-start(bf16[8,16,256]{2,1,0:T(8,128)(2,1)S(1)} %get-tuple-element.46), channel_id=1, source_target_pairs={{0,8},{2,10},{4,12},{6,14},{8,0},{10,2},{12,4},{14,6},{1,9},{3,11}... | collective-permute-start | bytes 196616 | tf_op jit(solution)/shard_map/ppermute | solution.py:328
  34.9 4.9 %collective-permute-start.15 = (bf16[8,16,256]{2,1,0:T(8,128)(2,1)S(1)}, bf16[8,16,256]{2,1,0:T(8,128)(2,1)S(1)}, u32[]{:S(2)}, u32[]{:S(2)}) collective-permute-start(bf16[8,16,256]{2,1,0:T(8,128)(2,1)S(1)} %get-tuple-element.49), channel_id=1, source_target_pairs={{0,2},{2,0},{4,6},{6,4},{8,10},{10,8},{12,14},{14,12},{1,3},{3,1},... | collective-permute-start | bytes 196616 | tf_op jit(solution)/shard_map/ppermute | solution.py:328

commit v8 on v7

--- a/solution.py
+++ b/solution.py
@@ -185,12 +185,15 @@
     return sums[:count] + sums[count : 2 * count] + sums[2 * count :]
 
 
+NORM = (0, 1, 3, 2)
+
+
 def norm_body(pos, gain, shift, *refs):
     blocks, (out, placed, raw) = refs[:8], refs[8:]
     z, x = pos[0], pos[1]
-    for k in range(4):
-        placed[x, z ^ k] = blocks[k][...]
-        placed[1 - x, z ^ k] = blocks[4 + k][...]
+    for i, k in enumerate(NORM):
+        placed[x, z ^ k] = blocks[i][...]
+        placed[1 - x, z ^ k] = blocks[4 + i][...]
     for p in range(2):
         raw[p, :, 0:4, :] = jnp.zeros((8, 4, 128), jnp.float32)
         raw[p, :, 68:72, :] = jnp.zeros((8, 4, 128), jnp.float32)
@@ -365,7 +368,7 @@
         norm_body,
         jax.ShapeDtypeStruct((2, 8, 96, 128), bf16),
         [pltpu.VMEM((2, 4, 8, 16, 128), bf16), pltpu.VMEM((2, 8, 72, 128), f32)],
-    )(pos, lanes_of(norm_gain), lanes_of(norm_shift), *near, *far)
+    )(pos, lanes_of(norm_gain), lanes_of(norm_shift), *[near[k] for k in NORM], *[far[k] for k in NORM])
     sibling = lax.ppermute(acts, "ch", [(0, 1), (1, 0)])
 
     offsets = jnp.arange(2 * RIM, dtype=jnp.int32)

time: 41.2 us -> 41.2 us (level)
  no operation moved by 1% of the time
where the time goes in v8:
time: 41.2 us; the launch traced here: 41.1 us
  starting transfers between devices  20.8 us (50%)
  waiting for transfers between devices  9.97 us (24%)
  Pallas kernels  8.3 us (20%)
  local copies, waits for them, and re-layouts  1.61 us (4%)
    ppermute x14, starting transfers between devices, exchanged(): return lax.ppermute(block, ('tile', 'tm'), route)  19.9 us
    ppermute x14, waiting for transfers between devices, exchanged(): return lax.ppermute(block, ('tile', 'tm'), route)  9.25 us
    pallas_call x6, Pallas kernels, run(): pl.pallas_call(body, out_shape=outs, in_specs=specs, out_specs=jax.tree.m...  8.3 us
    dynamic_slice x1, local copies, waits for them, and re-layouts, quarter(): return lax.dynamic_slice_in_dim(kernel, start, 128, axis=4)  1.37 us
    ppermute x2, starting transfers between devices, across(): return lax.ppermute(block, ('tm', 'ch'), route)  0.91 us
  transfers between devices with their start and end apart: 17, of which 9 were waited for; matrix products, arithmetic and copies ran while one was open for 1% of the time, Pallas kernels for 8%

profile of v8, /device:TPU:0, one launch (start us, length us, event | category | flops | bytes accessed | tf_op | source)
XLA Modules:
  0.0 41.1 jit_solution(16067336231356130397)
XLA Ops:
  0.0 0.0 copy-start
  0.0 0.0 copy-start.2
  0.0 0.0 copy-start.3
  0.0 0.0 copy-start.4
  0.0 1.4 %constant_dynamic-slice_fusion = (bf16[3,3,3,32,128]{4,3,2,1,0:T(8,128)(2,1)S(1)}, bf16[3,3,3,32,128]{4,3,2,1,0:T(8,128)(2,1)S(1)}, bf16[3,3,3,32,128]{4,3,2,1,0:T(8,128)(2,1)S(1)}, bf16[3,3,3,32,128]{4,3,2,1,0:T(8,128)(2,1)S(1)}) fusion(bf16[3,3,3,32,512]{4,3,2,1,0:T(8,128)(2,1)} %param.9, s32[]{:T(128)S(6)} %select_n.20, s32[]{:T(128)S(6)} %select_n.18, ...), kind=kLoop, calls=%fused_computation.1 | loop fusion | bytes 1769488 | tf_op jit(solution)/shard_map/dynamic_slice | solution.py:348
  1.4 3.1 %collective-permute-start.1 = (bf16[3,3,3,32,128]{4,3,2,1,0:T(8,128)(2,1)S(1)}, bf16[3,3,3,32,128]{4,3,2,1,0:T(8,128)(2,1)S(1)}, u32[]{:S(2)}, u32[]{:S(2)}) collective-permute-start(bf16[3,3,3,32,128]{4,3,2,1,0:T(8,128)(2,1)S(1)} %get-tuple-element.31), channel_id=1, source_target_pairs={{0,2},{2,0},{4,6},{6,4},{8,10},{10,8},{12,14},{14,12},{1,3},{3,1},... | collective-permute-start | bytes 663560 | tf_op jit(solution)/shard_map/ppermute | solution.py:331
  4.5 0.1 pad_add_fusion.pos
  4.5 0.0 copy-done
  4.5 0.7 %shard_map.64 = (bf16[8,16,128]{2,1,0:T(8,128)(2,1)S(1)}, bf16[8,16,128]{2,1,0:T(8,128)(2,1)S(1)}, bf16[8,16,128]{2,1,0:T(8,128)(2,1)S(1)}, bf16[8,16,128]{2,1,0:T(8,128)(2,1)S(1)}) custom-call(s32[2]{0:T(128)S(1)} %pad_add_fusion.pos, bf16[2,8,16,256]{3,2,1,0:T(8,128)(2,1)S(1)} %copy-done), custom_call_target="tpu_custom_call" | custom-call | flops 1000 | bytes 1000 | tf_op jit(solution)/shard_map/pallas_call | solution.py:147
  5.2 3.7 %collective-permute-start.2 = (bf16[8,16,128]{2,1,0:T(8,128)(2,1)S(1)}, bf16[8,16,128]{2,1,0:T(8,128)(2,1)S(1)}, u32[]{:S(2)}, u32[]{:S(2)}) collective-permute-start(bf16[8,16,128]{2,1,0:T(8,128)(2,1)S(1)} %get-tuple-element.32), channel_id=1, source_target_pairs={{0,12},{2,14},{4,8},{6,10},{8,4},{10,6},{12,0},{14,2},{1,13},{3,15... | collective-permute-start | bytes 98312 | tf_op jit(solution)/shard_map/ppermute | solution.py:331
  8.9 0.0 collective-permute-start.10
  8.9 0.0 collective-permute-start
  8.9 0.8 %collective-permute-start.3 = (bf16[8,16,128]{2,1,0:T(8,128)(2,1)S(1)}, bf16[8,16,128]{2,1,0:T(8,128)(2,1)S(1)}, u32[]{:S(2)}, u32[]{:S(2)}) collective-permute-start(bf16[8,16,128]{2,1,0:T(8,128)(2,1)S(1)} %get-tuple-element.34), channel_id=1, source_target_pairs={{0,8},{2,10},{4,12},{6,14},{8,0},{10,2},{12,4},{14,6},{1,9},{3,11}... | collective-permute-start | bytes 98312 | tf_op jit(solution)/shard_map/ppermute | solution.py:331
  9.7 0.0 copy-done.2
  9.7 0.1 dynamic_slice.18
  9.7 0.0 copy-done.3
  9.7 0.1 dynamic_slice.19
  9.8 1.2 %collective-permute-done.2.refs_2_ = bf16[8,16,128]{2,1,0:T(8,128)(2,1)S(1)} collective-permute-done((bf16[8,16,128]{2,1,0:T(8,128)(2,1)S(1)}, bf16[8,16,128]{2,1,0:T(8,128)(2,1)S(1)}, u32[]{:S(2)}, u32[]{:S(2)}) %collective-permute-start.2) | collective-permute-done | bytes 32800 | tf_op jit(solution)/shard_map/ppermute | solution.py:331
  11.0 0.3 collective-permute-start.4
  11.3 1.5 %collective-permute-done.refs_1_ = bf16[8,16,128]{2,1,0:T(8,128)(2,1)S(1)} collective-permute-done((bf16[8,16,128]{2,1,0:T(8,128)(2,1)S(1)}, bf16[8,16,128]{2,1,0:T(8,128)(2,1)S(1)}, u32[]{:S(2)}, u32[]{:S(2)}) %collective-permute-start) | collective-permute-done | bytes 32800 | tf_op jit(solution)/shard_map/ppermute | solution.py:331
  12.8 1.0 %collective-permute-start.5 = (bf16[8,16,128]{2,1,0:T(8,128)(2,1)S(1)}, bf16[8,16,128]{2,1,0:T(8,128)(2,1)S(1)}, u32[]{:S(2)}, u32[]{:S(2)}) collective-permute-start(bf16[8,16,128]{2,1,0:T(8,128)(2,1)S(1)} %collective-permute-done.refs_1_), channel_id=1, source_target_pairs={{0,2},{2,0},{4,6},{6,4},{8,10},{10,8},{12,14},{14,12},{1,3},{3,1},... | collective-permute-start | bytes 98312 | tf_op jit(solution)/shard_map/ppermute | solution.py:331
  13.8 0.0 collective-permute-done.3.refs_3_
  13.8 1.0 %collective-permute-start.7 = (bf16[8,16,128]{2,1,0:T(8,128)(2,1)S(1)}, bf16[8,16,128]{2,1,0:T(8,128)(2,1)S(1)}, u32[]{:S(2)}, u32[]{:S(2)}) collective-permute-start(bf16[8,16,128]{2,1,0:T(8,128)(2,1)S(1)} %collective-permute-done.3.refs_3_), channel_id=1, source_target_pairs={{0,2},{2,0},{4,6},{6,4},{8,10},{10,8},{12,14},{14,12},{1,3},{3,1},... | collective-permute-start | bytes 98312 | tf_op jit(solution)/shard_map/ppermute | solution.py:331
  14.8 0.0 collective-permute-done.1.same_far
  14.8 1.0 %collective-permute-start.6 = (bf16[8,16,128]{2,1,0:T(8,128)(2,1)S(1)}, bf16[8,16,128]{2,1,0:T(8,128)(2,1)S(1)}, u32[]{:S(2)}, u32[]{:S(2)}) collective-permute-start(bf16[8,16,128]{2,1,0:T(8,128)(2,1)S(1)} %collective-permute-done.2.refs_2_), channel_id=1, source_target_pairs={{0,2},{2,0},{4,6},{6,4},{8,10},{10,8},{12,14},{14,12},{1,3},{3,1},... | collective-permute-start | bytes 98312 | tf_op jit(solution)/shard_map/ppermute | solution.py:331
  15.8 0.1 maximum_bitcast_fusion
  15.9 0.4 collective-permute-done.4.refs_4_
  16.3 0.9 %collective-permute-start.9 = (bf16[3,3,3,32,128]{4,3,2,1,0:T(8,128)(2,1)S(1)}, bf16[3,3,3,32,128]{4,3,2,1,0:T(8,128)(2,1)S(1)}, u32[]{:S(2)}, u32[]{:S(2)}) collective-permute-start(bf16[3,3,3,32,128]{4,3,2,1,0:T(8,128)(2,1)S(1)} %get-tuple-element.36), channel_id=1, source_target_pairs={{0,1},{1,0},{2,3},{3,2},{4,5},{5,4},{6,7},{7,6},{8,9},{9,8},{10,11... | collective-permute-start | bytes 663560 | tf_op jit(solution)/shard_map/ppermute | solution.py:336
  17.2 0.0 collective-permute-done.5.refs_5_
  17.2 0.9 %collective-permute-done.7.refs_7_ = bf16[8,16,128]{2,1,0:T(8,128)(2,1)S(1)} collective-permute-done((bf16[8,16,128]{2,1,0:T(8,128)(2,1)S(1)}, bf16[8,16,128]{2,1,0:T(8,128)(2,1)S(1)}, u32[]{:S(2)}, u32[]{:S(2)}) %collective-permute-start.7) | collective-permute-done | bytes 32800 | tf_op jit(solution)/shard_map/ppermute | solution.py:331
  18.1 0.7 %collective-permute-done.6.refs_6_ = bf16[8,16,128]{2,1,0:T(8,128)(2,1)S(1)} collective-permute-done((bf16[8,16,128]{2,1,0:T(8,128)(2,1)S(1)}, bf16[8,16,128]{2,1,0:T(8,128)(2,1)S(1)}, u32[]{:S(2)}, u32[]{:S(2)}) %collective-permute-start.6) | collective-permute-done | bytes 32800 | tf_op jit(solution)/shard_map/ppermute | solution.py:331
  18.8 1.2 %shard_map.65.mine = bf16[2,8,96,128]{3,2,1,0:T(8,128)(2,1)S(1)} custom-call(s32[2]{0:T(128)S(1)} %pad_add_fusion.pos, f32[1,128]{1,0:T(1,128)S(1)} %get-tuple-element.55.gain, f32[1,128]{1,0:T(1,128)S(1)} %get-tuple-element.56.shift, bf16[8,16,128]{2,1,0:T(8,128)(2,1)S(1)} %get-tuple-element.29.refs_0_, ...), custom_call_target="tpu_custom_call" | custom-call | flops 1000 | bytes 1000 | tf_op jit(solution)/shard_map/pallas_call | solution.py:147
  20.1 0.1 collective-permute-start.8
  20.1 0.0 copy-done.4
  20.2 0.1 add_divide_fusion
  20.3 0.0 collective-permute-done.10.other_far
  20.3 0.0 collective-permute-done.9.other
  20.3 0.9 %shard_map.66 = (bf16[3,768,256]{2,1,0:T(8,128)(2,1)S(1)}, bf16[3,768,256]{2,1,0:T(8,128)(2,1)S(1)}) custom-call(s32[2]{0:T(128)S(1)} %pad_add_fusion.pos, bf16[3,3,3,32,128]{4,3,2,1,0:T(8,128)(2,1)S(1)} %get-tuple-element.35.same, bf16[3,3,3,32,128]{4,3,2,1,0:T(8,128)(2,1)S(1)} %collective-permute-done.9.other, ...), custom_call_target="tpu_custom_call" | custom-call | flops 1000 | bytes 1000 | tf_op jit(solution)/shard_map/pallas_call | solution.py:147
  21.1 0.7 %collective-permute-done.8.sibling = bf16[2,8,96,128]{3,2,1,0:T(8,128)(2,1)S(1)} collective-permute-done((bf16[2,8,96,128]{3,2,1,0:T(8,128)(2,1)S(1)}, bf16[2,8,96,128]{3,2,1,0:T(8,128)(2,1)S(1)}, u32[]{:S(2)}, u32[]{:S(2)}) %collective-permute-start.8) | collective-permute-done | bytes 393248 | tf_op jit(solution)/shard_map/ppermute | solution.py:372
  21.8 0.1 broadcast_in_dim.20.blend
  21.9 0.0 copy-start.1
  21.9 3.8 %shard_map.67 = (bf16[8,16,256]{2,1,0:T(8,128)(2,1)S(1)}, bf16[8,16,256]{2,1,0:T(8,128)(2,1)S(1)}, bf16[8,16,256]{2,1,0:T(8,128)(2,1)S(1)}, bf16[8,16,256]{2,1,0...) custom-call(s32[2]{0:T(128)S(1)} %pad_add_fusion.pos, ...), custom_call_target="tpu_custom_call" | custom-call | flops 1000 | bytes 1000 | tf_op jit(solution)/shard_map/pallas_call | solution.py:147
  25.7 2.1 %collective-permute-start.11 = (bf16[2,8,16,256]{3,2,1,0:T(8,128)(2,1)S(1)}, bf16[2,8,16,256]{3,2,1,0:T(8,128)(2,1)S(1)}, u32[]{:S(2)}, u32[]{:S(2)}) collective-permute-start(bf16[2,8,16,256]{3,2,1,0:T(8,128)(2,1)S(1)} %get-tuple-element.42), channel_id=1, source_target_pairs={{0,4},{2,6},{4,0},{6,2},{8,12},{10,14},{12,8},{14,10},{1,5},{3,7},... | collective-permute-start | bytes 393224 | tf_op jit(solution)/shard_map/ppermute | solution.py:331
  27.8 1.8 %collective-permute-start.13 = (bf16[8,16,256]{2,1,0:T(8,128)(2,1)S(1)}, bf16[8,16,256]{2,1,0:T(8,128)(2,1)S(1)}, u32[]{:S(2)}, u32[]{:S(2)}) collective-permute-start(bf16[8,16,256]{2,1,0:T(8,128)(2,1)S(1)} %get-tuple-element.47), channel_id=1, source_target_pairs={{0,14},{2,12},{4,10},{6,8},{8,6},{10,4},{12,2},{14,0},{1,15},{3,13... | collective-permute-start | bytes 196616 | tf_op jit(solution)/shard_map/ppermute | solution.py:331
  29.6 0.6 %collective-permute-start.14 = (bf16[8,16,256]{2,1,0:T(8,128)(2,1)S(1)}, bf16[8,16,256]{2,1,0:T(8,128)(2,1)S(1)}, u32[]{:S(2)}, u32[]{:S(2)}) collective-permute-start(bf16[8,16,256]{2,1,0:T(8,128)(2,1)S(1)} %get-tuple-element.48), channel_id=1, source_target_pairs={{0,10},{2,8},{4,14},{6,12},{8,2},{10,0},{12,6},{14,4},{1,11},{3,9}... | collective-permute-start | bytes 196616 | tf_op jit(solution)/shard_map/ppermute | solution.py:331
  30.2 3.1 %collective-permute-start.16 = (bf16[8,16,256]{2,1,0:T(8,128)(2,1)S(1)}, bf16[8,16,256]{2,1,0:T(8,128)(2,1)S(1)}, u32[]{:S(2)}, u32[]{:S(2)}) collective-permute-start(bf16[8,16,256]{2,1,0:T(8,128)(2,1)S(1)} %get-tuple-element.50), channel_id=1, source_target_pairs={{0,6},{2,4},{4,2},{6,0},{8,14},{10,12},{12,10},{14,8},{1,7},{3,5},... | collective-permute-start | bytes 196616 | tf_op jit(solution)/shard_map/ppermute | solution.py:331
  33.3 0.0 collective-permute-done.11.came
  33.3 0.6 %shard_map.68 = (f32[8,16,256]{2,1,0:T(8,128)S(1)}, bf16[8,16,256]{2,1,0:T(8,128)(2,1)S(1)}) custom-call(s32[2]{0:T(128)S(1)} %pad_add_fusion.pos, f32[2,8,16,256]{3,2,1,0:T(8,128)S(1)} %get-tuple-element.41.kept, bf16[2,8,16,256]{3,2,1,0:T(8,128)(2,1)S(1)} %collective-permute-done.11.came), custom_call_target="tpu_custom_call" | custom-call | flops 1000 | bytes 1000 | tf_op jit(solution)/shard_map/pallas_call | solution.py:147
  33.9 1.1 %collective-permute-start.12 = (bf16[8,16,256]{2,1,0:T(8,128)(2,1)S(1)}, bf16[8,16,256]{2,1,0:T(8,128)(2,1)S(1)}, u32[]{:S(2)}, u32[]{:S(2)}) collective-permute-start(bf16[8,16,256]{2,1,0:T(8,128)(2,1)S(1)} %get-tuple-element.46), channel_id=1, source_target_pairs={{0,8},{2,10},{4,12},{6,14},{8,0},{10,2},{12,4},{14,6},{1,9},{3,11}... | collective-permute-start | bytes 196616 | tf_op jit(solution)/shard_map/ppermute | solution.py:331
  34.9 0.3 collective-permute-start.15
  35.3 0.1 collective-permute-done.13.refs_0_
  35.4 2.7 %collective-permute-done.14.refs_1_ = bf16[8,16,256]{2,1,0:T(8,128)(2,1)S(1)} collective-permute-done((bf16[8,16,256]{2,1,0:T(8,128)(2,1)S(1)}, bf16[8,16,256]{2,1,0:T(8,128)(2,1)S(1)}, u32[]{:S(2)}, u32[]{:S(2)}) %collective-permute-start.14) | collective-permute-done | bytes 65568 | tf_op jit(solution)/shard_map/ppermute | solution.py:331
  38.1 0.0 collective-permute-done.16.refs_3_
  38.1 1.6 %collective-permute-done.12.same = bf16[8,16,256]{2,1,0:T(8,128)(2,1)S(1)} collective-permute-done((bf16[8,16,256]{2,1,0:T(8,128)(2,1)S(1)}, bf16[8,16,256]{2,1,0:T(8,128)(2,1)S(1)}, u32[]{:S(2)}, u32[]{:S(2)}) %collective-permute-start.12) | collective-permute-done | bytes 65568 | tf_op jit(solution)/shard_map/ppermute | solution.py:331
  39.8 0.0 collective-permute-done.15.refs_2_
  39.8 0.0 copy-done.1
  39.8 1.3 %shard_map.69 = bf16[2,8,16,256]{3,2,1,0:T(8,128)(2,1)} custom-call(s32[2]{0:T(128)S(1)} %pad_add_fusion.pos, f32[1,256]{1,0:T(1,128)S(1)} %bitcast.7, f32[8,16,256]{2,1,0:T(8,128)S(1)} %get-tuple-element.45.own, bf16[8,16,256]{2,1,0:T(8,128)(2,1)S(1)} %collective-permute-done.12.same, bf16[8,16,256]{2,1,0:T(8,128)(2,1)S(1)} %collective-permute-done.13.refs_0_, ...), custom_call_target="tpu_custom_call" | custom-call | flops 1000 | bytes 1000 | tf_op jit(solution)/shard_map/pallas_call | solution.py:147
  (2 shorter events, 0.0 us)
Async XLA Ops:
  0.0 4.5 %copy-start = (bf16[2,8,16,256]{3,2,1,0:T(8,128)(2,1)S(1)}, bf16[2,8,16,256]{3,2,1,0:T(8,128)(2,1)}, u32[]{:S(2)}) copy-start(bf16[2,8,16,256]{3,2,1,0:T(8,128)(2,1)} %latent) | copy-start | bytes 393220
  0.0 9.7 %copy-start.2 = (f32[256]{0:T(256)S(1)}, f32[256]{0:T(256)}, u32[]{:S(2)}) copy-start(f32[256]{0:T(256)} %param.7) | copy-start | bytes 3076
  0.0 9.7 %copy-start.3 = (f32[256]{0:T(256)S(1)}, f32[256]{0:T(256)}, u32[]{:S(2)}) copy-start(f32[256]{0:T(256)} %param.8) | copy-start | bytes 3076
  0.0 20.1 %copy-start.4 = (s32[4]{0:T(128)S(1)}, s32[4]{0:T(128)}, u32[]{:S(2)}) copy-start(s32[4]{0:T(128)} %param.11) | copy-start | bytes 52
  1.4 13.4 %collective-permute-start.1 = (bf16[3,3,3,32,128]{4,3,2,1,0:T(8,128)(2,1)S(1)}, bf16[3,3,3,32,128]{4,3,2,1,0:T(8,128)(2,1)S(1)}, u32[]{:S(2)}, u32[]{:S(2)}) collective-permute-start(bf16[3,3,3,32,128]{4,3,2,1,0:T(8,128)(2,1)S(1)} %get-tuple-element.31), channel_id=1, source_target_pairs={{0,2},{2,0},{4,6},{6,4},{8,10},{10,8},{12,14},{14,12},{1,3},{3,1},... | collective-permute-start | bytes 663560 | tf_op jit(solution)/shard_map/ppermute | solution.py:331
  5.2 5.8 %collective-permute-start.2 = (bf16[8,16,128]{2,1,0:T(8,128)(2,1)S(1)}, bf16[8,16,128]{2,1,0:T(8,128)(2,1)S(1)}, u32[]{:S(2)}, u32[]{:S(2)}) collective-permute-start(bf16[8,16,128]{2,1,0:T(8,128)(2,1)S(1)} %get-tuple-element.32), channel_id=1, source_target_pairs={{0,12},{2,14},{4,8},{6,10},{8,4},{10,6},{12,0},{14,2},{1,13},{3,15... | collective-permute-start | bytes 98312 | tf_op jit(solution)/shard_map/ppermute | solution.py:331
  8.9 11.4 %collective-permute-start.10 = (bf16[3,3,3,32,128]{4,3,2,1,0:T(8,128)(2,1)S(1)}, bf16[3,3,3,32,128]{4,3,2,1,0:T(8,128)(2,1)S(1)}, u32[]{:S(2)}, u32[]{:S(2)}) collective-permute-start(bf16[3,3,3,32,128]{4,3,2,1,0:T(8,128)(2,1)S(1)} %get-tuple-element.38), channel_id=1, source_target_pairs={{0,3},{1,2},{2,1},{3,0},{4,7},{5,6},{6,5},{7,4},{8,11},{9,10},{10,... | collective-permute-start | bytes 663560 | tf_op jit(solution)/shard_map/ppermute | solution.py:336
  8.9 3.9 %collective-permute-start = (bf16[8,16,128]{2,1,0:T(8,128)(2,1)S(1)}, bf16[8,16,128]{2,1,0:T(8,128)(2,1)S(1)}, u32[]{:S(2)}, u32[]{:S(2)}) collective-permute-start(bf16[8,16,128]{2,1,0:T(8,128)(2,1)S(1)} %get-tuple-element.30), channel_id=1, source_target_pairs={{0,4},{2,6},{4,0},{6,2},{8,12},{10,14},{12,8},{14,10},{1,5},{3,7},... | collective-permute-start | bytes 98312 | tf_op jit(solution)/shard_map/ppermute | solution.py:331
  8.9 4.9 %collective-permute-start.3 = (bf16[8,16,128]{2,1,0:T(8,128)(2,1)S(1)}, bf16[8,16,128]{2,1,0:T(8,128)(2,1)S(1)}, u32[]{:S(2)}, u32[]{:S(2)}) collective-permute-start(bf16[8,16,128]{2,1,0:T(8,128)(2,1)S(1)} %get-tuple-element.34), channel_id=1, source_target_pairs={{0,8},{2,10},{4,12},{6,14},{8,0},{10,2},{12,4},{14,6},{1,9},{3,11}... | collective-permute-start | bytes 98312 | tf_op jit(solution)/shard_map/ppermute | solution.py:331
  11.0 5.3 %collective-permute-start.4 = (bf16[8,16,128]{2,1,0:T(8,128)(2,1)S(1)}, bf16[8,16,128]{2,1,0:T(8,128)(2,1)S(1)}, u32[]{:S(2)}, u32[]{:S(2)}) collective-permute-start(bf16[8,16,128]{2,1,0:T(8,128)(2,1)S(1)} %get-tuple-element.29.refs_0_), channel_id=1, source_target_pairs={{0,2},{2,0},{4,6},{6,4},{8,10},{10,8},{12,14},{14,12},{1,3},{3,1},... | collective-permute-start | bytes 98312 | tf_op jit(solution)/shard_map/ppermute | solution.py:331
  12.8 4.4 %collective-permute-start.5 = (bf16[8,16,128]{2,1,0:T(8,128)(2,1)S(1)}, bf16[8,16,128]{2,1,0:T(8,128)(2,1)S(1)}, u32[]{:S(2)}, u32[]{:S(2)}) collective-permute-start(bf16[8,16,128]{2,1,0:T(8,128)(2,1)S(1)} %collective-permute-done.refs_1_), channel_id=1, source_target_pairs={{0,2},{2,0},{4,6},{6,4},{8,10},{10,8},{12,14},{14,12},{1,3},{3,1},... | collective-permute-start | bytes 98312 | tf_op jit(solution)/shard_map/ppermute | solution.py:331
  13.8 4.3 %collective-permute-start.7 = (bf16[8,16,128]{2,1,0:T(8,128)(2,1)S(1)}, bf16[8,16,128]{2,1,0:T(8,128)(2,1)S(1)}, u32[]{:S(2)}, u32[]{:S(2)}) collective-permute-start(bf16[8,16,128]{2,1,0:T(8,128)(2,1)S(1)} %collective-permute-done.3.refs_3_), channel_id=1, source_target_pairs={{0,2},{2,0},{4,6},{6,4},{8,10},{10,8},{12,14},{14,12},{1,3},{3,1},... | collective-permute-start | bytes 98312 | tf_op jit(solution)/shard_map/ppermute | solution.py:331
  14.8 4.0 %collective-permute-start.6 = (bf16[8,16,128]{2,1,0:T(8,128)(2,1)S(1)}, bf16[8,16,128]{2,1,0:T(8,128)(2,1)S(1)}, u32[]{:S(2)}, u32[]{:S(2)}) collective-permute-start(bf16[8,16,128]{2,1,0:T(8,128)(2,1)S(1)} %collective-permute-done.2.refs_2_), channel_id=1, source_target_pairs={{0,2},{2,0},{4,6},{6,4},{8,10},{10,8},{12,14},{14,12},{1,3},{3,1},... | collective-permute-start | bytes 98312 | tf_op jit(solution)/shard_map/ppermute | solution.py:331
  16.3 4.0 %collective-permute-start.9 = (bf16[3,3,3,32,128]{4,3,2,1,0:T(8,128)(2,1)S(1)}, bf16[3,3,3,32,128]{4,3,2,1,0:T(8,128)(2,1)S(1)}, u32[]{:S(2)}, u32[]{:S(2)}) collective-permute-start(bf16[3,3,3,32,128]{4,3,2,1,0:T(8,128)(2,1)S(1)} %get-tuple-element.36), channel_id=1, source_target_pairs={{0,1},{1,0},{2,3},{3,2},{4,5},{5,4},{6,7},{7,6},{8,9},{9,8},{10,11... | collective-permute-start | bytes 663560 | tf_op jit(solution)/shard_map/ppermute | solution.py:336
  20.1 1.8 %collective-permute-start.8 = (bf16[2,8,96,128]{3,2,1,0:T(8,128)(2,1)S(1)}, bf16[2,8,96,128]{3,2,1,0:T(8,128)(2,1)S(1)}, u32[]{:S(2)}, u32[]{:S(2)}) collective-permute-start(bf16[2,8,96,128]{3,2,1,0:T(8,128)(2,1)S(1)} %shard_map.65.mine), channel_id=1, source_target_pairs={{0,1},{1,0},{2,3},{3,2},{4,5},{5,4},{6,7},{7,6},{8,9},{9,8},{10,11... | collective-permute-start | bytes 1179656 | tf_op jit(solution)/shard_map/ppermute | solution.py:372
  21.9 17.9 %copy-start.1 = (f32[256]{0:T(256)S(1)}, f32[256]{0:T(256)}, u32[]{:S(2)}) copy-start(f32[256]{0:T(256)} %param.10) | copy-start | bytes 3076
  25.7 7.6 %collective-permute-start.11 = (bf16[2,8,16,256]{3,2,1,0:T(8,128)(2,1)S(1)}, bf16[2,8,16,256]{3,2,1,0:T(8,128)(2,1)S(1)}, u32[]{:S(2)}, u32[]{:S(2)}) collective-permute-start(bf16[2,8,16,256]{3,2,1,0:T(8,128)(2,1)S(1)} %get-tuple-element.42), channel_id=1, source_target_pairs={{0,4},{2,6},{4,0},{6,2},{8,12},{10,14},{12,8},{14,10},{1,5},{3,7},... | collective-permute-start | bytes 393224 | tf_op jit(solution)/shard_map/ppermute | solution.py:331
  27.8 7.7 %collective-permute-start.13 = (bf16[8,16,256]{2,1,0:T(8,128)(2,1)S(1)}, bf16[8,16,256]{2,1,0:T(8,128)(2,1)S(1)}, u32[]{:S(2)}, u32[]{:S(2)}) collective-permute-start(bf16[8,16,256]{2,1,0:T(8,128)(2,1)S(1)} %get-tuple-element.47), channel_id=1, source_target_pairs={{0,14},{2,12},{4,10},{6,8},{8,6},{10,4},{12,2},{14,0},{1,15},{3,13... | collective-permute-start | bytes 196616 | tf_op jit(solution)/shard_map/ppermute | solution.py:331
  29.6 8.6 %collective-permute-start.14 = (bf16[8,16,256]{2,1,0:T(8,128)(2,1)S(1)}, bf16[8,16,256]{2,1,0:T(8,128)(2,1)S(1)}, u32[]{:S(2)}, u32[]{:S(2)}) collective-permute-start(bf16[8,16,256]{2,1,0:T(8,128)(2,1)S(1)} %get-tuple-element.48), channel_id=1, source_target_pairs={{0,10},{2,8},{4,14},{6,12},{8,2},{10,0},{12,6},{14,4},{1,11},{3,9}... | collective-permute-start | bytes 196616 | tf_op jit(solution)/shard_map/ppermute | solution.py:331
  30.2 7.9 %collective-permute-start.16 = (bf16[8,16,256]{2,1,0:T(8,128)(2,1)S(1)}, bf16[8,16,256]{2,1,0:T(8,128)(2,1)S(1)}, u32[]{:S(2)}, u32[]{:S(2)}) collective-permute-start(bf16[8,16,256]{2,1,0:T(8,128)(2,1)S(1)} %get-tuple-element.50), channel_id=1, source_target_pairs={{0,6},{2,4},{4,2},{6,0},{8,14},{10,12},{12,10},{14,8},{1,7},{3,5},... | collective-permute-start | bytes 196616 | tf_op jit(solution)/shard_map/ppermute | solution.py:331
  33.9 5.9 %collective-permute-start.12 = (bf16[8,16,256]{2,1,0:T(8,128)(2,1)S(1)}, bf16[8,16,256]{2,1,0:T(8,128)(2,1)S(1)}, u32[]{:S(2)}, u32[]{:S(2)}) collective-permute-start(bf16[8,16,256]{2,1,0:T(8,128)(2,1)S(1)} %get-tuple-element.46), channel_id=1, source_target_pairs={{0,8},{2,10},{4,12},{6,14},{8,0},{10,2},{12,4},{14,6},{1,9},{3,11}... | collective-permute-start | bytes 196616 | tf_op jit(solution)/shard_map/ppermute | solution.py:331
  34.9 4.9 %collective-permute-start.15 = (bf16[8,16,256]{2,1,0:T(8,128)(2,1)S(1)}, bf16[8,16,256]{2,1,0:T(8,128)(2,1)S(1)}, u32[]{:S(2)}, u32[]{:S(2)}) collective-permute-start(bf16[8,16,256]{2,1,0:T(8,128)(2,1)S(1)} %get-tuple-element.49), channel_id=1, source_target_pairs={{0,2},{2,0},{4,6},{6,4},{8,10},{10,8},{12,14},{14,12},{1,3},{3,1},... | collective-permute-start | bytes 196616 | tf_op jit(solution)/shard_map/ppermute | solution.py:331
